TPU v7x, 256 devices: a whole 4x4x8 slice. The times are simulated.
256 devices in a mesh: sf: 128 (over x, z, y), wa: 2 (over core).
Axes of the slice: x: 4, y: 4, z: 8, core: 2. Of those that a mesh axis runs over, the one named last changes fastest.
Arguments:
- visibilities: bfloat16 [2, 128, 2, 8, 128], P(None, 'sf', 'wa'), may hold values from -6 to 6
- kernels: bfloat16 [2, 8, 128, 2, 8, 128], P(None, None, 'sf', 'wa'), may hold values from 0.19921875 to 1.1953125
- vis_offsets: int32 [2, 128, 2, 8, 128], P(None, 'sf', 'wa'), may hold values from 0 to 504
- block_counts: int32 [128, 2], P('sf', 'wa'), may hold values from 1 to 8, as said below
- sub_rows: int32 [16], replicated, may hold values from 0 to 448, as said below
- sub_cols: int32 [8], replicated, may hold values from 0 to 448, as said below
- facet_rows: int32 [16], replicated, may hold values from 0 to 448, as said below
- facet_cols: int32 [8], replicated, may hold values from 0 to 448, as said below
- screen_n: float32 [128, 512, 512], P('sf'), may hold values from 0 to 1
- layer_w: float32 [2], replicated, may hold values from 0.5 to 2
Outputs:
- image: float32 [2, 128, 512, 512], P(None, 'sf', 'wa')
Inputs may be any that keep to these rules, and one draw needn't show every extreme that they name: `block_counts`: live blocks of one subgrid and layer; some subgrid and layer has all 8 slots live. `sub_rows`: distinct values; one of them is the most. `sub_cols`: distinct values; one of them is the most. `facet_rows`: distinct values; one of them is the most. `facet_cols`: distinct values; one of them is the most.
All inputs are finite; a program needn't handle non-finite values.
Results may differ from a plain program's by a relative error of at most 0.0099.
Values may be sent and summed in bfloat16 or wider, within the bound.
No kernel may reach another device: no remote copies, remote signals or barrier semaphores. Data moves between devices by JAX's collectives and lax.ppermute only.
A program may use at most 64 MiB of HBM per device.

v0:
```python
import math

import jax
import jax.numpy as jnp
from jax import lax
from jax.experimental import pallas as pl
from jax.experimental.pallas import tpu as pltpu
from jax.sharding import PartitionSpec as P

SUB = 512
CON = 64
FAC = 512
VB = 128
F32 = jnp.float32
BF16 = jnp.bfloat16
NORM = 1.0 / math.sqrt(512.0)
NN = (((1,), (0,)), ((), ()))
NT = (((1,), (1,)), ((), ()))


def dot(first, second, numbers=NN):
    return lax.dot_general(first, second, numbers, preferred_element_type=F32)


def iota(shape, axis):
    return lax.broadcasted_iota(jnp.int32, shape, axis)


def sincos_small(theta):
    square = theta * theta
    cosine = 1.0 + square * (-0.5 + square * (1.0 / 24 + square * (-1.0 / 720 + square * (1.0 / 40320))))
    sine = theta * (1.0 + square * (-1.0 / 6 + square * (1.0 / 120 + square * (-1.0 / 5040 + square * (1.0 / 362880)))))
    return cosine, sine


def rotate_quarter(cosine, sine, quarter):
    odd = (quarter & 1) == 1
    real = jnp.where(odd, sine, cosine)
    imag = jnp.where(odd, cosine, sine)
    real = jnp.where(((quarter + 1) & 2) == 2, -real, real)
    imag = jnp.where((quarter & 2) == 2, -imag, imag)
    return real, imag


def unit_roots(steps):
    quarter = (steps + 64) >> 7
    rest = steps - (quarter << 7)
    cosine, sine = sincos_small(rest.astype(F32) * (2.0 * math.pi / 512))
    return rotate_quarter(cosine, sine, quarter)


def times(first, second):
    return (
        first[0] * second[0] - first[1] * second[1],
        first[0] * second[1] + first[1] * second[0],
    )


def cell_roots():
    low = unit_roots(iota((8, 512), 0) * iota((8, 512), 1) & 511)
    high = unit_roots(iota((8, 512), 0) * 8 * iota((8, 512), 1) & 511)
    real, imag = [], []
    for index in range(8):
        row = slice(index, index + 1)
        product = times((high[0][row], high[1][row]), low)
        real.append(product[0])
        imag.append(product[1])
    return jnp.concatenate(real, axis=0), jnp.concatenate(imag, axis=0)


def offset_roots(offsets_ref, count, lead=None):
    rows = iota((count, 512), 0)
    start = jnp.zeros((count, 512), jnp.int32)
    for index in range(count):
        start = jnp.where(rows == index, offsets_ref[index], start)
    steps = start * iota((count, 512), 1)
    real, imag = unit_roots(steps & 511)
    return real * NORM, imag * NORM


def lane_steps(offsets_ref, count, width):
    shape = (8, count * width)
    lane = iota(shape, 1)
    owner = lane // width
    start = jnp.zeros(shape, jnp.int32)
    for index in range(count):
        start = jnp.where(owner == index, offsets_ref[index], start)
    return start + (lane & 63), lane


def lane_roots(frequency, lead):
    row = iota(frequency.shape, 0)
    high = unit_roots((frequency * row * 64) & 511)
    middle = unit_roots((frequency * row * 8) & 511)
    low = unit_roots((frequency * row + lead) & 511)
    low = (low[0] * NORM, low[1] * NORM)
    return high, middle, low


def row_pick(pair, index):
    return pair[0][index : index + 1], pair[1][index : index + 1]


def front_kernel(
    counts_ref, rows_ref, cols_ref, vis_ref, kernels_ref, offsets_ref, out_ref,
    spread, weighted, col_table, row_small, cell, stacked, row_table,
):
    @pl.when(pl.program_id(0) == 0)
    def _():
        slot = iota((8, 128), 0)
        live = counts_ref[0, 0]
        vis = vis_ref[...].astype(F32)
        tile = iota((64, 8, 128), 0)
        for block in range(8):
            lanes = slice(block * VB, (block + 1) * VB)
            rolled, home = [], []
            for axis in range(2):
                shift = slot - offsets_ref[axis, block : block + 1, :]
                values = jnp.zeros((8, VB), F32)
                for column in range(8):
                    entry = kernels_ref[axis, column, block : block + 1, :].astype(F32)
                    values = jnp.where((shift & 7) == column, entry, values)
                rolled.append(values)
                home.append(-(shift >> 3))
            here = tile == home[0][None]
            spread[:, lanes] = jnp.where(here, rolled[0][None], 0.0).reshape(512, VB).astype(BF16)
            here = tile == home[1][None]
            for part in range(2):
                sample = jnp.where(block < live, vis[part, block : block + 1, :], 0.0)
                value = rolled[1] * sample
                weighted[part * 512 : (part + 1) * 512, lanes] = (
                    jnp.where(here, value[None], 0.0).reshape(512, VB).astype(BF16)
                )
        frequency, lane = lane_steps(cols_ref, 8, 128)
        high, middle, low = lane_roots(frequency, jnp.where((lane & 64) == 0, 0, 128))
        for index in range(8):
            outer = row_pick(high, index)
            for inner in range(8):
                real, imag = times(times(outer, row_pick(middle, inner)), low)
                base = index * 64 + inner * 8
                col_table[base : base + 8, :] = real
                col_table[512 + base : 512 + base + 8, :] = imag
        subgrid = dot(spread[...], weighted[...], NT).astype(BF16)
        half = dot(subgrid, col_table[...].astype(BF16))
        stacked[:512, :] = half.astype(BF16)
        sign = jnp.where((iota((1, 128), 1) & 64) == 0, -1.0, 1.0)
        for block in range(8):
            lanes = slice(block * 128, (block + 1) * 128)
            stacked[512:, lanes] = (pltpu.roll(half[:, lanes], 64, 1) * sign).astype(BF16)
        small = offset_roots(rows_ref, 16)
        row_small[0] = small[0]
        row_small[1] = small[1]
        base = cell_roots()
        cell[0] = base[0]
        cell[1] = base[1]

    step = pl.program_id(0)
    base = (cell[0], cell[1])
    for local in range(4):
        row = pl.ds(step * 4 + local, 1)
        real, imag = times((row_small[0, row, :], row_small[1, row, :]), base)
        rows = slice(local * 64, (local + 1) * 64)
        row_table[rows, :512] = real.astype(BF16)
        row_table[rows, 512:] = (-imag).astype(BF16)
    result = dot(row_table[...], stacked[...]).astype(BF16)
    for local in range(4):
        for column in range(8):
            out_ref[local * 8 + column] = result[
                local * 64 : (local + 1) * 64, column * 128 : (column + 1) * 128
            ]


def smem():
    return pl.BlockSpec(memory_space=pltpu.SMEM)


def vmem():
    return pl.BlockSpec(memory_space=pltpu.VMEM)


def front(counts, facet_rows, facet_cols, vis, kernels, offsets):
    return pl.pallas_call(
        front_kernel,
        grid=(4,),
        out_shape=jax.ShapeDtypeStruct((128, 64, 128), BF16),
        in_specs=[smem(), smem(), smem(), vmem(), vmem(), vmem()],
        out_specs=pl.BlockSpec((32, 64, 128), lambda i: (i, 0, 0)),
        scratch_shapes=[
            pltpu.VMEM((512, 1024), BF16),
            pltpu.VMEM((1024, 1024), BF16),
            pltpu.VMEM((1024, 1024), F32),
            pltpu.VMEM((2, 16, 512), F32),
            pltpu.VMEM((2, 64, 512), F32),
            pltpu.VMEM((1024, 1024), BF16),
            pltpu.VMEM((256, 1024), BF16),
        ],
        compiler_params=pltpu.CompilerParams(vmem_limit_bytes=40 << 20),
        cost_estimate=pl.CostEstimate(flops=6 * 10**9, bytes_accessed=4 << 20, transcendentals=0),
        name="front",
    )(counts, facet_rows, facet_cols, vis, kernels, offsets)


def tables_kernel(rows_ref, cols_ref, weight_ref, screen_ref, row_out, col_out, screen_out):
    frequency, lane = lane_steps(rows_ref, 16, 64)
    high, middle, low = lane_roots(frequency, 0)
    for index in range(8):
        outer = row_pick(high, index)
        for inner in range(0, 8, 2):
            first = times(times(outer, row_pick(middle, inner)), low)
            second = times(times(outer, row_pick(middle, inner + 1)), low)
            base = index * 64 + inner * 8
            for part in range(2):
                row_out[base : base + 16, part * 1024 : (part + 1) * 1024] = jnp.concatenate(
                    [first[part], second[part]], axis=0
                ).astype(BF16)
    small = offset_roots(cols_ref, 8)
    base = cell_roots()
    for column in range(8):
        real, imag = times(row_pick(small, column), base)
        real, imag = real.astype(BF16), imag.astype(BF16)
        rows = slice(column * 128, column * 128 + 64)
        col_out[rows, :512] = real
        col_out[rows, 512:] = imag
        rows = slice(column * 128 + 64, column * 128 + 128)
        col_out[rows, :512] = -imag
        col_out[rows, 512:] = real
    weight = weight_ref[0] * 4.0
    for chunk in range(8):
        rows = slice(chunk * 64, (chunk + 1) * 64)
        turns = screen_ref[0, rows, :] * weight
        whole = jnp.floor(turns + 0.5)
        cosine, sine = sincos_small((turns - whole) * (0.5 * math.pi))
        real, imag = rotate_quarter(cosine, sine, whole.astype(jnp.int32))
        screen_out[0, rows, :] = real
        screen_out[1, rows, :] = imag


def tables(sub_rows, sub_cols, weight, screen):
    return pl.pallas_call(
        tables_kernel,
        out_shape=[
            jax.ShapeDtypeStruct((512, 2048), BF16),
            jax.ShapeDtypeStruct((1024, 1024), BF16),
            jax.ShapeDtypeStruct((2, 512, 512), F32),
        ],
        in_specs=[smem(), smem(), smem(), vmem()],
        out_specs=[vmem(), vmem(), vmem()],
        compiler_params=pltpu.CompilerParams(vmem_limit_bytes=40 << 20),
        cost_estimate=pl.CostEstimate(flops=10**9, bytes_accessed=16 << 20, transcendentals=0),
        name="tables",
    )(sub_rows, sub_cols, weight, screen)


def facet_half(blocks_ref, row_ref, col_ref, screen_ref, middle):
    sign = jnp.where((iota((1, 128), 1) & 64) == 0, -1.0, 1.0)
    for pair in range(4):
        placed = jnp.concatenate(
            [blocks_ref[:, 2 * pair + part].reshape(1024, 128) for part in range(2)], axis=1
        )
        straight = dot(row_ref[:, :1024], placed)
        crossed = dot(row_ref[:, 1024:], placed)
        for part in range(2):
            lanes = slice(part * 128, part * 128 + 128)
            middle[:, pair * 256 + part * 128 : pair * 256 + part * 128 + 128] = (
                straight[:, lanes] + pltpu.roll(crossed[:, lanes], 64, 1) * sign
            ).astype(BF16)
    facet = dot(middle[...], col_ref[...])
    real, imag = facet[:, :512], facet[:, 512:]
    cosine, sine = screen_ref[0], screen_ref[1]
    return real * cosine - imag * sine, real * sine + imag * cosine


def back_kernel(half_ref, blocks_ref, row_ref, col_ref, screen_ref, out_ref, middle):
    real, imag = facet_half(blocks_ref, row_ref, col_ref, screen_ref, middle)
    out_ref[0] = real.astype(out_ref.dtype)
    out_ref[1] = imag.astype(out_ref.dtype)


def back(half, blocks, row_table, col_table, screen, dtype, name):
    return pl.pallas_call(
        back_kernel,
        grid_spec=pltpu.PrefetchScalarGridSpec(
            num_scalar_prefetch=1,
            grid=(1,),
            in_specs=[
                pl.BlockSpec((16, 8, 64, 128), lambda i, h: (0, 0, 0, 0)),
                pl.BlockSpec((256, 2048), lambda i, h: (h[0], 0)),
                pl.BlockSpec((1024, 1024), lambda i, h: (0, 0)),
                pl.BlockSpec((2, 256, 512), lambda i, h: (0, h[0], 0)),
            ],
            out_specs=pl.BlockSpec((2, 256, 512), lambda i, h: (0, 0, 0)),
            scratch_shapes=[pltpu.VMEM((256, 1024), BF16)],
        ),
        out_shape=jax.ShapeDtypeStruct((2, 256, 512), dtype),
        compiler_params=pltpu.CompilerParams(vmem_limit_bytes=40 << 20),
        cost_estimate=pl.CostEstimate(flops=2 * 10**9, bytes_accessed=8 << 20, transcendentals=0),
        name=name,
    )(half, blocks, row_table, col_table, screen)


def per_device(
    visibilities, kernels, vis_offsets, block_counts,
    sub_rows, sub_cols, facet_rows, facet_cols, screen_n, layer_w,
):
    outgoing = front(
        block_counts, facet_rows, facet_cols,
        visibilities.reshape(2, 8, VB), kernels.reshape(2, 8, 8, VB), vis_offsets.reshape(2, 8, VB),
    )
    incoming = lax.all_to_all(outgoing, "sf", split_axis=0, concat_axis=0, tiled=True)
    layer = lax.axis_index("wa")
    weight = lax.dynamic_slice_in_dim(layer_w, layer, 1)
    row_table, col_table, screen = tables(sub_rows, sub_cols, weight, screen_n)
    blocks = incoming.reshape(16, 8, CON, 128)
    other = (1 - layer).reshape(1)
    sent = back(other, blocks, row_table, col_table, screen, BF16, "back_other")
    received = lax.ppermute(sent, "wa", [(0, 1), (1, 0)])
    own = back(layer.reshape(1), blocks, row_table, col_table, screen, F32, "back_own")
    return (own + received.astype(F32))[:, None]


def solution(mesh):
    in_specs = (
        P(None, "sf", "wa", None, None),
        P(None, None, "sf", "wa", None, None),
        P(None, "sf", "wa", None, None),
        P("sf", "wa"),
        P(),
        P(),
        P(),
        P(),
        P("sf", None, None),
        P(),
    )
    out_specs = P(None, "sf", "wa", None)
    return jax.shard_map(
        per_device, mesh=mesh, in_specs=in_specs, out_specs=out_specs, check_vma=False
    )
```

profile of v0, /device:TPU:1, one launch (start us, length us, event | category | flops | bytes accessed | tf_op | source)
XLA Modules:
  0.0 91.9 jit_solution(15135355877446117782)
XLA Ops:
  0.7 0.0 copy-start.8
  0.7 0.7 copy-done.8
  1.4 0.7 copy-done.9
  2.1 0.7 copy-done.10
  2.8 0.7 copy-done.11
  3.5 0.7 copy-done.12
  4.1 6.9 %front.1 = bf16[128,64,128]{2,1,0:T(8,128)(2,1)S(1)} custom-call(s32[1,1]{1,0:T(1,128)S(6)} %copy.12.counts_ref, s32[16]{0:T(128)S(1)} %copy-done.11, s32[8]{0:T(128)S(1)} %copy-done.12, bf16[2,8,128]{2,1,0:T(8,128)(2,1)S(1)} %bitcast.14, bf16[2,8,8,128]{3,2,1,0:T(8,128)(2,1)S(1)} %bitcast.12, s32[2,8,128]{2,1,0:T(8,128)S(1)} %bitcast.13), custom_call_target="tpu_custom_call" | custom-call | flops 6000000000 | bytes 4194304 | tf_op jit(solution)/shard_map/front/pallas_call | solution.py:182
  11.0 0.0 copy-start.6
  11.0 1.3 %copy-done.6 = bf16[128,64,128]{2,1,0:T(8,128)(2,1)} copy-done((bf16[128,64,128]{2,1,0:T(8,128)(2,1)}, bf16[128,64,128]{2,1,0:T(8,128)(2,1)S(1)}, u32[]{:S(2)}) %copy-start.6) | copy-done | bytes 2097176
  12.4 16.5 %all-to-all-start = ((bf16[128,64,128]{2,1,0:T(8,128)(2,1)}), bf16[128,64,128]{2,1,0:T(8,128)(2,1)S(1)}, u32[]{:S(2)}, u32[]{:S(2)}) async-start(bf16[128,64,128]{2,1,0:T(8,128)(2,1)} %copy-done.6), calls=%async_computation | async-start | bytes 4194304 | tf_op jit(solution)/shard_map/all_to_all | solution.py:309
  28.9 0.7 dynamic_slice.3.weight_ref
  29.5 4.3 %tables.1 = (bf16[512,2048]{1,0:T(8,128)(2,1)S(1)}, bf16[1024,1024]{1,0:T(8,128)(2,1)S(1)}, f32[2,512,512]{2,1,0:T(8,128)S(1)}) custom-call(s32[16]{0:T(128)S(1)} %copy-done.13, s32[8]{0:T(128)S(1)} %copy-done.14, f32[1]{0:T(128)} %dynamic_slice.3.weight_ref, f32[1,512,512]{2,1,0:T(8,128)S(1)} %copy-done.7), custom_call_target="tpu_custom_call" | custom-call | flops 1000000000 | bytes 16777216 | tf_op jit(solution)/shard_map/tables/pallas_call | solution.py:239
  33.8 1.3 %copy-done = bf16[512,2048]{1,0:T(8,128)(2,1)} copy-done((bf16[512,2048]{1,0:T(8,128)(2,1)}, bf16[512,2048]{1,0:T(8,128)(2,1)S(1)}, u32[]{:S(2)}) %copy-start) | copy-done | bytes 2097176
  35.1 1.4 %copy-done.2 = bf16[1024,1024]{1,0:T(8,128)(2,1)} copy-done((bf16[1024,1024]{1,0:T(8,128)(2,1)}, bf16[1024,1024]{1,0:T(8,128)(2,1)S(1)}, u32[]{:S(2)}) %copy-start.2) | copy-done | bytes 2097176
  36.5 1.4 %copy-done.4 = f32[2,512,512]{2,1,0:T(8,128)} copy-done((f32[2,512,512]{2,1,0:T(8,128)}, f32[2,512,512]{2,1,0:T(8,128)S(1)}, u32[]{:S(2)}) %copy-start.4) | copy-done | bytes 2097176
  37.8 40.3 %all-to-all-done = bf16[128,64,128]{2,1,0:T(8,128)(2,1)S(1)} async-done(((bf16[128,64,128]{2,1,0:T(8,128)(2,1)}), bf16[128,64,128]{2,1,0:T(8,128)(2,1)S(1)}, u32[]{:S(2)}, u32[]{:S(2)}) %all-to-all-start) | async-done | bytes 2097184 | tf_op jit(solution)/shard_map/all_to_all | solution.py:309
  78.1 1.6 %copy-done.1 = bf16[512,2048]{1,0:T(8,128)(2,1)S(1)} copy-done((bf16[512,2048]{1,0:T(8,128)(2,1)S(1)}, bf16[512,2048]{1,0:T(8,128)(2,1)}, u32[]{:S(2)}) %copy-start.1) | copy-done | bytes 2097176
  79.7 1.6 %copy-done.3 = bf16[1024,1024]{1,0:T(8,128)(2,1)S(1)} copy-done((bf16[1024,1024]{1,0:T(8,128)(2,1)S(1)}, bf16[1024,1024]{1,0:T(8,128)(2,1)}, u32[]{:S(2)}) %copy-start.3) | copy-done | bytes 2097176
  81.3 1.6 %copy-done.5 = f32[2,512,512]{2,1,0:T(8,128)S(1)} copy-done((f32[2,512,512]{2,1,0:T(8,128)S(1)}, f32[2,512,512]{2,1,0:T(8,128)}, u32[]{:S(2)}) %copy-start.5) | copy-done | bytes 2097176
  82.9 1.9 %back_other.1 = bf16[2,256,512]{2,1,0:T(8,128)(2,1)S(1)} custom-call(s32[1]{0:T(128)} %bitcast.5.half_ref, bf16[16,8,64,128]{3,2,1,0:T(8,128)(2,1)S(1)} %bitcast.10, bf16[512,2048]{1,0:T(8,128)(2,1)S(1)} %copy-done.1, bf16[1024,1024]{1,0:T(8,128)(2,1)S(1)} %copy-done.3, f32[2,512,512]{2,1,0:T(8,128)S(1)} %copy-done.5), custom_call_target="tpu_custom_call" | custom-call | flops 2000000000 | bytes 8388608 | tf_op jit(solution)/shard_map/back_other/pallas_call | solution.py:280
  84.7 4.1 %collective-permute-start = (bf16[2,256,512]{2,1,0:T(8,128)(2,1)S(1)}, bf16[2,256,512]{2,1,0:T(8,128)(2,1)S(1)}, u32[]{:S(2)}, u32[]{:S(2)}) collective-permute-start(bf16[2,256,512]{2,1,0:T(8,128)(2,1)S(1)} %back_other.1), channel_id=1, source_target_pairs={{0,1},{1,0},{2,3},{3,2},{4,5},{5,4},{6,7},{7,6},{8,9},{9,8},{10,11... | collective-permute-start | bytes 1572872 | tf_op jit(solution)/shard_map/ppermute | solution.py:316
  88.9 1.8 %back_own.1 = f32[2,256,512]{2,1,0:T(8,128)S(1)} custom-call(s32[1]{0:T(128)} %bitcast.half_ref, bf16[16,8,64,128]{3,2,1,0:T(8,128)(2,1)S(1)} %bitcast.11, bf16[512,2048]{1,0:T(8,128)(2,1)S(1)} %copy-done.1, bf16[1024,1024]{1,0:T(8,128)(2,1)S(1)} %copy-done.3, f32[2,512,512]{2,1,0:T(8,128)S(1)} %copy-done.5), custom_call_target="tpu_custom_call" | custom-call | flops 2000000000 | bytes 8388608 | tf_op jit(solution)/shard_map/back_own/pallas_call | solution.py:280
  90.7 0.0 collective-permute-done
  90.7 1.2 %add_bitcast_fusion = f32[2,1,256,512]{3,2,1,0:T(8,128)} fusion(f32[2,256,512]{2,1,0:T(8,128)S(1)} %back_own.1, bf16[2,256,512]{2,1,0:T(8,128)(2,1)S(1)} %collective-permute-done), kind=kLoop, calls=%fused_computation | loop fusion | flops 524288 | bytes 2621440 | tf_op jit(solution)/shard_map/broadcast_in_dim | solution.py:318
  (18 shorter events, 0.0 us)
Async XLA Ops:
  0.7 0.8 copy-start.8
  1.4 0.7 copy-start.9
  2.1 0.7 copy-start.10
  2.8 0.7 copy-start.11
  3.5 0.7 copy-start.12
  11.0 1.3 %copy-start.6 = (bf16[128,64,128]{2,1,0:T(8,128)(2,1)}, bf16[128,64,128]{2,1,0:T(8,128)(2,1)S(1)}, u32[]{:S(2)}) copy-start(bf16[128,64,128]{2,1,0:T(8,128)(2,1)S(1)} %front.1) | copy-start | bytes 6291460
  12.3 16.5 %copy-start.15 = (f32[2]{0:T(128)S(1)}, f32[2]{0:T(128)}, u32[]{:S(2)}) copy-start(f32[2]{0:T(128)} %param.19) | copy-start | bytes 28
  12.3 17.2 %copy-start.7 = (f32[1,512,512]{2,1,0:T(8,128)S(1)}, f32[1,512,512]{2,1,0:T(8,128)}, u32[]{:S(2)}) copy-start(f32[1,512,512]{2,1,0:T(8,128)} %screen_ref.1) | copy-start | bytes 3145732
  12.3 17.2 %copy-start.13 = (s32[16]{0:T(128)S(1)}, s32[16]{0:T(128)}, u32[]{:S(2)}) copy-start(s32[16]{0:T(128)} %rows_ref.3) | copy-start | bytes 196
  12.4 17.2 %copy-start.14 = (s32[8]{0:T(128)S(1)}, s32[8]{0:T(128)}, u32[]{:S(2)}) copy-start(s32[8]{0:T(128)} %cols_ref.3) | copy-start | bytes 100
  12.4 65.7 %all-to-all-start = ((bf16[128,64,128]{2,1,0:T(8,128)(2,1)}), bf16[128,64,128]{2,1,0:T(8,128)(2,1)S(1)}, u32[]{:S(2)}, u32[]{:S(2)}) async-start(bf16[128,64,128]{2,1,0:T(8,128)(2,1)} %copy-done.6), calls=%async_computation | async-start | bytes 4194304 | tf_op jit(solution)/shard_map/all_to_all | solution.py:309
  33.8 1.3 %copy-start = (bf16[512,2048]{1,0:T(8,128)(2,1)}, bf16[512,2048]{1,0:T(8,128)(2,1)S(1)}, u32[]{:S(2)}) copy-start(bf16[512,2048]{1,0:T(8,128)(2,1)S(1)} %get-tuple-element.8.row_ref) | copy-start | bytes 6291460
  35.1 1.4 %copy-start.2 = (bf16[1024,1024]{1,0:T(8,128)(2,1)}, bf16[1024,1024]{1,0:T(8,128)(2,1)S(1)}, u32[]{:S(2)}) copy-start(bf16[1024,1024]{1,0:T(8,128)(2,1)S(1)} %get-tuple-element.9.col_ref) | copy-start | bytes 6291460
  36.5 1.4 %copy-start.4 = (f32[2,512,512]{2,1,0:T(8,128)}, f32[2,512,512]{2,1,0:T(8,128)S(1)}, u32[]{:S(2)}) copy-start(f32[2,512,512]{2,1,0:T(8,128)S(1)} %get-tuple-element.10.screen_ref) | copy-start | bytes 6291460
  78.1 1.6 %copy-start.1 = (bf16[512,2048]{1,0:T(8,128)(2,1)S(1)}, bf16[512,2048]{1,0:T(8,128)(2,1)}, u32[]{:S(2)}) copy-start(bf16[512,2048]{1,0:T(8,128)(2,1)} %copy-done) | copy-start | bytes 6291460
  79.7 1.6 %copy-start.3 = (bf16[1024,1024]{1,0:T(8,128)(2,1)S(1)}, bf16[1024,1024]{1,0:T(8,128)(2,1)}, u32[]{:S(2)}) copy-start(bf16[1024,1024]{1,0:T(8,128)(2,1)} %copy-done.2) | copy-start | bytes 6291460
  81.3 1.6 %copy-start.5 = (f32[2,512,512]{2,1,0:T(8,128)S(1)}, f32[2,512,512]{2,1,0:T(8,128)}, u32[]{:S(2)}) copy-start(f32[2,512,512]{2,1,0:T(8,128)} %copy-done.4) | copy-start | bytes 6291460
  84.7 6.0 %collective-permute-start = (bf16[2,256,512]{2,1,0:T(8,128)(2,1)S(1)}, bf16[2,256,512]{2,1,0:T(8,128)(2,1)S(1)}, u32[]{:S(2)}, u32[]{:S(2)}) collective-permute-start(bf16[2,256,512]{2,1,0:T(8,128)(2,1)S(1)} %back_other.1), channel_id=1, source_target_pairs={{0,1},{1,0},{2,3},{3,2},{4,5},{5,4},{6,7},{7,6},{8,9},{9,8},{10,11... | collective-permute-start | bytes 1572872 | tf_op jit(solution)/shard_map/ppermute | solution.py:316
where the time goes:
time: 92.3 us; the launch traced here: 91.9 us
  waiting for transfers between devices  40.3 us (44%)
  starting transfers between devices  20.6 us (22%)
  Pallas kernels  14.8 us (16%)
  local copies, waits for them, and re-layouts  14.2 us (15%)
  other arithmetic  1.16 us (1%)
    all_to_all x1, waiting for transfers between devices, per_device(): lax.all_to_all(outgoing, 'sf', split_axis=0, concat_axis=0, tiled=True)  40.3 us
    all_to_all x1, starting transfers between devices, per_device(): lax.all_to_all(outgoing, 'sf', split_axis=0, concat_axis=0, tiled=True)  16.5 us
    unnamed x32, local copies, waits for them, and re-layouts  13.6 us
    pallas_call x1, Pallas kernels, front(): pl.pallas_call(front_kernel, grid=(4,), out_shape=jax.ShapeDtypeStruct((1...  6.89 us
    pallas_call x1, Pallas kernels, tables(): pl.pallas_call(tables_kernel, out_shape=[jax.ShapeDtypeStruct((512, 2048)...  4.27 us
    ppermute x1, starting transfers between devices, per_device(): received = lax.ppermute(sent, 'wa', [(0, 1), (1, 0)])  4.13 us
    pallas_call x2, Pallas kernels, back(): pl.pallas_call(back_kernel, grid_spec=pltpu.PrefetchScalarGridSpec(num_sc...  3.7 us
  transfers between devices with their start and end apart: 2, of which 1 were waited for; matrix products, arithmetic and copies ran while one was open for 1% of the time, Pallas kernels for 7%

commit v1 on v0

--- a/solution.py
+++ b/solution.py
@@ -68,7 +68,7 @@
     return jnp.concatenate(real, axis=0), jnp.concatenate(imag, axis=0)
 
 
-def offset_roots(offsets_ref, count, lead=None):
+def offset_roots(offsets_ref, count):
     rows = iota((count, 512), 0)
     start = jnp.zeros((count, 512), jnp.int32)
     for index in range(count):
@@ -101,108 +101,41 @@
     return pair[0][index : index + 1], pair[1][index : index + 1]
 
 
-def front_kernel(
-    counts_ref, rows_ref, cols_ref, vis_ref, kernels_ref, offsets_ref, out_ref,
-    spread, weighted, col_table, row_small, cell, stacked, row_table,
-):
-    @pl.when(pl.program_id(0) == 0)
-    def _():
-        slot = iota((8, 128), 0)
-        live = counts_ref[0, 0]
-        vis = vis_ref[...].astype(F32)
-        tile = iota((64, 8, 128), 0)
+def pack_kernel(counts_ref, vis_ref, kernels_ref, offsets_ref, out_ref):
+    live = counts_ref[0, 0]
+    slot = iota((8, 128), 0)
+    samples = [jnp.where(slot < live, vis_ref[part].astype(F32), 0.0) for part in range(2)]
+    out_ref[0:16, :] = jnp.concatenate(samples, axis=0).astype(BF16)
+    for axis in range(2):
+        offsets = offsets_ref[axis]
+        low = offsets & 7
+        digits = jnp.concatenate([(offsets >> 3).astype(F32), low.astype(F32)], axis=0)
+        out_ref[16 + axis * 16 : 32 + axis * 16, :] = digits.astype(BF16)
+        turned = []
         for block in range(8):
-            lanes = slice(block * VB, (block + 1) * VB)
-            rolled, home = [], []
-            for axis in range(2):
-                shift = slot - offsets_ref[axis, block : block + 1, :]
-                values = jnp.zeros((8, VB), F32)
-                for column in range(8):
-                    entry = kernels_ref[axis, column, block : block + 1, :].astype(F32)
-                    values = jnp.where((shift & 7) == column, entry, values)
-                rolled.append(values)
-                home.append(-(shift >> 3))
-            here = tile == home[0][None]
-            spread[:, lanes] = jnp.where(here, rolled[0][None], 0.0).reshape(512, VB).astype(BF16)
-            here = tile == home[1][None]
-            for part in range(2):
-                sample = jnp.where(block < live, vis[part, block : block + 1, :], 0.0)
-                value = rolled[1] * sample
-                weighted[part * 512 : (part + 1) * 512, lanes] = (
-                    jnp.where(here, value[None], 0.0).reshape(512, VB).astype(BF16)
-                )
-        frequency, lane = lane_steps(cols_ref, 8, 128)
-        high, middle, low = lane_roots(frequency, jnp.where((lane & 64) == 0, 0, 128))
-        for index in range(8):
-            outer = row_pick(high, index)
-            for inner in range(8):
-                real, imag = times(times(outer, row_pick(middle, inner)), low)
-                base = index * 64 + inner * 8
-                col_table[base : base + 8, :] = real
-                col_table[512 + base : 512 + base + 8, :] = imag
-        subgrid = dot(spread[...], weighted[...], NT).astype(BF16)
-        half = dot(subgrid, col_table[...].astype(BF16))
-        stacked[:512, :] = half.astype(BF16)
-        sign = jnp.where((iota((1, 128), 1) & 64) == 0, -1.0, 1.0)
-        for block in range(8):
-            lanes = slice(block * 128, (block + 1) * 128)
-            stacked[512:, lanes] = (pltpu.roll(half[:, lanes], 64, 1) * sign).astype(BF16)
-        small = offset_roots(rows_ref, 16)
-        row_small[0] = small[0]
-        row_small[1] = small[1]
-        base = cell_roots()
-        cell[0] = base[0]
-        cell[1] = base[1]
-
-    step = pl.program_id(0)
-    base = (cell[0], cell[1])
-    for local in range(4):
-        row = pl.ds(step * 4 + local, 1)
-        real, imag = times((row_small[0, row, :], row_small[1, row, :]), base)
-        rows = slice(local * 64, (local + 1) * 64)
-        row_table[rows, :512] = real.astype(BF16)
-        row_table[rows, 512:] = (-imag).astype(BF16)
-    result = dot(row_table[...], stacked[...]).astype(BF16)
-    for local in range(4):
-        for column in range(8):
-            out_ref[local * 8 + column] = result[
-                local * 64 : (local + 1) * 64, column * 128 : (column + 1) * 128
-            ]
-
-
-def smem():
-    return pl.BlockSpec(memory_space=pltpu.SMEM)
-
-
-def vmem():
-    return pl.BlockSpec(memory_space=pltpu.VMEM)
-
-
-def front(counts, facet_rows, facet_cols, vis, kernels, offsets):
-    return pl.pallas_call(
-        front_kernel,
-        grid=(4,),
-        out_shape=jax.ShapeDtypeStruct((128, 64, 128), BF16),
-        in_specs=[smem(), smem(), smem(), vmem(), vmem(), vmem()],
-        out_specs=pl.BlockSpec((32, 64, 128), lambda i: (i, 0, 0)),
-        scratch_shapes=[
-            pltpu.VMEM((512, 1024), BF16),
-            pltpu.VMEM((1024, 1024), BF16),
-            pltpu.VMEM((1024, 1024), F32),
-            pltpu.VMEM((2, 16, 512), F32),
-            pltpu.VMEM((2, 64, 512), F32),
-            pltpu.VMEM((1024, 1024), BF16),
-            pltpu.VMEM((256, 1024), BF16),
-        ],
-        compiler_params=pltpu.CompilerParams(vmem_limit_bytes=40 << 20),
-        cost_estimate=pl.CostEstimate(flops=6 * 10**9, bytes_accessed=4 << 20, transcendentals=0),
-        name="front",
-    )(counts, facet_rows, facet_cols, vis, kernels, offsets)
-
-
-def tables_kernel(rows_ref, cols_ref, weight_ref, screen_ref, row_out, col_out, screen_out):
-    frequency, lane = lane_steps(rows_ref, 16, 64)
-    high, middle, low = lane_roots(frequency, 0)
+            shift = (slot - low[block : block + 1, :]) & 7
+            values = jnp.zeros((8, VB), F32)
+            for column in range(8):
+                entry = kernels_ref[axis, column, block : block + 1, :].astype(F32)
+                values = jnp.where(shift == column, entry, values)
+            turned.append(values)
+        out_ref[48 + axis * 64 : 112 + axis * 64, :] = jnp.concatenate(turned, axis=0).astype(BF16)
+
+
+def pack(counts, vis, kernels, offsets):
+    return pl.pallas_call(
+        pack_kernel,
+        out_shape=jax.ShapeDtypeStruct((176, 128), BF16),
+        in_specs=[smem(), vmem(), vmem(), vmem()],
+        out_specs=vmem(),
+        compiler_params=pltpu.CompilerParams(vmem_limit_bytes=4 << 20),
+        name="pack",
+    )(counts, vis, kernels, offsets)
+
+
+def lane_table(offsets_ref, count, width, lead, out_ref, place):
+    frequency, lane = lane_steps(offsets_ref, count, width)
+    high, middle, low = lane_roots(frequency, jnp.where((lane & lead) == 0, 0, 128))
     for index in range(8):
         outer = row_pick(high, index)
         for inner in range(0, 8, 2):
@@ -210,9 +143,114 @@
             second = times(times(outer, row_pick(middle, inner + 1)), low)
             base = index * 64 + inner * 8
             for part in range(2):
-                row_out[base : base + 16, part * 1024 : (part + 1) * 1024] = jnp.concatenate(
-                    [first[part], second[part]], axis=0
-                ).astype(BF16)
+                place(out_ref, part, base, jnp.concatenate([first[part], second[part]], axis=0).astype(BF16))
+
+
+def facet_tables_kernel(group_ref, rows_ref, cols_ref, row_out, col_out):
+    def below(ref, part, base, value):
+        ref[part * 512 + base : part * 512 + base + 16, :] = value
+
+    lane_table(cols_ref, 8, 128, 64, col_out, below)
+    base = cell_roots()
+    small = offset_roots([rows_ref[4 * index + group_ref[0]] for index in range(4)], 4)
+    for index in range(4):
+        real, imag = times(row_pick(small, index), base)
+        row_out[index * 64 : index * 64 + 64, :] = real.astype(BF16)
+        row_out[256 + index * 64 : 320 + index * 64, :] = (-imag).astype(BF16)
+
+
+def facet_tables(group, facet_rows, facet_cols):
+    return pl.pallas_call(
+        facet_tables_kernel,
+        out_shape=[
+            jax.ShapeDtypeStruct((512, 512), BF16),
+            jax.ShapeDtypeStruct((1024, 1024), BF16),
+        ],
+        in_specs=[smem(), smem(), smem()],
+        out_specs=[vmem(), vmem()],
+        compiler_params=pltpu.CompilerParams(vmem_limit_bytes=8 << 20),
+        cost_estimate=pl.CostEstimate(flops=10**9, bytes_accessed=4 << 20, transcendentals=0),
+        name="facet_tables",
+    )(group, facet_rows, facet_cols)
+
+
+def front_kernel(
+    group_ref, own_ref, first_ref, second_ref, third_ref, row_ref, col_ref, out_ref,
+    packs, spread, second_spread, turned, halves,
+):
+    step = pl.program_id(0)
+
+    @pl.when(step == 0)
+    def _():
+        for index, ref in enumerate((own_ref, first_ref, second_ref, third_ref)):
+            packs[index] = ref[...]
+
+    slot = iota((8, 128), 0)
+    tile = iota((64, 8, 128), 0)
+    samples = packs[step, 0:16, :].astype(F32)
+    for axis, target in ((0, spread), (1, second_spread)):
+        digits = packs[step, 16 + axis * 16 : 32 + axis * 16, :].astype(jnp.int32)
+        kernels = packs[step, 48 + axis * 64 : 112 + axis * 64, :].astype(F32)
+        for block in range(8):
+            home = digits[block : block + 1, :] + (digits[block + 8 : block + 9, :] > slot).astype(jnp.int32)
+            values = kernels[block * 8 : block * 8 + 8, :]
+            target[:, block * VB : (block + 1) * VB] = (
+                jnp.where(tile == home[None], values[None], 0.0).reshape(512, VB).astype(BF16)
+            )
+    for quarter in range(4):
+        lanes = slice(quarter * 256, (quarter + 1) * 256)
+        rows = dot(row_ref[...], spread[:, lanes])
+        real_part = jnp.concatenate([samples[2 * quarter + part : 2 * quarter + part + 1] for part in range(2)], axis=1)
+        imag_part = jnp.concatenate([samples[2 * quarter + part + 8 : 2 * quarter + part + 9] for part in range(2)], axis=1)
+        real, imag = times((rows[:256], rows[256:]), (real_part, imag_part))
+        turned[:256, lanes] = real.astype(BF16)
+        turned[256:, lanes] = imag.astype(BF16)
+    half = dot(turned[...], second_spread[...], NT).astype(BF16)
+    halves[:, :512] = half[:256]
+    halves[:, 512:] = half[256:]
+    result = dot(halves[...], col_ref[...]).astype(BF16)
+    for row in range(4):
+        for column in range(8):
+            out_ref[row * 8 + column, 0] = result[row * 64 : (row + 1) * 64, column * 128 : (column + 1) * 128]
+
+
+def smem():
+    return pl.BlockSpec(memory_space=pltpu.SMEM)
+
+
+def vmem():
+    return pl.BlockSpec(memory_space=pltpu.VMEM)
+
+
+def front(group, packs, row_table, col_table):
+    whole = lambda *shape: pl.BlockSpec(shape, lambda i, g: (0,) * len(shape))
+    return pl.pallas_call(
+        front_kernel,
+        grid_spec=pltpu.PrefetchScalarGridSpec(
+            num_scalar_prefetch=1,
+            grid=(4,),
+            in_specs=[whole(176, 128)] * 4 + [whole(512, 512), whole(1024, 1024)],
+            out_specs=pl.BlockSpec((32, 1, 64, 128), lambda i, g: (0, (g[0] + 4 - i) & 3, 0, 0)),
+            scratch_shapes=[
+                pltpu.VMEM((4, 176, 128), BF16),
+                pltpu.VMEM((512, 1024), BF16),
+                pltpu.VMEM((512, 1024), BF16),
+                pltpu.VMEM((512, 1024), BF16),
+                pltpu.VMEM((256, 1024), BF16),
+            ],
+        ),
+        out_shape=jax.ShapeDtypeStruct((32, 4, 64, 128), BF16),
+        compiler_params=pltpu.CompilerParams(vmem_limit_bytes=20 << 20),
+        cost_estimate=pl.CostEstimate(flops=6 * 10**9, bytes_accessed=4 << 20, transcendentals=0),
+        name="front",
+    )(group, *packs, row_table, col_table)
+
+
+def tables_kernel(rows_ref, cols_ref, weight_ref, screen_ref, row_out, col_out, screen_out):
+    def beside(ref, part, base, value):
+        ref[base : base + 16, part * 1024 : (part + 1) * 1024] = value
+
+    lane_table(rows_ref, 16, 64, 0, row_out, beside)
     small = offset_roots(cols_ref, 8)
     base = cell_roots()
     for column in range(8):
@@ -245,7 +283,7 @@
         ],
         in_specs=[smem(), smem(), smem(), vmem()],
         out_specs=[vmem(), vmem(), vmem()],
-        compiler_params=pltpu.CompilerParams(vmem_limit_bytes=40 << 20),
+        compiler_params=pltpu.CompilerParams(vmem_limit_bytes=20 << 20),
         cost_estimate=pl.CostEstimate(flops=10**9, bytes_accessed=16 << 20, transcendentals=0),
         name="tables",
     )(sub_rows, sub_cols, weight, screen)
@@ -283,7 +321,7 @@
             num_scalar_prefetch=1,
             grid=(1,),
             in_specs=[
-                pl.BlockSpec((16, 8, 64, 128), lambda i, h: (0, 0, 0, 0)),
+                pl.BlockSpec((4, 8, 4, 64, 128), lambda i, h: (0, 0, 0, 0, 0)),
                 pl.BlockSpec((256, 2048), lambda i, h: (h[0], 0)),
                 pl.BlockSpec((1024, 1024), lambda i, h: (0, 0)),
                 pl.BlockSpec((2, 256, 512), lambda i, h: (0, h[0], 0)),
@@ -292,25 +330,47 @@
             scratch_shapes=[pltpu.VMEM((256, 1024), BF16)],
         ),
         out_shape=jax.ShapeDtypeStruct((2, 256, 512), dtype),
-        compiler_params=pltpu.CompilerParams(vmem_limit_bytes=40 << 20),
+        compiler_params=pltpu.CompilerParams(vmem_limit_bytes=20 << 20),
         cost_estimate=pl.CostEstimate(flops=2 * 10**9, bytes_accessed=8 << 20, transcendentals=0),
         name=name,
     )(half, blocks, row_table, col_table, screen)
+
+
+def position(x, z, y):
+    return x * 32 + (z % 8) * 4 + y
+
+
+GROUPS = [
+    [position(x, 2 * k + l, y) for x in range(4) for l in range(2) for y in range(4)] for k in range(4)
+]
+
+
+def shifted(turn):
+    return [
+        (position(x, z, y), position(x, z + 2 * turn, y)) for x in range(4) for z in range(8) for y in range(4)
+    ]
 
 
 def per_device(
     visibilities, kernels, vis_offsets, block_counts,
     sub_rows, sub_cols, facet_rows, facet_cols, screen_n, layer_w,
 ):
-    outgoing = front(
-        block_counts, facet_rows, facet_cols,
+    place = lax.axis_index("sf")
+    group = ((place >> 3) & 3).reshape(1)
+    own = pack(
+        block_counts,
         visibilities.reshape(2, 8, VB), kernels.reshape(2, 8, 8, VB), vis_offsets.reshape(2, 8, VB),
     )
-    incoming = lax.all_to_all(outgoing, "sf", split_axis=0, concat_axis=0, tiled=True)
+    packs = [own] + [lax.ppermute(own, "sf", shifted(turn)) for turn in (1, 2, 3)]
+    facet_row_table, facet_col_table = facet_tables(group, facet_rows, facet_cols)
+    outgoing = front(group, packs, facet_row_table, facet_col_table)
+    incoming = lax.all_to_all(
+        outgoing, "sf", split_axis=0, concat_axis=0, tiled=True, axis_index_groups=GROUPS
+    )
     layer = lax.axis_index("wa")
     weight = lax.dynamic_slice_in_dim(layer_w, layer, 1)
     row_table, col_table, screen = tables(sub_rows, sub_cols, weight, screen_n)
-    blocks = incoming.reshape(16, 8, CON, 128)
+    blocks = incoming.reshape(4, 8, 4, CON, 128)
     other = (1 - layer).reshape(1)
     sent = back(other, blocks, row_table, col_table, screen, BF16, "back_other")
     received = lax.ppermute(sent, "wa", [(0, 1), (1, 0)])

time: 92.3 us -> 73 us (0.79)
  waiting for transfers between devices: 40.3 us -> 16.7 us
  Pallas kernels: 14.8 us -> 18.2 us
    all_to_all x1, waiting for transfers between devices: 40.3 us -> 16.3 us  [per_device(): lax.all_to_all(outgoing, 'sf', split_axis=0, concat_axis=0, tiled=True, a...]
    ppermute x0 -> x3, starting transfers between devices: none -> 10.2 us  [per_device(): lax.ppermute(own, 'sf', shifted(turn))]
    all_to_all x1, starting transfers between devices: 16.5 us -> 7.67 us  [per_device(): lax.all_to_all(outgoing, 'sf', split_axis=0, concat_axis=0, tiled=True, a...]
    pallas_call x1 -> x3, Pallas kernels: 6.89 us -> 10.3 us  [the longest x1 8.19 us: front(): pl.pallas_call(front_kernel, grid_spec=pltpu.PrefetchScalarGridSpec(num_s...]
  transfers between devices with their start and end apart: 2 -> 5, of which waited for: 1 -> 2; matrix products, arithmetic and copies ran while one was open for 1% -> 1% of each run, Pallas kernels for 7% -> 11%
where the time goes in v1:
time: 73 us; the launch traced here: 72.5 us
  starting transfers between devices  21.5 us (29%)
  Pallas kernels  18.2 us (25%)
  waiting for transfers between devices  16.7 us (23%)
  local copies, waits for them, and re-layouts  14.2 us (19%)
  other arithmetic  1.16 us (2%)
  between operations  0.77 us (1%)
    all_to_all x1, waiting for transfers between devices, per_device(): lax.all_to_all(outgoing, 'sf', split_axis=0, concat_axis=0, tiled=True, a...  16.3 us
    unnamed x32, local copies, waits for them, and re-layouts  13.6 us
    ppermute x3, starting transfers between devices, per_device(): lax.ppermute(own, 'sf', shifted(turn))  10.2 us
    pallas_call x1, Pallas kernels, front(): pl.pallas_call(front_kernel, grid_spec=pltpu.PrefetchScalarGridSpec(num_s...  8.19 us
    all_to_all x1, starting transfers between devices, per_device(): lax.all_to_all(outgoing, 'sf', split_axis=0, concat_axis=0, tiled=True, a...  7.67 us
    pallas_call x1, Pallas kernels, tables(): pl.pallas_call(tables_kernel, out_shape=[jax.ShapeDtypeStruct((512, 2048)...  4.22 us
    pallas_call x2, Pallas kernels, back(): pl.pallas_call(back_kernel, grid_spec=pltpu.PrefetchScalarGridSpec(num_sc...  3.69 us
    ppermute x1, starting transfers between devices, per_device(): received = lax.ppermute(sent, 'wa', [(0, 1), (1, 0)])  3.68 us
  transfers between devices with their start and end apart: 5, of which 2 were waited for; matrix products, arithmetic and copies ran while one was open for 1% of the time, Pallas kernels for 11%

profile of v1, /device:TPU:1, one launch (start us, length us, event | category | flops | bytes accessed | tf_op | source)
XLA Modules:
  0.0 72.5 jit_solution(4367177472334271346)
XLA Ops:
  0.7 0.7 %copy-done.7 = bf16[2,8,1,1,8,128]{5,4,3,2,1,0:T(8,128)(2,1)S(1)} copy-done((bf16[2,8,1,1,8,128]{5,4,3,2,1,0:T(8,128)(2,1)S(1)}, bf16[2,8,1,1,8,128]{5,4,3,2,1,0:T(8,128)(2,1)}, u32[]{:S(2)}) %copy-start.7) | copy-done | bytes 32792
  1.4 0.7 copy-done.8
  2.1 0.7 copy-done.9
  2.9 6.9 %collective-permute-start.2 = (bf16[176,128]{1,0:T(8,128)(2,1)S(1)}, bf16[176,128]{1,0:T(8,128)(2,1)S(1)}, u32[]{:S(2)}, u32[]{:S(2)}) collective-permute-start(bf16[176,128]{1,0:T(8,128)(2,1)S(1)} %pack.1.own_ref), channel_id=1, source_target_pairs={{0,48},{2,50},{4,52},{6,54},{8,56},{10,58},{12,60},{14,62},{16,0},... | collective-permute-start | bytes 135176 | tf_op jit(solution)/shard_map/ppermute | solution.py:364
  9.8 1.0 %collective-permute-start.1 = (bf16[176,128]{1,0:T(8,128)(2,1)S(1)}, bf16[176,128]{1,0:T(8,128)(2,1)S(1)}, u32[]{:S(2)}, u32[]{:S(2)}) collective-permute-start(bf16[176,128]{1,0:T(8,128)(2,1)S(1)} %pack.1.own_ref), channel_id=1, source_target_pairs={{0,32},{2,34},{4,36},{6,38},{8,40},{10,42},{12,44},{14,46},{16,48}... | collective-permute-start | bytes 135176 | tf_op jit(solution)/shard_map/ppermute | solution.py:364
  10.8 2.3 %collective-permute-start = (bf16[176,128]{1,0:T(8,128)(2,1)S(1)}, bf16[176,128]{1,0:T(8,128)(2,1)S(1)}, u32[]{:S(2)}, u32[]{:S(2)}) collective-permute-start(bf16[176,128]{1,0:T(8,128)(2,1)S(1)} %pack.1.own_ref), channel_id=1, source_target_pairs={{0,16},{2,18},{4,20},{6,22},{8,24},{10,26},{12,28},{14,30},{16,32}... | collective-permute-start | bytes 135176 | tf_op jit(solution)/shard_map/ppermute | solution.py:364
  13.1 0.7 copy-done.11
  13.7 0.7 copy-done.12
  14.4 2.0 %facet_tables.1 = (bf16[512,512]{1,0:T(8,128)(2,1)S(1)}, bf16[1024,1024]{1,0:T(8,128)(2,1)S(1)}) custom-call(s32[1]{0:T(128)} %bitcast.1.group_ref, s32[16]{0:T(128)S(1)} %copy-done.11, s32[8]{0:T(128)S(1)} %copy-done.12), custom_call_target="tpu_custom_call" | custom-call | flops 1000000000 | bytes 4194304 | tf_op jit(solution)/shard_map/facet_tables/pallas_call | solution.py:163
  16.8 8.2 %front.1 = bf16[32,4,64,128]{3,2,1,0:T(8,128)(2,1)S(1)} custom-call(s32[1]{0:T(128)} %bitcast.1.group_ref, bf16[176,128]{1,0:T(8,128)(2,1)S(1)} %pack.1.own_ref, bf16[176,128]{1,0:T(8,128)(2,1)S(1)} %collective-permute-done.first_ref, bf16[176,128]{1,0:T(8,128)(2,1)S(1)} %collective-permute-done.1.second_ref, ...), custom_call_target="tpu_custom_call" | custom-call | flops 6000000000 | bytes 4194304 | tf_op jit(solution)/shard_map/front/pallas_call | solution.py:227
  25.0 1.3 %copy-done.6 = bf16[32,4,64,128]{3,2,1,0:T(8,128)(2,1)} copy-done((bf16[32,4,64,128]{3,2,1,0:T(8,128)(2,1)}, bf16[32,4,64,128]{3,2,1,0:T(8,128)(2,1)S(1)}, u32[]{:S(2)}) %copy-start.6) | copy-done | bytes 2097176
  26.3 7.7 %all-to-all-start = ((bf16[32,4,64,128]{3,2,1,0:T(8,128)(2,1)}), bf16[32,4,64,128]{3,2,1,0:T(8,128)(2,1)S(1)}, u32[]{:S(2)}, u32[]{:S(2)}) async-start(bf16[32,4,64,128]{3,2,1,0:T(8,128)(2,1)} %copy-done.6), calls=%async_computation | async-start | bytes 4194304 | tf_op jit(solution)/shard_map/all_to_all | solution.py:367
  34.6 4.2 %tables.1 = (bf16[512,2048]{1,0:T(8,128)(2,1)S(1)}, bf16[1024,1024]{1,0:T(8,128)(2,1)S(1)}, f32[2,512,512]{2,1,0:T(8,128)S(1)}) custom-call(s32[16]{0:T(128)S(1)} %copy-done.13, s32[8]{0:T(128)S(1)} %copy-done.14, f32[1]{0:T(128)} %dynamic_slice.3.weight_ref, f32[1,512,512]{2,1,0:T(8,128)S(1)} %copy-done.10), custom_call_target="tpu_custom_call" | custom-call | flops 1000000000 | bytes 16777216 | tf_op jit(solution)/shard_map/tables/pallas_call | solution.py:277
  38.9 1.3 %copy-done = bf16[512,2048]{1,0:T(8,128)(2,1)} copy-done((bf16[512,2048]{1,0:T(8,128)(2,1)}, bf16[512,2048]{1,0:T(8,128)(2,1)S(1)}, u32[]{:S(2)}) %copy-start) | copy-done | bytes 2097176
  40.2 1.3 %copy-done.2 = bf16[1024,1024]{1,0:T(8,128)(2,1)} copy-done((bf16[1024,1024]{1,0:T(8,128)(2,1)}, bf16[1024,1024]{1,0:T(8,128)(2,1)S(1)}, u32[]{:S(2)}) %copy-start.2) | copy-done | bytes 2097176
  41.5 1.4 %copy-done.4 = f32[2,512,512]{2,1,0:T(8,128)} copy-done((f32[2,512,512]{2,1,0:T(8,128)}, f32[2,512,512]{2,1,0:T(8,128)S(1)}, u32[]{:S(2)}) %copy-start.4) | copy-done | bytes 2097176
  42.9 16.3 %all-to-all-done = bf16[32,4,64,128]{3,2,1,0:T(8,128)(2,1)S(1)} async-done(((bf16[32,4,64,128]{3,2,1,0:T(8,128)(2,1)}), bf16[32,4,64,128]{3,2,1,0:T(8,128)(2,1)S(1)}, u32[]{:S(2)}, u32[]{:S(2)}) %all-to-all-start) | async-done | bytes 2097184 | tf_op jit(solution)/shard_map/all_to_all | solution.py:367
  59.2 1.6 %copy-done.1 = bf16[512,2048]{1,0:T(8,128)(2,1)S(1)} copy-done((bf16[512,2048]{1,0:T(8,128)(2,1)S(1)}, bf16[512,2048]{1,0:T(8,128)(2,1)}, u32[]{:S(2)}) %copy-start.1) | copy-done | bytes 2097176
  60.8 1.6 %copy-done.3 = bf16[1024,1024]{1,0:T(8,128)(2,1)S(1)} copy-done((bf16[1024,1024]{1,0:T(8,128)(2,1)S(1)}, bf16[1024,1024]{1,0:T(8,128)(2,1)}, u32[]{:S(2)}) %copy-start.3) | copy-done | bytes 2097176
  62.4 1.6 %copy-done.5 = f32[2,512,512]{2,1,0:T(8,128)S(1)} copy-done((f32[2,512,512]{2,1,0:T(8,128)S(1)}, f32[2,512,512]{2,1,0:T(8,128)}, u32[]{:S(2)}) %copy-start.5) | copy-done | bytes 2097176
  64.0 1.8 %back_other.1 = bf16[2,256,512]{2,1,0:T(8,128)(2,1)S(1)} custom-call(s32[1]{0:T(128)} %bitcast.6.half_ref, bf16[4,8,4,64,128]{4,3,2,1,0:T(8,128)(2,1)S(1)} %bitcast.11, bf16[512,2048]{1,0:T(8,128)(2,1)S(1)} %copy-done.1, bf16[1024,1024]{1,0:T(8,128)(2,1)S(1)} %copy-done.3, f32[2,512,512]{2,1,0:T(8,128)S(1)} %copy-done.5), custom_call_target="tpu_custom_call" | custom-call | flops 2000000000 | bytes 8388608 | tf_op jit(solution)/shard_map/back_other/pallas_call | solution.py:318
  65.8 3.7 %collective-permute-start.3 = (bf16[2,256,512]{2,1,0:T(8,128)(2,1)S(1)}, bf16[2,256,512]{2,1,0:T(8,128)(2,1)S(1)}, u32[]{:S(2)}, u32[]{:S(2)}) collective-permute-start(bf16[2,256,512]{2,1,0:T(8,128)(2,1)S(1)} %back_other.1), channel_id=1, source_target_pairs={{0,1},{1,0},{2,3},{3,2},{4,5},{5,4},{6,7},{7,6},{8,9},{9,8},{10,11... | collective-permute-start | bytes 1572872 | tf_op jit(solution)/shard_map/ppermute | solution.py:376
  69.5 1.8 %back_own.1 = f32[2,256,512]{2,1,0:T(8,128)S(1)} custom-call(s32[1]{0:T(128)} %bitcast.half_ref, bf16[4,8,4,64,128]{4,3,2,1,0:T(8,128)(2,1)S(1)} %bitcast.12, bf16[512,2048]{1,0:T(8,128)(2,1)S(1)} %copy-done.1, bf16[1024,1024]{1,0:T(8,128)(2,1)S(1)} %copy-done.3, f32[2,512,512]{2,1,0:T(8,128)S(1)} %copy-done.5), custom_call_target="tpu_custom_call" | custom-call | flops 2000000000 | bytes 8388608 | tf_op jit(solution)/shard_map/back_own/pallas_call | solution.py:318
  71.4 1.2 %add_bitcast_fusion = f32[2,1,256,512]{3,2,1,0:T(8,128)} fusion(f32[2,256,512]{2,1,0:T(8,128)S(1)} %back_own.1, bf16[2,256,512]{2,1,0:T(8,128)(2,1)S(1)} %collective-permute-done.3), kind=kLoop, calls=%fused_computation | loop fusion | flops 524288 | bytes 2621440 | tf_op jit(solution)/shard_map/broadcast_in_dim | solution.py:378
  (26 shorter events, 1.1 us)
Async XLA Ops:
  0.7 0.8 %copy-start.7 = (bf16[2,8,1,1,8,128]{5,4,3,2,1,0:T(8,128)(2,1)S(1)}, bf16[2,8,1,1,8,128]{5,4,3,2,1,0:T(8,128)(2,1)}, u32[]{:S(2)}) copy-start(bf16[2,8,1,1,8,128]{5,4,3,2,1,0:T(8,128)(2,1)} %param.11) | copy-start | bytes 98308
  1.4 0.7 copy-start.8
  2.1 0.7 copy-start.9
  2.9 13.5 %collective-permute-start.2 = (bf16[176,128]{1,0:T(8,128)(2,1)S(1)}, bf16[176,128]{1,0:T(8,128)(2,1)S(1)}, u32[]{:S(2)}, u32[]{:S(2)}) collective-permute-start(bf16[176,128]{1,0:T(8,128)(2,1)S(1)} %pack.1.own_ref), channel_id=1, source_target_pairs={{0,48},{2,50},{4,52},{6,54},{8,56},{10,58},{12,60},{14,62},{16,0},... | collective-permute-start | bytes 135176 | tf_op jit(solution)/shard_map/ppermute | solution.py:364
  9.8 6.9 %collective-permute-start.1 = (bf16[176,128]{1,0:T(8,128)(2,1)S(1)}, bf16[176,128]{1,0:T(8,128)(2,1)S(1)}, u32[]{:S(2)}, u32[]{:S(2)}) collective-permute-start(bf16[176,128]{1,0:T(8,128)(2,1)S(1)} %pack.1.own_ref), channel_id=1, source_target_pairs={{0,32},{2,34},{4,36},{6,38},{8,40},{10,42},{12,44},{14,46},{16,48}... | collective-permute-start | bytes 135176 | tf_op jit(solution)/shard_map/ppermute | solution.py:364
  10.8 6.0 %collective-permute-start = (bf16[176,128]{1,0:T(8,128)(2,1)S(1)}, bf16[176,128]{1,0:T(8,128)(2,1)S(1)}, u32[]{:S(2)}, u32[]{:S(2)}) collective-permute-start(bf16[176,128]{1,0:T(8,128)(2,1)S(1)} %pack.1.own_ref), channel_id=1, source_target_pairs={{0,16},{2,18},{4,20},{6,22},{8,24},{10,26},{12,28},{14,30},{16,32}... | collective-permute-start | bytes 135176 | tf_op jit(solution)/shard_map/ppermute | solution.py:364
  13.1 0.7 copy-start.11
  13.7 0.7 copy-start.12
  25.0 1.3 %copy-start.6 = (bf16[32,4,64,128]{3,2,1,0:T(8,128)(2,1)}, bf16[32,4,64,128]{3,2,1,0:T(8,128)(2,1)S(1)}, u32[]{:S(2)}) copy-start(bf16[32,4,64,128]{3,2,1,0:T(8,128)(2,1)S(1)} %front.1) | copy-start | bytes 6291460
  26.3 7.7 %copy-start.15 = (f32[2]{0:T(128)S(1)}, f32[2]{0:T(128)}, u32[]{:S(2)}) copy-start(f32[2]{0:T(128)} %param.19) | copy-start | bytes 28
  26.3 8.3 %copy-start.10 = (f32[1,512,512]{2,1,0:T(8,128)S(1)}, f32[1,512,512]{2,1,0:T(8,128)}, u32[]{:S(2)}) copy-start(f32[1,512,512]{2,1,0:T(8,128)} %screen_ref.1) | copy-start | bytes 3145732
  26.3 8.3 %copy-start.13 = (s32[16]{0:T(128)S(1)}, s32[16]{0:T(128)}, u32[]{:S(2)}) copy-start(s32[16]{0:T(128)} %rows_ref.3) | copy-start | bytes 196
  26.3 8.3 %copy-start.14 = (s32[8]{0:T(128)S(1)}, s32[8]{0:T(128)}, u32[]{:S(2)}) copy-start(s32[8]{0:T(128)} %cols_ref.3) | copy-start | bytes 100
  26.3 32.9 %all-to-all-start = ((bf16[32,4,64,128]{3,2,1,0:T(8,128)(2,1)}), bf16[32,4,64,128]{3,2,1,0:T(8,128)(2,1)S(1)}, u32[]{:S(2)}, u32[]{:S(2)}) async-start(bf16[32,4,64,128]{3,2,1,0:T(8,128)(2,1)} %copy-done.6), calls=%async_computation | async-start | bytes 4194304 | tf_op jit(solution)/shard_map/all_to_all | solution.py:367
  38.9 1.3 %copy-start = (bf16[512,2048]{1,0:T(8,128)(2,1)}, bf16[512,2048]{1,0:T(8,128)(2,1)S(1)}, u32[]{:S(2)}) copy-start(bf16[512,2048]{1,0:T(8,128)(2,1)S(1)} %get-tuple-element.12.row_ref) | copy-start | bytes 6291460
  40.2 1.3 %copy-start.2 = (bf16[1024,1024]{1,0:T(8,128)(2,1)}, bf16[1024,1024]{1,0:T(8,128)(2,1)S(1)}, u32[]{:S(2)}) copy-start(bf16[1024,1024]{1,0:T(8,128)(2,1)S(1)} %get-tuple-element.13.col_ref) | copy-start | bytes 6291460
  41.5 1.4 %copy-start.4 = (f32[2,512,512]{2,1,0:T(8,128)}, f32[2,512,512]{2,1,0:T(8,128)S(1)}, u32[]{:S(2)}) copy-start(f32[2,512,512]{2,1,0:T(8,128)S(1)} %get-tuple-element.14.screen_ref) | copy-start | bytes 6291460
  59.2 1.6 %copy-start.1 = (bf16[512,2048]{1,0:T(8,128)(2,1)S(1)}, bf16[512,2048]{1,0:T(8,128)(2,1)}, u32[]{:S(2)}) copy-start(bf16[512,2048]{1,0:T(8,128)(2,1)} %copy-done) | copy-start | bytes 6291460
  60.8 1.6 %copy-start.3 = (bf16[1024,1024]{1,0:T(8,128)(2,1)S(1)}, bf16[1024,1024]{1,0:T(8,128)(2,1)}, u32[]{:S(2)}) copy-start(bf16[1024,1024]{1,0:T(8,128)(2,1)} %copy-done.2) | copy-start | bytes 6291460
  62.4 1.6 %copy-start.5 = (f32[2,512,512]{2,1,0:T(8,128)S(1)}, f32[2,512,512]{2,1,0:T(8,128)}, u32[]{:S(2)}) copy-start(f32[2,512,512]{2,1,0:T(8,128)} %copy-done.4) | copy-start | bytes 6291460
  65.8 5.5 %collective-permute-start.3 = (bf16[2,256,512]{2,1,0:T(8,128)(2,1)S(1)}, bf16[2,256,512]{2,1,0:T(8,128)(2,1)S(1)}, u32[]{:S(2)}, u32[]{:S(2)}) collective-permute-start(bf16[2,256,512]{2,1,0:T(8,128)(2,1)S(1)} %back_other.1), channel_id=1, source_target_pairs={{0,1},{1,0},{2,3},{3,2},{4,5},{5,4},{6,7},{7,6},{8,9},{9,8},{10,11... | collective-permute-start | bytes 1572872 | tf_op jit(solution)/shard_map/ppermute | solution.py:376

commit v2 on v1

v2 whole, which is shorter than its diff:
```python
import math

import jax
import jax.numpy as jnp
from jax import lax
from jax.experimental import pallas as pl
from jax.experimental.pallas import tpu as pltpu
from jax.sharding import PartitionSpec as P

SUB = 512
CON = 64
FAC = 512
VB = 128
F32 = jnp.float32
BF16 = jnp.bfloat16
NORM = 1.0 / math.sqrt(512.0)
NN = (((1,), (0,)), ((), ()))
NT = (((1,), (1,)), ((), ()))
LIMIT = 64 << 20


def dot(first, second, numbers=NN):
    return lax.dot_general(first, second, numbers, preferred_element_type=F32)


def iota(shape, axis):
    return lax.broadcasted_iota(jnp.int32, shape, axis)


def sincos_small(theta):
    square = theta * theta
    cosine = 1.0 + square * (-0.5 + square * (1.0 / 24 + square * (-1.0 / 720 + square * (1.0 / 40320))))
    sine = theta * (1.0 + square * (-1.0 / 6 + square * (1.0 / 120 + square * (-1.0 / 5040 + square * (1.0 / 362880)))))
    return cosine, sine


def rotate_quarter(cosine, sine, quarter):
    odd = (quarter & 1) == 1
    real = jnp.where(odd, sine, cosine)
    imag = jnp.where(odd, cosine, sine)
    real = jnp.where(((quarter + 1) & 2) == 2, -real, real)
    imag = jnp.where((quarter & 2) == 2, -imag, imag)
    return real, imag


def unit_roots(steps):
    quarter = (steps + 64) >> 7
    rest = steps - (quarter << 7)
    cosine, sine = sincos_small(rest.astype(F32) * (2.0 * math.pi / 512))
    return rotate_quarter(cosine, sine, quarter)


def times(first, second):
    return (
        first[0] * second[0] - first[1] * second[1],
        first[0] * second[1] + first[1] * second[0],
    )


def cell_roots():
    low = unit_roots(iota((8, 512), 0) * iota((8, 512), 1) & 511)
    high = unit_roots(iota((8, 512), 0) * 8 * iota((8, 512), 1) & 511)
    real, imag = [], []
    for index in range(8):
        row = slice(index, index + 1)
        product = times((high[0][row], high[1][row]), low)
        real.append(product[0])
        imag.append(product[1])
    return jnp.concatenate(real, axis=0), jnp.concatenate(imag, axis=0)


def offset_roots(offsets_ref, count):
    rows = iota((count, 512), 0)
    start = jnp.zeros((count, 512), jnp.int32)
    for index in range(count):
        start = jnp.where(rows == index, offsets_ref[index], start)
    steps = start * iota((count, 512), 1)
    real, imag = unit_roots(steps & 511)
    return real * NORM, imag * NORM


def lane_steps(offsets_ref, count, width):
    shape = (8, count * width)
    lane = iota(shape, 1)
    owner = lane // width
    start = jnp.zeros(shape, jnp.int32)
    for index in range(count):
        start = jnp.where(owner == index, offsets_ref[index], start)
    return start + (lane & 63), lane


def lane_roots(frequency, lead):
    row = iota(frequency.shape, 0)
    high = unit_roots((frequency * row * 64) & 511)
    middle = unit_roots((frequency * row * 8) & 511)
    low = unit_roots((frequency * row + lead) & 511)
    low = (low[0] * NORM, low[1] * NORM)
    return high, middle, low


def row_pick(pair, index):
    return pair[0][index : index + 1], pair[1][index : index + 1]


def fetch(sources, targets, sems):
    copies = [
        pltpu.make_async_copy(source, target, sems.at[index])
        for index, (source, target) in enumerate(zip(sources, targets))
    ]
    for copy in copies:
        copy.start()
    return copies


def pack_kernel(counts_hbm, vis_hbm, kernels_hbm, offsets_hbm, out_ref, counts, vis, kernels, all_offsets, sems):
    copies = fetch((counts_hbm, vis_hbm, kernels_hbm, offsets_hbm), (counts, vis, kernels, all_offsets), sems)
    for copy in copies:
        copy.wait()
    live = counts[0, 0]
    slot = iota((8, 128), 0)
    samples = [jnp.where(slot < live, vis[part].astype(F32), 0.0) for part in range(2)]
    out_ref[0:16, :] = jnp.concatenate(samples, axis=0).astype(BF16)
    for axis in range(2):
        offsets = all_offsets[axis]
        low = offsets & 7
        digits = jnp.concatenate([(offsets >> 3).astype(F32), low.astype(F32)], axis=0)
        out_ref[16 + axis * 16 : 32 + axis * 16, :] = digits.astype(BF16)
        turned = []
        for block in range(8):
            shift = (slot - low[block : block + 1, :]) & 7
            values = jnp.zeros((8, VB), F32)
            for column in range(8):
                entry = kernels[axis, column, block : block + 1, :].astype(F32)
                values = jnp.where(shift == column, entry, values)
            turned.append(values)
        out_ref[48 + axis * 64 : 112 + axis * 64, :] = jnp.concatenate(turned, axis=0).astype(BF16)


def pack(counts, vis, kernels, offsets):
    return pl.pallas_call(
        pack_kernel,
        out_shape=jax.ShapeDtypeStruct((176, 128), BF16),
        in_specs=[hbm()] * 4,
        out_specs=vmem(),
        scratch_shapes=[
            pltpu.SMEM((1, 1), jnp.int32),
            pltpu.VMEM((2, 8, VB), BF16),
            pltpu.VMEM((2, 8, 8, VB), BF16),
            pltpu.VMEM((2, 8, VB), jnp.int32),
            pltpu.SemaphoreType.DMA((4,)),
        ],
        compiler_params=pltpu.CompilerParams(vmem_limit_bytes=LIMIT),
        name="pack",
    )(counts, vis, kernels, offsets)


def lane_table(offsets_ref, count, width, lead, out_ref, place):
    frequency, lane = lane_steps(offsets_ref, count, width)
    high, middle, low = lane_roots(frequency, jnp.where((lane & lead) == 0, 0, 128))
    for index in range(8):
        outer = row_pick(high, index)
        for inner in range(0, 8, 2):
            first = times(times(outer, row_pick(middle, inner)), low)
            second = times(times(outer, row_pick(middle, inner + 1)), low)
            base = index * 64 + inner * 8
            for part in range(2):
                place(out_ref, part, base, jnp.concatenate([first[part], second[part]], axis=0).astype(BF16))


def grid_slot(samples, digits, kernels, row_table, col_table, spreads, turned, halves, sent, arrive=None):
    slot = iota((8, 128), 0)
    tile = iota((64, 8, 128), 0)
    for axis in range(2):
        for block in range(8):
            home = digits[axis][block : block + 1, :] + (digits[axis][block + 8 : block + 9, :] > slot).astype(jnp.int32)
            values = kernels[axis][block * 8 : block * 8 + 8, :]
            spreads[axis, :, block * VB : (block + 1) * VB] = (
                jnp.where(tile == home[None], values[None], 0.0).reshape(512, VB).astype(BF16)
            )
    if arrive is not None:
        arrive()
    for quarter in range(4):
        lanes = slice(quarter * 256, (quarter + 1) * 256)
        rows = dot(row_table[...], spreads[0, :, lanes])
        real_part, imag_part = (
            jnp.concatenate([samples[8 * half + 2 * quarter + part : 8 * half + 2 * quarter + part + 1] for part in range(2)], axis=1)
            for half in range(2)
        )
        real, imag = times((rows[:256], rows[256:]), (real_part, imag_part))
        turned[:256, lanes] = real.astype(BF16)
        turned[256:, lanes] = imag.astype(BF16)
    half = dot(turned[...], spreads[1], NT).astype(BF16)
    halves[:, :512] = half[:256]
    halves[:, 512:] = half[256:]
    result = dot(halves[...], col_table[...]).astype(BF16)
    for row in range(4):
        for column in range(8):
            sent[row * 8 + column] = result[row * 64 : (row + 1) * 64, column * 128 : (column + 1) * 128]


def unpacked(ref):
    return (
        ref[0:16, :].astype(F32),
        [ref[16 + axis * 16 : 32 + axis * 16, :].astype(jnp.int32) for axis in range(2)],
        [ref[48 + axis * 64 : 112 + axis * 64, :].astype(F32) for axis in range(2)],
    )


def front_scratch(slots):
    return [
        pltpu.VMEM((2, 512, 1024), BF16),
        pltpu.VMEM((512, 1024), BF16),
        pltpu.VMEM((256, 1024), BF16),
        pltpu.VMEM((slots, 32, 64, 128), BF16),
        pltpu.SemaphoreType.DMA((slots,)),
    ]


def table_scratch():
    return [pltpu.VMEM((512, 512), BF16), pltpu.VMEM((1024, 1024), BF16), pltpu.SemaphoreType.DMA((2,))]


def front_own_kernel(
    group_ref, rows_ref, cols_ref, own_ref, row_hbm, col_hbm, out_hbm,
    spreads, turned, halves, sent, sems, row_out, col_out, table_sems,
):
    def below(ref, part, base, value):
        ref[part * 512 + base : part * 512 + base + 16, :] = value

    lane_table(cols_ref, 8, 128, 64, col_out, below)
    base = cell_roots()
    small = offset_roots([rows_ref[4 * index + group_ref[0]] for index in range(4)], 4)
    for index in range(4):
        real, imag = times(row_pick(small, index), base)
        row_out[index * 64 : index * 64 + 64, :] = real.astype(BF16)
        row_out[256 + index * 64 : 320 + index * 64, :] = (-imag).astype(BF16)
    copies = fetch((row_out, col_out), (row_hbm, col_hbm), table_sems)
    grid_slot(*unpacked(own_ref), row_out, col_out, spreads, turned, halves, sent.at[0])
    copy = pltpu.make_async_copy(sent.at[0], out_hbm.at[:, group_ref[0] & 3], sems.at[0])
    copy.start()
    for copy in copies + [copy]:
        copy.wait()


def front_own(group, facet_rows, facet_cols, own):
    return pl.pallas_call(
        front_own_kernel,
        out_shape=[
            jax.ShapeDtypeStruct((512, 512), BF16),
            jax.ShapeDtypeStruct((1024, 1024), BF16),
            jax.ShapeDtypeStruct((32, 4, 64, 128), BF16),
        ],
        in_specs=[smem(), smem(), smem(), vmem()],
        out_specs=[hbm()] * 3,
        scratch_shapes=front_scratch(1) + table_scratch(),
        compiler_params=pltpu.CompilerParams(vmem_limit_bytes=LIMIT),
        cost_estimate=pl.CostEstimate(flops=3 * 10**9, bytes_accessed=4 << 20, transcendentals=0),
        name="front_own",
    )(group, facet_rows, facet_cols, own)


def front_others_kernel(
    group_ref, first_ref, second_ref, third_ref, row_hbm, col_hbm, begun_hbm, out_hbm,
    spreads, turned, halves, sent, sems, row_table, col_table, table_sems,
):
    tables = fetch((row_hbm, col_hbm), (row_table, col_table), table_sems)

    def arrive():
        for copy in tables:
            copy.wait()

    copies = []
    for index, ref in enumerate((first_ref, second_ref, third_ref)):
        grid_slot(
            *unpacked(ref), row_table, col_table, spreads, turned, halves, sent.at[index],
            arrive if index == 0 else None,
        )
        source = (group_ref[0] + 3 - index) & 3
        copy = pltpu.make_async_copy(sent.at[index], out_hbm.at[:, source], sems.at[index])
        copy.start()
        copies.append(copy)
    for copy in copies:
        copy.wait()


def front_others(group, packs, row_table, col_table, begun):
    return pl.pallas_call(
        front_others_kernel,
        out_shape=jax.ShapeDtypeStruct((32, 4, 64, 128), BF16),
        in_specs=[smem()] + [vmem()] * 3 + [hbm()] * 3,
        out_specs=hbm(),
        scratch_shapes=front_scratch(3) + table_scratch(),
        input_output_aliases={6: 0},
        compiler_params=pltpu.CompilerParams(vmem_limit_bytes=LIMIT),
        cost_estimate=pl.CostEstimate(flops=6 * 10**9, bytes_accessed=4 << 20, transcendentals=0),
        name="front_others",
    )(group, *packs, row_table, col_table, begun)


def smem():
    return pl.BlockSpec(memory_space=pltpu.SMEM)


def vmem():
    return pl.BlockSpec(memory_space=pltpu.VMEM)


def hbm():
    return pl.BlockSpec(memory_space=pltpu.HBM)


def tables_kernel(
    layer_ref, rows_ref, cols_ref, weights_ref, screen_hbm, row_hbm, col_hbm, screen_out_hbm,
    screen, row_out, col_out, screen_out, sems,
):
    layer = layer_ref[0]
    (arrival,) = fetch((screen_hbm.at[0, pl.ds(layer * 256, 256)],), (screen,), sems.at[pl.ds(3, 1)])

    def beside(ref, part, base, value):
        ref[base : base + 16, part * 1024 : (part + 1) * 1024] = value

    lane_table(rows_ref, 16, 64, 0, row_out, beside)
    small = offset_roots(cols_ref, 8)
    base = cell_roots()
    for column in range(8):
        real, imag = times(row_pick(small, column), base)
        real, imag = real.astype(BF16), imag.astype(BF16)
        rows = slice(column * 128, column * 128 + 64)
        col_out[rows, :512] = real
        col_out[rows, 512:] = imag
        rows = slice(column * 128 + 64, column * 128 + 128)
        col_out[rows, :512] = -imag
        col_out[rows, 512:] = real
    arrival.wait()
    for side in range(2):
        weight = weights_ref[layer if side == 0 else 1 - layer] * 4.0
        for chunk in range(4):
            rows = slice(chunk * 64, (chunk + 1) * 64)
            turns = screen[rows, :] * weight
            whole = jnp.floor(turns + 0.5)
            cosine, sine = sincos_small((turns - whole) * (0.5 * math.pi))
            real, imag = rotate_quarter(cosine, sine, whole.astype(jnp.int32))
            screen_out[side, 0, rows, :] = real
            screen_out[side, 1, rows, :] = imag
    for copy in fetch((row_out, col_out, screen_out), (row_hbm, col_hbm, screen_out_hbm), sems):
        copy.wait()


def tables(layer, sub_rows, sub_cols, weights, screen):
    return pl.pallas_call(
        tables_kernel,
        out_shape=[
            jax.ShapeDtypeStruct((512, 2048), BF16),
            jax.ShapeDtypeStruct((1024, 1024), BF16),
            jax.ShapeDtypeStruct((2, 2, 256, 512), F32),
        ],
        in_specs=[smem(), smem(), smem(), smem(), hbm()],
        out_specs=[hbm()] * 3,
        scratch_shapes=[
            pltpu.VMEM((256, 512), F32),
            pltpu.VMEM((512, 2048), BF16),
            pltpu.VMEM((1024, 1024), BF16),
            pltpu.VMEM((2, 2, 256, 512), F32),
            pltpu.SemaphoreType.DMA((4,)),
        ],
        compiler_params=pltpu.CompilerParams(vmem_limit_bytes=LIMIT),
        cost_estimate=pl.CostEstimate(flops=10**9, bytes_accessed=16 << 20, transcendentals=0),
        name="tables",
    )(layer, sub_rows, sub_cols, weights, screen)


def block_copies(blocks_hbm, blocks, sems):
    return fetch(
        [blocks_hbm.at[:, 2 * pair : 2 * pair + 2] for pair in range(4)],
        [blocks.at[:, 2 * pair : 2 * pair + 2] for pair in range(4)],
        sems,
    )


def middle_rows(blocks, copies, row_table, store):
    sign = jnp.where((iota((1, 128), 1) & 64) == 0, -1.0, 1.0)
    for pair in range(4):
        copies[pair].wait()
        placed = jnp.concatenate(
            [blocks[:, 2 * pair + part].reshape(1024, 128) for part in range(2)], axis=1
        )
        straight = dot(row_table[:, :1024], placed)
        crossed = dot(row_table[:, 1024:], placed)
        for part in range(2):
            lanes = slice(part * 128, part * 128 + 128)
            value = straight[:, lanes] + pltpu.roll(crossed[:, lanes], 64, 1) * sign
            store(slice(pair * 256 + part * 128, pair * 256 + part * 128 + 128), value.astype(BF16))


def screened(middle, col_table, screen):
    facet = dot(middle, col_table)
    return times((facet[:, :512], facet[:, 512:]), (screen[0], screen[1]))


def back_other_kernel(half_ref, blocks_hbm, row_hbm, out_ref, row_table, blocks, sems, block_sems):
    (copy,) = fetch((row_hbm.at[pl.ds(half_ref[0] * 256, 256)],), (row_table,), sems)
    arriving = block_copies(blocks_hbm, blocks, block_sems)
    copy.wait()

    def store(lanes, value):
        out_ref[:, lanes] = value

    middle_rows(blocks, arriving, row_table, store)


def back_other(half, blocks, row_table):
    return pl.pallas_call(
        back_other_kernel,
        out_shape=jax.ShapeDtypeStruct((256, 1024), BF16),
        in_specs=[smem(), hbm(), hbm()],
        out_specs=vmem(),
        scratch_shapes=[
            pltpu.VMEM((256, 2048), BF16),
            pltpu.VMEM((4, 8, 4, CON, 128), BF16),
            pltpu.SemaphoreType.DMA((1,)),
            pltpu.SemaphoreType.DMA((4,)),
        ],
        compiler_params=pltpu.CompilerParams(vmem_limit_bytes=LIMIT),
        cost_estimate=pl.CostEstimate(flops=10**9, bytes_accessed=4 << 20, transcendentals=0),
        name="back_other",
    )(half, blocks, row_table)


def back_own_kernel(
    half_ref, blocks_hbm, row_hbm, col_hbm, screen_hbm, out_ref,
    row_table, blocks, col_table, screen, middle, sems, block_sems,
):
    (first,) = fetch((row_hbm.at[pl.ds(half_ref[0] * 256, 256)],), (row_table,), sems)
    arriving = block_copies(blocks_hbm, blocks, block_sems)
    copies = fetch((col_hbm, screen_hbm.at[0]), (col_table, screen), sems.at[pl.ds(1, 2)])
    first.wait()

    def store(lanes, value):
        middle[:, lanes] = value

    middle_rows(blocks, arriving, row_table, store)
    for copy in copies:
        copy.wait()
    real, imag = screened(middle[...], col_table[...], screen)
    out_ref[0] = real
    out_ref[1] = imag


def back_own(half, blocks, row_table, col_table, screen):
    return pl.pallas_call(
        back_own_kernel,
        out_shape=jax.ShapeDtypeStruct((2, 256, 512), F32),
        in_specs=[smem()] + [hbm()] * 4,
        out_specs=vmem(),
        scratch_shapes=[
            pltpu.VMEM((256, 2048), BF16),
            pltpu.VMEM((4, 8, 4, CON, 128), BF16),
            pltpu.VMEM((1024, 1024), BF16),
            pltpu.VMEM((2, 256, 512), F32),
            pltpu.VMEM((256, 1024), BF16),
            pltpu.SemaphoreType.DMA((3,)),
            pltpu.SemaphoreType.DMA((4,)),
        ],
        compiler_params=pltpu.CompilerParams(vmem_limit_bytes=LIMIT),
        cost_estimate=pl.CostEstimate(flops=2 * 10**9, bytes_accessed=8 << 20, transcendentals=0),
        name="back_own",
    )(half, blocks, row_table, col_table, screen)


def finish_kernel(middle_ref, own_ref, col_hbm, screen_hbm, out_hbm, col_table, screen, image, sems):
    copies = fetch((col_hbm, screen_hbm.at[1]), (col_table, screen), sems)
    copies[0].wait()
    copies[1].wait()
    leaving = []
    for chunk in range(2):
        rows = slice(chunk * 128, chunk * 128 + 128)
        value = screened(middle_ref[rows, :], col_table[...], (screen[0, rows, :], screen[1, rows, :]))
        for part in range(2):
            image[chunk, part] = own_ref[part, rows, :] + value[part]
        copy = pltpu.make_async_copy(image.at[chunk], out_hbm.at[:, pl.ds(chunk * 128, 128)], sems.at[2 + chunk])
        copy.start()
        leaving.append(copy)
    for copy in leaving:
        copy.wait()


def finish(middle, own, col_table, screen):
    return pl.pallas_call(
        finish_kernel,
        out_shape=jax.ShapeDtypeStruct((2, 256, 512), F32),
        in_specs=[vmem(), vmem(), hbm(), hbm()],
        out_specs=hbm(),
        scratch_shapes=[
            pltpu.VMEM((1024, 1024), BF16),
            pltpu.VMEM((2, 256, 512), F32),
            pltpu.VMEM((2, 2, 128, 512), F32),
            pltpu.SemaphoreType.DMA((4,)),
        ],
        compiler_params=pltpu.CompilerParams(vmem_limit_bytes=LIMIT),
        cost_estimate=pl.CostEstimate(flops=10**9, bytes_accessed=8 << 20, transcendentals=0),
        name="finish",
    )(middle, own, col_table, screen)


def position(x, z, y):
    return x * 32 + (z % 8) * 4 + y


GROUPS = [
    [position(x, 2 * k + l, y) for x in range(4) for l in range(2) for y in range(4)] for k in range(4)
]


def shifted(turn):
    return [
        (position(x, z, y), position(x, z + 2 * turn, y)) for x in range(4) for z in range(8) for y in range(4)
    ]


def per_device(
    visibilities, kernels, vis_offsets, block_counts,
    sub_rows, sub_cols, facet_rows, facet_cols, screen_n, layer_w,
):
    place = lax.axis_index("sf")
    group = ((place >> 3) & 3).reshape(1)
    own = pack(
        block_counts,
        visibilities.reshape(2, 8, VB), kernels.reshape(2, 8, 8, VB), vis_offsets.reshape(2, 8, VB),
    )
    packs = [lax.ppermute(own, "sf", shifted(turn)) for turn in (1, 2, 3)]
    facet_row_table, facet_col_table, begun = front_own(group, facet_rows, facet_cols, own)
    outgoing = front_others(group, packs, facet_row_table, facet_col_table, begun)
    incoming = lax.all_to_all(
        outgoing, "sf", split_axis=0, concat_axis=0, tiled=True, axis_index_groups=GROUPS
    )
    layer = lax.axis_index("wa").reshape(1)
    row_table, col_table, screen = tables(layer, sub_rows, sub_cols, layer_w, screen_n)
    blocks = incoming.reshape(4, 8, 4, CON, 128)
    theirs = back_other(1 - layer, blocks, row_table)
    received = lax.ppermute(theirs, "wa", [(0, 1), (1, 0)])
    own_part = back_own(layer, blocks, row_table, col_table, screen)
    return finish(received, own_part, col_table, screen)[:, None]


def solution(mesh):
    in_specs = (
        P(None, "sf", "wa", None, None),
        P(None, None, "sf", "wa", None, None),
        P(None, "sf", "wa", None, None),
        P("sf", "wa"),
        P(),
        P(),
        P(),
        P(),
        P("sf", None, None),
        P(),
    )
    out_specs = P(None, "sf", "wa", None)
    return jax.shard_map(
        per_device, mesh=mesh, in_specs=in_specs, out_specs=out_specs, check_vma=False
    )
```

time: 73 us -> 80.3 us (1.100)
  Pallas kernels: 18.2 us -> 35.7 us
  local copies, waits for them, and re-layouts: 14.2 us -> 0 us
  waiting for transfers between devices: 16.7 us -> 22.1 us
  other arithmetic: 1.16 us -> 0 us
    pallas_call x4 -> x5, Pallas kernels: 13.9 us -> 29.1 us  [the longest x1 9.17 us: front_others(): pl.pallas_call(front_others_kernel, out_shape=jax.ShapeDtypeStruct((32, 4...]
    unnamed x32 -> x0, local copies, waits for them, and re-layouts: 13.6 us -> none
    all_to_all x1, waiting for transfers between devices: 16.3 us -> 22.1 us  [per_device(): lax.all_to_all(outgoing, 'sf', split_axis=0, concat_axis=0, tiled=True, a...]
    pallas_call x1, Pallas kernels: 0.07 us -> 1.5 us  [pack(): pl.pallas_call(pack_kernel, out_shape=jax.ShapeDtypeStruct((176, 128), BF...]
    broadcast_in_dim x1 -> x0, other arithmetic: 1.16 us -> none  [per_device(): return (own + received.astype(F32))[:, None]]
    pallas_call x1, Pallas kernels: 4.22 us -> 5.12 us  [tables(): pl.pallas_call(tables_kernel, out_shape=[jax.ShapeDtypeStruct((512, 2048)...]
  transfers between devices with their start and end apart: 5 -> 5, of which waited for: 2 -> 1; matrix products, arithmetic and copies ran while one was open for 1% -> 0% of each run, Pallas kernels for 11% -> 19%
where the time goes in v2:
time: 80.3 us; the launch traced here: 79.9 us
  Pallas kernels  35.7 us (44%)
  waiting for transfers between devices  22.1 us (28%)
  starting transfers between devices  21.1 us (26%)
  between operations  0.91 us (1%)
    all_to_all x1, waiting for transfers between devices, per_device(): lax.all_to_all(outgoing, 'sf', split_axis=0, concat_axis=0, tiled=True, a...  22.1 us
    ppermute x3, starting transfers between devices, per_device(): packs = [lax.ppermute(own, 'sf', shifted(turn)) for turn in (1, 2, 3)]  10.2 us
    pallas_call x1, Pallas kernels, front_others(): pl.pallas_call(front_others_kernel, out_shape=jax.ShapeDtypeStruct((32, 4...  9.17 us
    all_to_all x1, starting transfers between devices, per_device(): lax.all_to_all(outgoing, 'sf', split_axis=0, concat_axis=0, tiled=True, a...  7.82 us
    pallas_call x1, Pallas kernels, back_own(): pl.pallas_call(back_own_kernel, out_shape=jax.ShapeDtypeStruct((2, 256, 5...  5.25 us
    pallas_call x1, Pallas kernels, front_own(): pl.pallas_call(front_own_kernel, out_shape=[jax.ShapeDtypeStruct((512, 51...  5.17 us
    pallas_call x1, Pallas kernels, tables(): pl.pallas_call(tables_kernel, out_shape=[jax.ShapeDtypeStruct((512, 2048)...  5.12 us
    pallas_call x1, Pallas kernels, finish(): pl.pallas_call(finish_kernel, out_shape=jax.ShapeDtypeStruct((2, 256, 512...  4.94 us
  transfers between devices with their start and end apart: 5, of which 1 were waited for; matrix products, arithmetic and copies ran while one was open for 0% of the time, Pallas kernels for 19%

profile of v2, /device:TPU:1, one launch (start us, length us, event | category | flops | bytes accessed | tf_op | source)
XLA Modules:
  0.0 79.9 jit_solution(14019207243293575370)
XLA Ops:
  0.7 1.5 %pack.1.own_ref = bf16[176,128]{1,0:T(8,128)(2,1)} custom-call(s32[1,1]{1,0:T(1,128)S(6)} %copy.14.counts_hbm, bf16[2,8,128]{2,1,0:T(8,128)(2,1)} %bitcast.11, bf16[2,8,8,128]{3,2,1,0:T(8,128)(2,1)} %bitcast.9, s32[2,8,128]{2,1,0:T(8,128)} %bitcast.10), custom_call_target="tpu_custom_call" | custom-call | tf_op jit(solution)/shard_map/pack/pallas_call | solution.py:140
  2.2 6.9 %collective-permute-start.2 = (bf16[176,128]{1,0:T(8,128)(2,1)}, bf16[176,128]{1,0:T(8,128)(2,1)}, u32[]{:S(2)}, u32[]{:S(2)}) collective-permute-start(bf16[176,128]{1,0:T(8,128)(2,1)} %pack.1.own_ref), channel_id=1, source_target_pairs={{0,48},{2,50},{4,52},{6,54},{8,56},{10,58},{12,60},{14,62},{16,0},... | collective-permute-start | bytes 135176 | tf_op jit(solution)/shard_map/ppermute | solution.py:530
  9.1 1.0 %collective-permute-start.1 = (bf16[176,128]{1,0:T(8,128)(2,1)}, bf16[176,128]{1,0:T(8,128)(2,1)}, u32[]{:S(2)}, u32[]{:S(2)}) collective-permute-start(bf16[176,128]{1,0:T(8,128)(2,1)} %pack.1.own_ref), channel_id=1, source_target_pairs={{0,32},{2,34},{4,36},{6,38},{8,40},{10,42},{12,44},{14,46},{16,48}... | collective-permute-start | bytes 135176 | tf_op jit(solution)/shard_map/ppermute | solution.py:530
  10.1 2.3 %collective-permute-start = (bf16[176,128]{1,0:T(8,128)(2,1)}, bf16[176,128]{1,0:T(8,128)(2,1)}, u32[]{:S(2)}, u32[]{:S(2)}) collective-permute-start(bf16[176,128]{1,0:T(8,128)(2,1)} %pack.1.own_ref), channel_id=1, source_target_pairs={{0,16},{2,18},{4,20},{6,22},{8,24},{10,26},{12,28},{14,30},{16,32}... | collective-permute-start | bytes 135176 | tf_op jit(solution)/shard_map/ppermute | solution.py:530
  12.3 5.2 %front_own.1 = (bf16[512,512]{1,0:T(8,128)(2,1)}, bf16[1024,1024]{1,0:T(8,128)(2,1)}, bf16[32,4,64,128]{3,2,1,0:T(8,128)(2,1)}) custom-call(s32[1]{0:T(128)} %bitcast.1.group_ref, s32[16]{0:T(128)} %rows_ref.2, s32[8]{0:T(128)} %cols_ref.2, bf16[176,128]{1,0:T(8,128)(2,1)} %pack.1.own_ref), custom_call_target="tpu_custom_call" | custom-call | flops 3000000000 | bytes 4194304 | tf_op jit(solution)/shard_map/front_own/pallas_call | solution.py:246
  17.5 0.0 collective-permute-done.2.third_ref
  17.5 0.0 collective-permute-done.1.second_ref
  17.5 0.0 collective-permute-done.first_ref
  17.5 9.2 %front_others.1 = bf16[32,4,64,128]{3,2,1,0:T(8,128)(2,1)} custom-call(s32[1]{0:T(128)} %bitcast.1.group_ref, bf16[176,128]{1,0:T(8,128)(2,1)} %collective-permute-done.first_ref, bf16[176,128]{1,0:T(8,128)(2,1)} %collective-permute-done.1.second_ref, bf16[176,128]{1,0:T(8,128)(2,1)} %collective-permute-done.2.third_ref, ...), custom_call_target="tpu_custom_call", output_to_operand_aliasing={{}: (6, {})} | custom-call | flops 6000000000 | bytes 4194304 | tf_op jit(solution)/shard_map/front_others/pallas_call | solution.py:287
  26.7 7.8 %all-to-all-start = ((bf16[32,4,64,128]{3,2,1,0:T(8,128)(2,1)}), bf16[32,4,64,128]{3,2,1,0:T(8,128)(2,1)}, u32[]{:S(2)}, u32[]{:S(2)}) async-start(bf16[32,4,64,128]{3,2,1,0:T(8,128)(2,1)} %front_others.1), calls=%async_computation | async-start | bytes 4194304 | tf_op jit(solution)/shard_map/all_to_all | solution.py:533
  34.6 5.1 %tables.1 = (bf16[512,2048]{1,0:T(8,128)(2,1)}, bf16[1024,1024]{1,0:T(8,128)(2,1)}, f32[2,2,256,512]{3,2,1,0:T(8,128)}) custom-call(s32[1]{0:T(128)} %bitcast.layer_ref.half_ref, s32[16]{0:T(128)} %rows_ref.3, s32[8]{0:T(128)} %cols_ref.3, f32[2]{0:T(128)} %weights_ref.1, f32[1,512,512]{2,1,0:T(8,128)} %screen_hbm.1), custom_call_target="tpu_custom_call" | custom-call | flops 1000000000 | bytes 16777216 | tf_op jit(solution)/shard_map/tables/pallas_call | solution.py:350
  39.7 22.1 %all-to-all-done = bf16[32,4,64,128]{3,2,1,0:T(8,128)(2,1)} async-done(((bf16[32,4,64,128]{3,2,1,0:T(8,128)(2,1)}), bf16[32,4,64,128]{3,2,1,0:T(8,128)(2,1)}, u32[]{:S(2)}, u32[]{:S(2)}) %all-to-all-start) | async-done | bytes 2097184 | tf_op jit(solution)/shard_map/all_to_all | solution.py:533
  61.8 4.6 %back_other.1 = bf16[256,1024]{1,0:T(8,128)(2,1)} custom-call(s32[1]{0:T(128)S(6)} %sub.3.half_ref, bf16[4,8,4,64,128]{4,3,2,1,0:T(8,128)(2,1)} %bitcast.5.blocks_hbm, bf16[512,2048]{1,0:T(8,128)(2,1)} %get-tuple-element.14.row_hbm), custom_call_target="tpu_custom_call" | custom-call | flops 1000000000 | bytes 4194304 | tf_op jit(solution)/shard_map/back_other/pallas_call | solution.py:412
  66.4 3.1 %collective-permute-start.3 = (bf16[256,1024]{1,0:T(8,128)(2,1)}, bf16[256,1024]{1,0:T(8,128)(2,1)}, u32[]{:S(2)}, u32[]{:S(2)}) collective-permute-start(bf16[256,1024]{1,0:T(8,128)(2,1)} %back_other.1), channel_id=1, source_target_pairs={{0,1},{1,0},{2,3},{3,2},{4,5},{5,4},{6,7},{7,6},{8,9},{9,8},{10,11... | collective-permute-start | bytes 1572872 | tf_op jit(solution)/shard_map/ppermute | solution.py:540
  69.5 5.3 %back_own.1.own_ref = f32[2,256,512]{2,1,0:T(8,128)} custom-call(s32[1]{0:T(128)} %bitcast.layer_ref.half_ref, bf16[4,8,4,64,128]{4,3,2,1,0:T(8,128)(2,1)} %bitcast.5.blocks_hbm, bf16[512,2048]{1,0:T(8,128)(2,1)} %get-tuple-element.14.row_hbm, bf16[1024,1024]{1,0:T(8,128)(2,1)} %get-tuple-element.15.col_hbm, f32[2,2,256,512]{3,2,1,0:T(8,128)} %get-tuple-element.16.screen_hbm), custom_call_target="tpu_custom_call" | custom-call | flops 2000000000 | bytes 8388608 | tf_op jit(solution)/shard_map/back_own/pallas_call | solution.py:450
  74.7 0.0 collective-permute-done.3.middle_ref
  74.8 4.9 %finish.1 = f32[2,256,512]{2,1,0:T(8,128)} custom-call(bf16[256,1024]{1,0:T(8,128)(2,1)} %collective-permute-done.3.middle_ref, f32[2,256,512]{2,1,0:T(8,128)} %back_own.1.own_ref, bf16[1024,1024]{1,0:T(8,128)(2,1)} %get-tuple-element.15.col_hbm, f32[2,2,256,512]{3,2,1,0:T(8,128)} %get-tuple-element.16.screen_hbm), custom_call_target="tpu_custom_call" | custom-call | flops 1000000000 | bytes 8388608 | tf_op jit(solution)/shard_map/finish/pallas_call | solution.py:488
Async XLA Ops:
  2.2 15.4 %collective-permute-start.2 = (bf16[176,128]{1,0:T(8,128)(2,1)}, bf16[176,128]{1,0:T(8,128)(2,1)}, u32[]{:S(2)}, u32[]{:S(2)}) collective-permute-start(bf16[176,128]{1,0:T(8,128)(2,1)} %pack.1.own_ref), channel_id=1, source_target_pairs={{0,48},{2,50},{4,52},{6,54},{8,56},{10,58},{12,60},{14,62},{16,0},... | collective-permute-start | bytes 135176 | tf_op jit(solution)/shard_map/ppermute | solution.py:530
  9.1 8.4 %collective-permute-start.1 = (bf16[176,128]{1,0:T(8,128)(2,1)}, bf16[176,128]{1,0:T(8,128)(2,1)}, u32[]{:S(2)}, u32[]{:S(2)}) collective-permute-start(bf16[176,128]{1,0:T(8,128)(2,1)} %pack.1.own_ref), channel_id=1, source_target_pairs={{0,32},{2,34},{4,36},{6,38},{8,40},{10,42},{12,44},{14,46},{16,48}... | collective-permute-start | bytes 135176 | tf_op jit(solution)/shard_map/ppermute | solution.py:530
  10.1 7.5 %collective-permute-start = (bf16[176,128]{1,0:T(8,128)(2,1)}, bf16[176,128]{1,0:T(8,128)(2,1)}, u32[]{:S(2)}, u32[]{:S(2)}) collective-permute-start(bf16[176,128]{1,0:T(8,128)(2,1)} %pack.1.own_ref), channel_id=1, source_target_pairs={{0,16},{2,18},{4,20},{6,22},{8,24},{10,26},{12,28},{14,30},{16,32}... | collective-permute-start | bytes 135176 | tf_op jit(solution)/shard_map/ppermute | solution.py:530
  26.7 35.1 %all-to-all-start = ((bf16[32,4,64,128]{3,2,1,0:T(8,128)(2,1)}), bf16[32,4,64,128]{3,2,1,0:T(8,128)(2,1)}, u32[]{:S(2)}, u32[]{:S(2)}) async-start(bf16[32,4,64,128]{3,2,1,0:T(8,128)(2,1)} %front_others.1), calls=%async_computation | async-start | bytes 4194304 | tf_op jit(solution)/shard_map/all_to_all | solution.py:533
  66.4 8.4 %collective-permute-start.3 = (bf16[256,1024]{1,0:T(8,128)(2,1)}, bf16[256,1024]{1,0:T(8,128)(2,1)}, u32[]{:S(2)}, u32[]{:S(2)}) collective-permute-start(bf16[256,1024]{1,0:T(8,128)(2,1)} %back_other.1), channel_id=1, source_target_pairs={{0,1},{1,0},{2,3},{3,2},{4,5},{5,4},{6,7},{7,6},{8,9},{9,8},{10,11... | collective-permute-start | bytes 1572872 | tf_op jit(solution)/shard_map/ppermute | solution.py:540

commit v3 on v2

--- a/solution.py
+++ b/solution.py
@@ -16,7 +16,7 @@
 NORM = 1.0 / math.sqrt(512.0)
 NN = (((1,), (0,)), ((), ()))
 NT = (((1,), (1,)), ((), ()))
-LIMIT = 64 << 20
+LIMIT = 20 << 20
 
 
 def dot(first, second, numbers=NN):
@@ -112,10 +112,7 @@
     return copies
 
 
-def pack_kernel(counts_hbm, vis_hbm, kernels_hbm, offsets_hbm, out_ref, counts, vis, kernels, all_offsets, sems):
-    copies = fetch((counts_hbm, vis_hbm, kernels_hbm, offsets_hbm), (counts, vis, kernels, all_offsets), sems)
-    for copy in copies:
-        copy.wait()
+def pack_kernel(counts, vis, kernels, all_offsets, out_ref):
     live = counts[0, 0]
     slot = iota((8, 128), 0)
     samples = [jnp.where(slot < live, vis[part].astype(F32), 0.0) for part in range(2)]
@@ -140,15 +137,8 @@
     return pl.pallas_call(
         pack_kernel,
         out_shape=jax.ShapeDtypeStruct((176, 128), BF16),
-        in_specs=[hbm()] * 4,
+        in_specs=[smem()] + [vmem()] * 3,
         out_specs=vmem(),
-        scratch_shapes=[
-            pltpu.SMEM((1, 1), jnp.int32),
-            pltpu.VMEM((2, 8, VB), BF16),
-            pltpu.VMEM((2, 8, 8, VB), BF16),
-            pltpu.VMEM((2, 8, VB), jnp.int32),
-            pltpu.SemaphoreType.DMA((4,)),
-        ],
         compiler_params=pltpu.CompilerParams(vmem_limit_bytes=LIMIT),
         name="pack",
     )(counts, vis, kernels, offsets)
@@ -167,7 +157,7 @@
                 place(out_ref, part, base, jnp.concatenate([first[part], second[part]], axis=0).astype(BF16))
 
 
-def grid_slot(samples, digits, kernels, row_table, col_table, spreads, turned, halves, sent, arrive=None):
+def grid_slot(samples, digits, kernels, row_table, col_table, spreads, turned, halves, sent):
     slot = iota((8, 128), 0)
     tile = iota((64, 8, 128), 0)
     for axis in range(2):
@@ -177,8 +167,6 @@
             spreads[axis, :, block * VB : (block + 1) * VB] = (
                 jnp.where(tile == home[None], values[None], 0.0).reshape(512, VB).astype(BF16)
             )
-    if arrive is not None:
-        arrive()
     for quarter in range(4):
         lanes = slice(quarter * 256, (quarter + 1) * 256)
         rows = dot(row_table[...], spreads[0, :, lanes])
@@ -216,13 +204,9 @@
     ]
 
 
-def table_scratch():
-    return [pltpu.VMEM((512, 512), BF16), pltpu.VMEM((1024, 1024), BF16), pltpu.SemaphoreType.DMA((2,))]
-
-
 def front_own_kernel(
-    group_ref, rows_ref, cols_ref, own_ref, row_hbm, col_hbm, out_hbm,
-    spreads, turned, halves, sent, sems, row_out, col_out, table_sems,
+    group_ref, rows_ref, cols_ref, own_ref, row_out, col_out, out_hbm,
+    spreads, turned, halves, sent, sems,
 ):
     def below(ref, part, base, value):
         ref[part * 512 + base : part * 512 + base + 16, :] = value
@@ -234,12 +218,10 @@
         real, imag = times(row_pick(small, index), base)
         row_out[index * 64 : index * 64 + 64, :] = real.astype(BF16)
         row_out[256 + index * 64 : 320 + index * 64, :] = (-imag).astype(BF16)
-    copies = fetch((row_out, col_out), (row_hbm, col_hbm), table_sems)
     grid_slot(*unpacked(own_ref), row_out, col_out, spreads, turned, halves, sent.at[0])
     copy = pltpu.make_async_copy(sent.at[0], out_hbm.at[:, group_ref[0] & 3], sems.at[0])
     copy.start()
-    for copy in copies + [copy]:
-        copy.wait()
+    copy.wait()
 
 
 def front_own(group, facet_rows, facet_cols, own):
@@ -251,8 +233,8 @@
             jax.ShapeDtypeStruct((32, 4, 64, 128), BF16),
         ],
         in_specs=[smem(), smem(), smem(), vmem()],
-        out_specs=[hbm()] * 3,
-        scratch_shapes=front_scratch(1) + table_scratch(),
+        out_specs=[vmem(), vmem(), hbm()],
+        scratch_shapes=front_scratch(1),
         compiler_params=pltpu.CompilerParams(vmem_limit_bytes=LIMIT),
         cost_estimate=pl.CostEstimate(flops=3 * 10**9, bytes_accessed=4 << 20, transcendentals=0),
         name="front_own",
@@ -260,21 +242,12 @@
 
 
 def front_others_kernel(
-    group_ref, first_ref, second_ref, third_ref, row_hbm, col_hbm, begun_hbm, out_hbm,
-    spreads, turned, halves, sent, sems, row_table, col_table, table_sems,
+    group_ref, first_ref, second_ref, third_ref, row_table, col_table, begun_hbm, out_hbm,
+    spreads, turned, halves, sent, sems,
 ):
-    tables = fetch((row_hbm, col_hbm), (row_table, col_table), table_sems)
-
-    def arrive():
-        for copy in tables:
-            copy.wait()
-
     copies = []
     for index, ref in enumerate((first_ref, second_ref, third_ref)):
-        grid_slot(
-            *unpacked(ref), row_table, col_table, spreads, turned, halves, sent.at[index],
-            arrive if index == 0 else None,
-        )
+        grid_slot(*unpacked(ref), row_table, col_table, spreads, turned, halves, sent.at[index])
         source = (group_ref[0] + 3 - index) & 3
         copy = pltpu.make_async_copy(sent.at[index], out_hbm.at[:, source], sems.at[index])
         copy.start()
@@ -287,9 +260,9 @@
     return pl.pallas_call(
         front_others_kernel,
         out_shape=jax.ShapeDtypeStruct((32, 4, 64, 128), BF16),
-        in_specs=[smem()] + [vmem()] * 3 + [hbm()] * 3,
+        in_specs=[smem()] + [vmem()] * 5 + [hbm()],
         out_specs=hbm(),
-        scratch_shapes=front_scratch(3) + table_scratch(),
+        scratch_shapes=front_scratch(3),
         input_output_aliases={6: 0},
         compiler_params=pltpu.CompilerParams(vmem_limit_bytes=LIMIT),
         cost_estimate=pl.CostEstimate(flops=6 * 10**9, bytes_accessed=4 << 20, transcendentals=0),
@@ -310,29 +283,24 @@
 
 
 def tables_kernel(
-    layer_ref, rows_ref, cols_ref, weights_ref, screen_hbm, row_hbm, col_hbm, screen_out_hbm,
-    screen, row_out, col_out, screen_out, sems,
+    layer_ref, rows_ref, cols_ref, weights_ref, screen_hbm,
+    high_out, base_out, small_out, cell_out, own_out, other_out, screen, sems,
 ):
     layer = layer_ref[0]
-    (arrival,) = fetch((screen_hbm.at[0, pl.ds(layer * 256, 256)],), (screen,), sems.at[pl.ds(3, 1)])
-
-    def beside(ref, part, base, value):
-        ref[base : base + 16, part * 1024 : (part + 1) * 1024] = value
-
-    lane_table(rows_ref, 16, 64, 0, row_out, beside)
-    small = offset_roots(cols_ref, 8)
-    base = cell_roots()
-    for column in range(8):
-        real, imag = times(row_pick(small, column), base)
-        real, imag = real.astype(BF16), imag.astype(BF16)
-        rows = slice(column * 128, column * 128 + 64)
-        col_out[rows, :512] = real
-        col_out[rows, 512:] = imag
-        rows = slice(column * 128 + 64, column * 128 + 128)
-        col_out[rows, :512] = -imag
-        col_out[rows, 512:] = real
+    (arrival,) = fetch((screen_hbm.at[0, pl.ds(layer * 256, 256)],), (screen,), sems)
+    frequency, _ = lane_steps(rows_ref, 16, 64)
+    high, middle, low = lane_roots(frequency, 0)
+    small, cell = offset_roots(cols_ref, 8), cell_roots()
+    for part in range(2):
+        high_out[part] = high[part]
+        small_out[part] = small[part]
+        cell_out[part] = cell[part]
+    for index in range(8):
+        base = times(row_pick(middle, index), low)
+        for part in range(2):
+            base_out[part, index * 8 : index * 8 + 8, :] = base[part]
     arrival.wait()
-    for side in range(2):
+    for side, target in enumerate((own_out, other_out)):
         weight = weights_ref[layer if side == 0 else 1 - layer] * 4.0
         for chunk in range(4):
             rows = slice(chunk * 64, (chunk + 1) * 64)
@@ -340,47 +308,38 @@
             whole = jnp.floor(turns + 0.5)
             cosine, sine = sincos_small((turns - whole) * (0.5 * math.pi))
             real, imag = rotate_quarter(cosine, sine, whole.astype(jnp.int32))
-            screen_out[side, 0, rows, :] = real
-            screen_out[side, 1, rows, :] = imag
-    for copy in fetch((row_out, col_out, screen_out), (row_hbm, col_hbm, screen_out_hbm), sems):
-        copy.wait()
+            target[0, rows, :] = real.astype(BF16)
+            target[1, rows, :] = imag.astype(BF16)
 
 
 def tables(layer, sub_rows, sub_cols, weights, screen):
     return pl.pallas_call(
         tables_kernel,
         out_shape=[
-            jax.ShapeDtypeStruct((512, 2048), BF16),
-            jax.ShapeDtypeStruct((1024, 1024), BF16),
-            jax.ShapeDtypeStruct((2, 2, 256, 512), F32),
+            jax.ShapeDtypeStruct((2, 8, 1024), F32),
+            jax.ShapeDtypeStruct((2, 64, 1024), F32),
+            jax.ShapeDtypeStruct((2, 8, 512), F32),
+            jax.ShapeDtypeStruct((2, 64, 512), F32),
+            jax.ShapeDtypeStruct((2, 256, 512), BF16),
+            jax.ShapeDtypeStruct((2, 256, 512), BF16),
         ],
         in_specs=[smem(), smem(), smem(), smem(), hbm()],
-        out_specs=[hbm()] * 3,
-        scratch_shapes=[
-            pltpu.VMEM((256, 512), F32),
-            pltpu.VMEM((512, 2048), BF16),
-            pltpu.VMEM((1024, 1024), BF16),
-            pltpu.VMEM((2, 2, 256, 512), F32),
-            pltpu.SemaphoreType.DMA((4,)),
-        ],
-        compiler_params=pltpu.CompilerParams(vmem_limit_bytes=LIMIT),
-        cost_estimate=pl.CostEstimate(flops=10**9, bytes_accessed=16 << 20, transcendentals=0),
+        out_specs=[vmem()] * 6,
+        scratch_shapes=[pltpu.VMEM((256, 512), F32), pltpu.SemaphoreType.DMA((1,))],
+        compiler_params=pltpu.CompilerParams(vmem_limit_bytes=LIMIT),
+        cost_estimate=pl.CostEstimate(flops=10**9, bytes_accessed=8 << 20, transcendentals=0),
         name="tables",
     )(layer, sub_rows, sub_cols, weights, screen)
 
 
-def block_copies(blocks_hbm, blocks, sems):
-    return fetch(
-        [blocks_hbm.at[:, 2 * pair : 2 * pair + 2] for pair in range(4)],
-        [blocks.at[:, 2 * pair : 2 * pair + 2] for pair in range(4)],
-        sems,
-    )
-
-
-def middle_rows(blocks, copies, row_table, store):
+def middle_rows(half, blocks, high, base, row_table, store):
+    for index in range(4):
+        row = pl.ds(half * 4 + index, 1)
+        value = times((high[0, row, :], high[1, row, :]), (base[0], base[1]))
+        for part in range(2):
+            row_table[index * 64 : index * 64 + 64, part * 1024 : part * 1024 + 1024] = value[part].astype(BF16)
     sign = jnp.where((iota((1, 128), 1) & 64) == 0, -1.0, 1.0)
     for pair in range(4):
-        copies[pair].wait()
         placed = jnp.concatenate(
             [blocks[:, 2 * pair + part].reshape(1024, 128) for part in range(2)], axis=1
         )
@@ -394,90 +353,73 @@
 
 def screened(middle, col_table, screen):
     facet = dot(middle, col_table)
-    return times((facet[:, :512], facet[:, 512:]), (screen[0], screen[1]))
-
-
-def back_other_kernel(half_ref, blocks_hbm, row_hbm, out_ref, row_table, blocks, sems, block_sems):
-    (copy,) = fetch((row_hbm.at[pl.ds(half_ref[0] * 256, 256)],), (row_table,), sems)
-    arriving = block_copies(blocks_hbm, blocks, block_sems)
-    copy.wait()
-
+    return times((facet[:, :512], facet[:, 512:]), (screen[0].astype(F32), screen[1].astype(F32)))
+
+
+def back_other_kernel(half_ref, blocks, high, base, out_ref, row_table):
     def store(lanes, value):
         out_ref[:, lanes] = value
 
-    middle_rows(blocks, arriving, row_table, store)
-
-
-def back_other(half, blocks, row_table):
+    middle_rows(half_ref[0], blocks, high, base, row_table, store)
+
+
+def back_other(half, blocks, high, base):
     return pl.pallas_call(
         back_other_kernel,
         out_shape=jax.ShapeDtypeStruct((256, 1024), BF16),
-        in_specs=[smem(), hbm(), hbm()],
+        in_specs=[smem()] + [vmem()] * 3,
         out_specs=vmem(),
-        scratch_shapes=[
-            pltpu.VMEM((256, 2048), BF16),
-            pltpu.VMEM((4, 8, 4, CON, 128), BF16),
-            pltpu.SemaphoreType.DMA((1,)),
-            pltpu.SemaphoreType.DMA((4,)),
-        ],
+        scratch_shapes=[pltpu.VMEM((256, 2048), BF16)],
         compiler_params=pltpu.CompilerParams(vmem_limit_bytes=LIMIT),
         cost_estimate=pl.CostEstimate(flops=10**9, bytes_accessed=4 << 20, transcendentals=0),
         name="back_other",
-    )(half, blocks, row_table)
-
-
-def back_own_kernel(
-    half_ref, blocks_hbm, row_hbm, col_hbm, screen_hbm, out_ref,
-    row_table, blocks, col_table, screen, middle, sems, block_sems,
-):
-    (first,) = fetch((row_hbm.at[pl.ds(half_ref[0] * 256, 256)],), (row_table,), sems)
-    arriving = block_copies(blocks_hbm, blocks, block_sems)
-    copies = fetch((col_hbm, screen_hbm.at[0]), (col_table, screen), sems.at[pl.ds(1, 2)])
-    first.wait()
-
+    )(half, blocks, high, base)
+
+
+def back_own_kernel(half_ref, blocks, high, base, small, cell, screen, out_ref, col_out, row_table, middle):
     def store(lanes, value):
         middle[:, lanes] = value
 
-    middle_rows(blocks, arriving, row_table, store)
-    for copy in copies:
-        copy.wait()
-    real, imag = screened(middle[...], col_table[...], screen)
+    middle_rows(half_ref[0], blocks, high, base, row_table, store)
+    for column in range(8):
+        row = slice(column, column + 1)
+        value = times((small[0, row, :], small[1, row, :]), (cell[0], cell[1]))
+        real, imag = value[0].astype(BF16), value[1].astype(BF16)
+        rows = slice(column * 128, column * 128 + 64)
+        col_out[rows, :512] = real
+        col_out[rows, 512:] = imag
+        rows = slice(column * 128 + 64, column * 128 + 128)
+        col_out[rows, :512] = -imag
+        col_out[rows, 512:] = real
+    real, imag = screened(middle[...], col_out[...], screen)
     out_ref[0] = real
     out_ref[1] = imag
 
 
-def back_own(half, blocks, row_table, col_table, screen):
+def back_own(half, blocks, high, base, small, cell, screen):
     return pl.pallas_call(
         back_own_kernel,
-        out_shape=jax.ShapeDtypeStruct((2, 256, 512), F32),
-        in_specs=[smem()] + [hbm()] * 4,
-        out_specs=vmem(),
-        scratch_shapes=[
-            pltpu.VMEM((256, 2048), BF16),
-            pltpu.VMEM((4, 8, 4, CON, 128), BF16),
-            pltpu.VMEM((1024, 1024), BF16),
-            pltpu.VMEM((2, 256, 512), F32),
-            pltpu.VMEM((256, 1024), BF16),
-            pltpu.SemaphoreType.DMA((3,)),
-            pltpu.SemaphoreType.DMA((4,)),
+        out_shape=[
+            jax.ShapeDtypeStruct((2, 256, 512), F32),
+            jax.ShapeDtypeStruct((1024, 1024), BF16),
         ],
+        in_specs=[smem()] + [vmem()] * 6,
+        out_specs=[vmem(), vmem()],
+        scratch_shapes=[pltpu.VMEM((256, 2048), BF16), pltpu.VMEM((256, 1024), BF16)],
         compiler_params=pltpu.CompilerParams(vmem_limit_bytes=LIMIT),
         cost_estimate=pl.CostEstimate(flops=2 * 10**9, bytes_accessed=8 << 20, transcendentals=0),
         name="back_own",
-    )(half, blocks, row_table, col_table, screen)
-
-
-def finish_kernel(middle_ref, own_ref, col_hbm, screen_hbm, out_hbm, col_table, screen, image, sems):
-    copies = fetch((col_hbm, screen_hbm.at[1]), (col_table, screen), sems)
-    copies[0].wait()
-    copies[1].wait()
+    )(half, blocks, high, base, small, cell, screen)
+
+
+def finish_kernel(middle_ref, own_ref, col_ref, screen_ref, out_hbm, image, sems):
     leaving = []
     for chunk in range(2):
         rows = slice(chunk * 128, chunk * 128 + 128)
-        value = screened(middle_ref[rows, :], col_table[...], (screen[0, rows, :], screen[1, rows, :]))
+        value = screened(middle_ref[rows, :], col_ref[...], (screen_ref[0, rows, :], screen_ref[1, rows, :]))
         for part in range(2):
             image[chunk, part] = own_ref[part, rows, :] + value[part]
-        copy = pltpu.make_async_copy(image.at[chunk], out_hbm.at[:, pl.ds(chunk * 128, 128)], sems.at[2 + chunk])
+        copy = pltpu.make_async_copy(image.at[chunk], out_hbm.at[:, pl.ds(chunk * 128, 128)], sems.at[chunk])
         copy.start()
         leaving.append(copy)
     for copy in leaving:
@@ -488,14 +430,9 @@
     return pl.pallas_call(
         finish_kernel,
         out_shape=jax.ShapeDtypeStruct((2, 256, 512), F32),
-        in_specs=[vmem(), vmem(), hbm(), hbm()],
+        in_specs=[vmem()] * 4,
         out_specs=hbm(),
-        scratch_shapes=[
-            pltpu.VMEM((1024, 1024), BF16),
-            pltpu.VMEM((2, 256, 512), F32),
-            pltpu.VMEM((2, 2, 128, 512), F32),
-            pltpu.SemaphoreType.DMA((4,)),
-        ],
+        scratch_shapes=[pltpu.VMEM((2, 2, 128, 512), F32), pltpu.SemaphoreType.DMA((2,))],
         compiler_params=pltpu.CompilerParams(vmem_limit_bytes=LIMIT),
         cost_estimate=pl.CostEstimate(flops=10**9, bytes_accessed=8 << 20, transcendentals=0),
         name="finish",
@@ -534,12 +471,12 @@
         outgoing, "sf", split_axis=0, concat_axis=0, tiled=True, axis_index_groups=GROUPS
     )
     layer = lax.axis_index("wa").reshape(1)
-    row_table, col_table, screen = tables(layer, sub_rows, sub_cols, layer_w, screen_n)
+    high, base, small, cell, own_screen, other_screen = tables(layer, sub_rows, sub_cols, layer_w, screen_n)
     blocks = incoming.reshape(4, 8, 4, CON, 128)
-    theirs = back_other(1 - layer, blocks, row_table)
+    theirs = back_other(1 - layer, blocks, high, base)
     received = lax.ppermute(theirs, "wa", [(0, 1), (1, 0)])
-    own_part = back_own(layer, blocks, row_table, col_table, screen)
-    return finish(received, own_part, col_table, screen)[:, None]
+    own_part, col_table = back_own(layer, blocks, high, base, small, cell, own_screen)
+    return finish(received, own_part, col_table, other_screen)[:, None]
 
 
 def solution(mesh):

time: 80.3 us -> 71 us (0.88)
  Pallas kernels: 35.7 us -> 17.8 us
  local copies, waits for them, and re-layouts: 0 us -> 6.8 us
  starting transfers between devices: 21.1 us -> 22.3 us
    unnamed x0 -> x24, local copies, waits for them, and re-layouts: none -> 6.8 us
    pallas_call x2, Pallas kernels: 10.4 us -> 4.5 us  [the longest x1 2.39 us: tables(): pl.pallas_call(tables_kernel, out_shape=[jax.ShapeDtypeStruct((2, 8, 1024...]
    pallas_call x1, Pallas kernels: 4.94 us -> 1.68 us  [finish(): pl.pallas_call(finish_kernel, out_shape=jax.ShapeDtypeStruct((2, 256, 512...]
    pallas_call x1, Pallas kernels: 4.59 us -> 1.36 us  [back_other(): pl.pallas_call(back_other_kernel, out_shape=jax.ShapeDtypeStruct((256, 10...]
    pallas_call x1, Pallas kernels: 9.17 us -> 6.62 us  [front_others(): pl.pallas_call(front_others_kernel, out_shape=jax.ShapeDtypeStruct((32, 4...]
    pallas_call x1, Pallas kernels: 5.17 us -> 3.53 us  [front_own(): pl.pallas_call(front_own_kernel, out_shape=[jax.ShapeDtypeStruct((512, 51...]
    pallas_call x1, Pallas kernels: 1.5 us -> 0.07 us  [pack(): pl.pallas_call(pack_kernel, out_shape=jax.ShapeDtypeStruct((176, 128), BF...]
    ppermute x3, starting transfers between devices: 10.2 us -> 11.4 us  [per_device(): packs = [lax.ppermute(own, 'sf', shifted(turn)) for turn in (1, 2, 3)]]
  transfers between devices with their start and end apart: 5 -> 5, of which waited for: 1 -> 1; matrix products, arithmetic and copies ran while one was open for 0% -> 0% of each run, Pallas kernels for 19% -> 11%
where the time goes in v3:
time: 71 us; the launch traced here: 70.6 us
  waiting for transfers between devices  22.8 us (32%)
  starting transfers between devices  22.3 us (31%)
  Pallas kernels  17.8 us (25%)
  local copies, waits for them, and re-layouts  6.8 us (10%)
  between operations  0.96 us (1%)
    all_to_all x1, waiting for transfers between devices, per_device(): lax.all_to_all(outgoing, 'sf', split_axis=0, concat_axis=0, tiled=True, a...  22.8 us
    ppermute x3, starting transfers between devices, per_device(): packs = [lax.ppermute(own, 'sf', shifted(turn)) for turn in (1, 2, 3)]  11.4 us
    all_to_all x1, starting transfers between devices, per_device(): lax.all_to_all(outgoing, 'sf', split_axis=0, concat_axis=0, tiled=True, a...  7.81 us
    unnamed x24, local copies, waits for them, and re-layouts  6.8 us
    pallas_call x1, Pallas kernels, front_others(): pl.pallas_call(front_others_kernel, out_shape=jax.ShapeDtypeStruct((32, 4...  6.62 us
    pallas_call x1, Pallas kernels, front_own(): pl.pallas_call(front_own_kernel, out_shape=[jax.ShapeDtypeStruct((512, 51...  3.53 us
    ppermute x1, starting transfers between devices, per_device(): received = lax.ppermute(theirs, 'wa', [(0, 1), (1, 0)])  3.11 us
    pallas_call x1, Pallas kernels, tables(): pl.pallas_call(tables_kernel, out_shape=[jax.ShapeDtypeStruct((2, 8, 1024...  2.39 us
  transfers between devices with their start and end apart: 5, of which 1 were waited for; matrix products, arithmetic and copies ran while one was open for 0% of the time, Pallas kernels for 11%

profile of v3, /device:TPU:1, one launch (start us, length us, event | category | flops | bytes accessed | tf_op | source)
XLA Modules:
  0.0 70.6 jit_solution(10498554294353655296)
XLA Ops:
  0.7 0.7 %copy-done.1 = bf16[2,8,1,1,8,128]{5,4,3,2,1,0:T(8,128)(2,1)S(1)} copy-done((bf16[2,8,1,1,8,128]{5,4,3,2,1,0:T(8,128)(2,1)S(1)}, bf16[2,8,1,1,8,128]{5,4,3,2,1,0:T(8,128)(2,1)}, u32[]{:S(2)}) %copy-start.1) | copy-done | bytes 32792
  1.4 0.7 copy-done.2
  2.1 0.7 copy-done.3
  2.8 0.1 pack.1.own_ref
  2.9 3.9 %collective-permute-start = (bf16[176,128]{1,0:T(8,128)(2,1)S(1)}, bf16[176,128]{1,0:T(8,128)(2,1)S(1)}, u32[]{:S(2)}, u32[]{:S(2)}) collective-permute-start(bf16[176,128]{1,0:T(8,128)(2,1)S(1)} %pack.1.own_ref), channel_id=1, source_target_pairs={{0,16},{2,18},{4,20},{6,22},{8,24},{10,26},{12,28},{14,30},{16,32}... | collective-permute-start | bytes 135176 | tf_op jit(solution)/shard_map/ppermute | solution.py:467
  6.8 5.1 %collective-permute-start.1 = (bf16[176,128]{1,0:T(8,128)(2,1)S(1)}, bf16[176,128]{1,0:T(8,128)(2,1)S(1)}, u32[]{:S(2)}, u32[]{:S(2)}) collective-permute-start(bf16[176,128]{1,0:T(8,128)(2,1)S(1)} %pack.1.own_ref), channel_id=1, source_target_pairs={{0,32},{2,34},{4,36},{6,38},{8,40},{10,42},{12,44},{14,46},{16,48}... | collective-permute-start | bytes 135176 | tf_op jit(solution)/shard_map/ppermute | solution.py:467
  11.9 2.4 %collective-permute-start.2 = (bf16[176,128]{1,0:T(8,128)(2,1)S(1)}, bf16[176,128]{1,0:T(8,128)(2,1)S(1)}, u32[]{:S(2)}, u32[]{:S(2)}) collective-permute-start(bf16[176,128]{1,0:T(8,128)(2,1)S(1)} %pack.1.own_ref), channel_id=1, source_target_pairs={{0,48},{2,50},{4,52},{6,54},{8,56},{10,58},{12,60},{14,62},{16,0},... | collective-permute-start | bytes 135176 | tf_op jit(solution)/shard_map/ppermute | solution.py:467
  14.3 0.7 copy-done.5
  14.9 0.7 copy-done.6
  15.6 3.5 %front_own.1 = (bf16[512,512]{1,0:T(8,128)(2,1)S(1)}, bf16[1024,1024]{1,0:T(8,128)(2,1)S(1)}, bf16[32,4,64,128]{3,2,1,0:T(8,128)(2,1)S(1)}) custom-call(s32[1]{0:T(128)} %bitcast.1.group_ref, s32[16]{0:T(128)S(1)} %copy-done.5, s32[8]{0:T(128)S(1)} %copy-done.6, bf16[176,128]{1,0:T(8,128)(2,1)S(1)} %pack.1.own_ref), custom_call_target="tpu_custom_call" | custom-call | flops 3000000000 | bytes 4194304 | tf_op jit(solution)/shard_map/front_own/pallas_call | solution.py:228
  19.1 0.0 collective-permute-done.first_ref
  19.1 6.6 %front_others.1 = bf16[32,4,64,128]{3,2,1,0:T(8,128)(2,1)S(1)} custom-call(s32[1]{0:T(128)} %bitcast.1.group_ref, bf16[176,128]{1,0:T(8,128)(2,1)S(1)} %collective-permute-done.first_ref, bf16[176,128]{1,0:T(8,128)(2,1)S(1)} %collective-permute-done.1.second_ref, ...), custom_call_target="tpu_custom_call", output_to_operand_aliasing={{}: (6, {})} | custom-call | flops 6000000000 | bytes 4194304 | tf_op jit(solution)/shard_map/front_others/pallas_call | solution.py:260
  25.8 1.3 %copy-done = bf16[32,4,64,128]{3,2,1,0:T(8,128)(2,1)} copy-done((bf16[32,4,64,128]{3,2,1,0:T(8,128)(2,1)}, bf16[32,4,64,128]{3,2,1,0:T(8,128)(2,1)S(1)}, u32[]{:S(2)}) %copy-start) | copy-done | bytes 2097176
  27.1 7.8 %all-to-all-start = ((bf16[32,4,64,128]{3,2,1,0:T(8,128)(2,1)}), bf16[32,4,64,128]{3,2,1,0:T(8,128)(2,1)S(1)}, u32[]{:S(2)}, u32[]{:S(2)}) async-start(bf16[32,4,64,128]{3,2,1,0:T(8,128)(2,1)} %copy-done), calls=%async_computation | async-start | bytes 4194304 | tf_op jit(solution)/shard_map/all_to_all | solution.py:470
  35.0 0.0 copy-start.4
  35.0 1.2 %copy-done.4 = f32[1,512,512]{2,1,0:T(8,128)S(1)} copy-done((f32[1,512,512]{2,1,0:T(8,128)S(1)}, f32[1,512,512]{2,1,0:T(8,128)}, u32[]{:S(2)}) %copy-start.4) | copy-done | bytes 1048600
  36.2 2.4 %tables.1 = (f32[2,8,1024]{2,1,0:T(8,128)S(1)}, f32[2,64,1024]{2,1,0:T(8,128)S(1)}, f32[2,8,512]{2,1,0:T(8,128)S(1)}, f32[2,64,512]{2,1,0:T(8,128)S(1)}, bf16[2,...) custom-call(s32[1]{0:T(128)} %bitcast.layer_ref.half_ref, s32[16]{0:T(128)S(1)} %copy-done.7, s32[8]{0:T(128)S(1)} %copy-done.8, ...), custom_call_target="tpu_custom_call" | custom-call | flops 1000000000 | bytes 8388608 | tf_op jit(solution)/shard_map/tables/pallas_call | solution.py:316
  38.6 0.0 copy-start.10
  38.6 0.8 %copy-done.10 = bf16[2,256,512]{2,1,0:T(8,128)(2,1)} copy-done((bf16[2,256,512]{2,1,0:T(8,128)(2,1)}, bf16[2,256,512]{2,1,0:T(8,128)(2,1)S(1)}, u32[]{:S(2)}) %copy-start.10) | copy-done | bytes 524312
  39.4 22.8 %all-to-all-done = bf16[32,4,64,128]{3,2,1,0:T(8,128)(2,1)S(1)} async-done(((bf16[32,4,64,128]{3,2,1,0:T(8,128)(2,1)}), bf16[32,4,64,128]{3,2,1,0:T(8,128)(2,1)S(1)}, u32[]{:S(2)}, u32[]{:S(2)}) %all-to-all-start) | async-done | bytes 2097184 | tf_op jit(solution)/shard_map/all_to_all | solution.py:470
  62.2 1.4 %back_other.1 = bf16[256,1024]{1,0:T(8,128)(2,1)S(1)} custom-call(s32[1]{0:T(128)S(6)} %sub.3.half_ref, bf16[4,8,4,64,128]{4,3,2,1,0:T(8,128)(2,1)S(1)} %bitcast.9, f32[2,8,1024]{2,1,0:T(8,128)S(1)} %get-tuple-element.19.high, f32[2,64,1024]{2,1,0:T(8,128)S(1)} %get-tuple-element.20.base), custom_call_target="tpu_custom_call" | custom-call | flops 1000000000 | bytes 4194304 | tf_op jit(solution)/shard_map/back_other/pallas_call | solution.py:367
  63.5 3.1 %collective-permute-start.3 = (bf16[256,1024]{1,0:T(8,128)(2,1)S(1)}, bf16[256,1024]{1,0:T(8,128)(2,1)S(1)}, u32[]{:S(2)}, u32[]{:S(2)}) collective-permute-start(bf16[256,1024]{1,0:T(8,128)(2,1)S(1)} %back_other.1), channel_id=1, source_target_pairs={{0,1},{1,0},{2,3},{3,2},{4,5},{5,4},{6,7},{7,6},{8,9},{9,8},{10,11... | collective-permute-start | bytes 1572872 | tf_op jit(solution)/shard_map/ppermute | solution.py:477
  66.6 2.1 %back_own.1 = (f32[2,256,512]{2,1,0:T(8,128)S(1)}, bf16[1024,1024]{1,0:T(8,128)(2,1)S(1)}) custom-call(s32[1]{0:T(128)} %bitcast.layer_ref.half_ref, bf16[4,8,4,64,128]{4,3,2,1,0:T(8,128)(2,1)S(1)} %bitcast.10, f32[2,8,1024]{2,1,0:T(8,128)S(1)} %get-tuple-element.19.high, f32[2,64,1024]{2,1,0:T(8,128)S(1)} %get-tuple-element.20.base, ...), custom_call_target="tpu_custom_call" | custom-call | flops 2000000000 | bytes 8388608 | tf_op jit(solution)/shard_map/back_own/pallas_call | solution.py:400
  68.8 1.7 %finish.1 = f32[2,256,512]{2,1,0:T(8,128)} custom-call(bf16[256,1024]{1,0:T(8,128)(2,1)S(1)} %collective-permute-done.3.middle_ref, f32[2,256,512]{2,1,0:T(8,128)S(1)} %get-tuple-element.24.own_ref, bf16[1024,1024]{1,0:T(8,128)(2,1)S(1)} %get-tuple-element.25.col_ref, bf16[2,256,512]{2,1,0:T(8,128)(2,1)S(1)} %get-tuple-element.26.screen_ref), custom_call_target="tpu_custom_call" | custom-call | flops 1000000000 | bytes 8388608 | tf_op jit(solution)/shard_map/finish/pallas_call | solution.py:430
  (17 shorter events, 0.0 us)
Async XLA Ops:
  0.7 0.8 %copy-start.1 = (bf16[2,8,1,1,8,128]{5,4,3,2,1,0:T(8,128)(2,1)S(1)}, bf16[2,8,1,1,8,128]{5,4,3,2,1,0:T(8,128)(2,1)}, u32[]{:S(2)}) copy-start(bf16[2,8,1,1,8,128]{5,4,3,2,1,0:T(8,128)(2,1)} %param.11) | copy-start | bytes 98308
  1.4 0.7 copy-start.2
  2.1 0.7 copy-start.3
  2.9 16.2 %collective-permute-start = (bf16[176,128]{1,0:T(8,128)(2,1)S(1)}, bf16[176,128]{1,0:T(8,128)(2,1)S(1)}, u32[]{:S(2)}, u32[]{:S(2)}) collective-permute-start(bf16[176,128]{1,0:T(8,128)(2,1)S(1)} %pack.1.own_ref), channel_id=1, source_target_pairs={{0,16},{2,18},{4,20},{6,22},{8,24},{10,26},{12,28},{14,30},{16,32}... | collective-permute-start | bytes 135176 | tf_op jit(solution)/shard_map/ppermute | solution.py:467
  6.8 12.4 %collective-permute-start.1 = (bf16[176,128]{1,0:T(8,128)(2,1)S(1)}, bf16[176,128]{1,0:T(8,128)(2,1)S(1)}, u32[]{:S(2)}, u32[]{:S(2)}) collective-permute-start(bf16[176,128]{1,0:T(8,128)(2,1)S(1)} %pack.1.own_ref), channel_id=1, source_target_pairs={{0,32},{2,34},{4,36},{6,38},{8,40},{10,42},{12,44},{14,46},{16,48}... | collective-permute-start | bytes 135176 | tf_op jit(solution)/shard_map/ppermute | solution.py:467
  11.9 7.3 %collective-permute-start.2 = (bf16[176,128]{1,0:T(8,128)(2,1)S(1)}, bf16[176,128]{1,0:T(8,128)(2,1)S(1)}, u32[]{:S(2)}, u32[]{:S(2)}) collective-permute-start(bf16[176,128]{1,0:T(8,128)(2,1)S(1)} %pack.1.own_ref), channel_id=1, source_target_pairs={{0,48},{2,50},{4,52},{6,54},{8,56},{10,58},{12,60},{14,62},{16,0},... | collective-permute-start | bytes 135176 | tf_op jit(solution)/shard_map/ppermute | solution.py:467
  14.3 0.7 copy-start.5
  14.9 0.7 copy-start.6
  25.8 1.3 %copy-start = (bf16[32,4,64,128]{3,2,1,0:T(8,128)(2,1)}, bf16[32,4,64,128]{3,2,1,0:T(8,128)(2,1)S(1)}, u32[]{:S(2)}) copy-start(bf16[32,4,64,128]{3,2,1,0:T(8,128)(2,1)S(1)} %front_others.1) | copy-start | bytes 6291460
  27.1 7.8 %copy-start.7 = (s32[16]{0:T(128)S(1)}, s32[16]{0:T(128)}, u32[]{:S(2)}) copy-start(s32[16]{0:T(128)} %rows_ref.3) | copy-start | bytes 196
  27.1 7.8 %copy-start.8 = (s32[8]{0:T(128)S(1)}, s32[8]{0:T(128)}, u32[]{:S(2)}) copy-start(s32[8]{0:T(128)} %cols_ref.3) | copy-start | bytes 100
  27.1 7.8 %copy-start.9 = (f32[2]{0:T(128)S(1)}, f32[2]{0:T(128)}, u32[]{:S(2)}) copy-start(f32[2]{0:T(128)} %weights_ref.1) | copy-start | bytes 28
  27.1 35.0 %all-to-all-start = ((bf16[32,4,64,128]{3,2,1,0:T(8,128)(2,1)}), bf16[32,4,64,128]{3,2,1,0:T(8,128)(2,1)S(1)}, u32[]{:S(2)}, u32[]{:S(2)}) async-start(bf16[32,4,64,128]{3,2,1,0:T(8,128)(2,1)} %copy-done), calls=%async_computation | async-start | bytes 4194304 | tf_op jit(solution)/shard_map/all_to_all | solution.py:470
  35.0 1.2 %copy-start.4 = (f32[1,512,512]{2,1,0:T(8,128)S(1)}, f32[1,512,512]{2,1,0:T(8,128)}, u32[]{:S(2)}) copy-start(f32[1,512,512]{2,1,0:T(8,128)} %screen_hbm.1) | copy-start | bytes 3145732
  38.6 0.8 %copy-start.10 = (bf16[2,256,512]{2,1,0:T(8,128)(2,1)}, bf16[2,256,512]{2,1,0:T(8,128)(2,1)S(1)}, u32[]{:S(2)}) copy-start(bf16[2,256,512]{2,1,0:T(8,128)(2,1)S(1)} %get-tuple-element.23.screen) | copy-start | bytes 1572868
  62.2 4.5 %copy-start.11 = (bf16[2,256,512]{2,1,0:T(8,128)(2,1)S(1)}, bf16[2,256,512]{2,1,0:T(8,128)(2,1)}, u32[]{:S(2)}) copy-start(bf16[2,256,512]{2,1,0:T(8,128)(2,1)} %copy-done.10) | copy-start | bytes 1572868
  63.5 5.2 %collective-permute-start.3 = (bf16[256,1024]{1,0:T(8,128)(2,1)S(1)}, bf16[256,1024]{1,0:T(8,128)(2,1)S(1)}, u32[]{:S(2)}, u32[]{:S(2)}) collective-permute-start(bf16[256,1024]{1,0:T(8,128)(2,1)S(1)} %back_other.1), channel_id=1, source_target_pairs={{0,1},{1,0},{2,3},{3,2},{4,5},{5,4},{6,7},{7,6},{8,9},{9,8},{10,11... | collective-permute-start | bytes 1572872 | tf_op jit(solution)/shard_map/ppermute | solution.py:477

commit v4 on v3

--- a/solution.py
+++ b/solution.py
@@ -55,6 +55,10 @@
         first[0] * second[0] - first[1] * second[1],
         first[0] * second[1] + first[1] * second[0],
     )
+
+
+def picked(ref, first, count):
+    return [ref[first + index] for index in range(count)]
 
 
 def cell_roots():
@@ -157,33 +161,54 @@
                 place(out_ref, part, base, jnp.concatenate([first[part], second[part]], axis=0).astype(BF16))
 
 
-def grid_slot(samples, digits, kernels, row_table, col_table, spreads, turned, halves, sent):
-    slot = iota((8, 128), 0)
+def spread_block(data, axis, block, spread):
+    _, digits, kernels = data
     tile = iota((64, 8, 128), 0)
-    for axis in range(2):
-        for block in range(8):
-            home = digits[axis][block : block + 1, :] + (digits[axis][block + 8 : block + 9, :] > slot).astype(jnp.int32)
-            values = kernels[axis][block * 8 : block * 8 + 8, :]
-            spreads[axis, :, block * VB : (block + 1) * VB] = (
-                jnp.where(tile == home[None], values[None], 0.0).reshape(512, VB).astype(BF16)
-            )
-    for quarter in range(4):
-        lanes = slice(quarter * 256, (quarter + 1) * 256)
-        rows = dot(row_table[...], spreads[0, :, lanes])
-        real_part, imag_part = (
-            jnp.concatenate([samples[8 * half + 2 * quarter + part : 8 * half + 2 * quarter + part + 1] for part in range(2)], axis=1)
-            for half in range(2)
-        )
-        real, imag = times((rows[:256], rows[256:]), (real_part, imag_part))
-        turned[:256, lanes] = real.astype(BF16)
-        turned[256:, lanes] = imag.astype(BF16)
-    half = dot(turned[...], spreads[1], NT).astype(BF16)
-    halves[:, :512] = half[:256]
-    halves[:, 512:] = half[256:]
-    result = dot(halves[...], col_table[...]).astype(BF16)
-    for row in range(4):
-        for column in range(8):
-            sent[row * 8 + column] = result[row * 64 : (row + 1) * 64, column * 128 : (column + 1) * 128]
+    home = digits[axis][block : block + 1, :] + (
+        digits[axis][block + 8 : block + 9, :] > iota((8, 128), 0)
+    ).astype(jnp.int32)
+    values = kernels[axis][block * 8 : block * 8 + 8, :]
+    spread[axis, :, block * VB : (block + 1) * VB] = (
+        jnp.where(tile == home[None], values[None], 0.0).reshape(512, VB).astype(BF16)
+    )
+
+
+def turn_rows(data, quarter, row_table, spread, turned):
+    samples = data[0]
+    lanes = slice(quarter * 256, (quarter + 1) * 256)
+    rows = dot(row_table[...], spread[0, :, lanes])
+    real_part, imag_part = (
+        jnp.concatenate([samples[8 * half + 2 * quarter + part : 8 * half + 2 * quarter + part + 1] for part in range(2)], axis=1)
+        for half in range(2)
+    )
+    real, imag = times((rows[:256], rows[256:]), (real_part, imag_part))
+    turned[:256, lanes] = real.astype(BF16)
+    turned[256:, lanes] = imag.astype(BF16)
+
+
+def peer(row, column):
+    return (column & 3) * 8 + (column >> 2) * 4 + row
+
+
+def grid_slots(refs, row_table, col_table, spread, turned, halves, store):
+    for index, ref in enumerate(refs):
+        data = unpacked(ref)
+        for axis in range(2):
+            for block in range(8):
+                spread_block(data, axis, block, spread)
+        for quarter in range(4):
+            turn_rows(data, quarter, row_table, spread, turned)
+        half = dot(turned[...], spread[1], NT).astype(BF16)
+        halves[index * 256 : index * 256 + 256, :512] = half[:256]
+        halves[index * 256 : index * 256 + 256, 512:] = half[256:]
+    for pair in range(4):
+        result = dot(halves[...], col_table[:, pair * 256 : pair * 256 + 256]).astype(BF16)
+        for index in range(len(refs)):
+            for row in range(4):
+                for part in range(2):
+                    start = index * 256 + row * 64
+                    value = result[start : start + 64, part * 128 : (part + 1) * 128]
+                    store(index, peer(row, 2 * pair + part), value)
 
 
 def unpacked(ref):
@@ -198,76 +223,71 @@
     return [
         pltpu.VMEM((2, 512, 1024), BF16),
         pltpu.VMEM((512, 1024), BF16),
-        pltpu.VMEM((256, 1024), BF16),
-        pltpu.VMEM((slots, 32, 64, 128), BF16),
-        pltpu.SemaphoreType.DMA((slots,)),
+        pltpu.VMEM((slots * 256, 1024), BF16),
     ]
 
 
 def front_own_kernel(
-    group_ref, rows_ref, cols_ref, own_ref, row_out, col_out, out_hbm,
-    spreads, turned, halves, sent, sems,
+    group_ref, offsets_ref, own_ref, row_out, col_out, out_ref, spreads, turned, halves,
 ):
     def below(ref, part, base, value):
         ref[part * 512 + base : part * 512 + base + 16, :] = value
 
-    lane_table(cols_ref, 8, 128, 64, col_out, below)
+    lane_table(picked(offsets_ref, 16, 8), 8, 128, 64, col_out, below)
     base = cell_roots()
-    small = offset_roots([rows_ref[4 * index + group_ref[0]] for index in range(4)], 4)
+    small = offset_roots([offsets_ref[4 * index + group_ref[0]] for index in range(4)], 4)
     for index in range(4):
         real, imag = times(row_pick(small, index), base)
         row_out[index * 64 : index * 64 + 64, :] = real.astype(BF16)
         row_out[256 + index * 64 : 320 + index * 64, :] = (-imag).astype(BF16)
-    grid_slot(*unpacked(own_ref), row_out, col_out, spreads, turned, halves, sent.at[0])
-    copy = pltpu.make_async_copy(sent.at[0], out_hbm.at[:, group_ref[0] & 3], sems.at[0])
-    copy.start()
-    copy.wait()
-
-
-def front_own(group, facet_rows, facet_cols, own):
+
+    def store(index, facet, value):
+        out_ref[facet] = value
+
+    grid_slots([own_ref], row_out, col_out, spreads, turned, halves, store)
+
+
+def front_own(group, offsets, own):
     return pl.pallas_call(
         front_own_kernel,
         out_shape=[
             jax.ShapeDtypeStruct((512, 512), BF16),
             jax.ShapeDtypeStruct((1024, 1024), BF16),
-            jax.ShapeDtypeStruct((32, 4, 64, 128), BF16),
+            jax.ShapeDtypeStruct((32, 64, 128), BF16),
         ],
-        in_specs=[smem(), smem(), smem(), vmem()],
-        out_specs=[vmem(), vmem(), hbm()],
+        in_specs=[smem(), smem(), vmem()],
+        out_specs=[vmem()] * 3,
         scratch_shapes=front_scratch(1),
         compiler_params=pltpu.CompilerParams(vmem_limit_bytes=LIMIT),
         cost_estimate=pl.CostEstimate(flops=3 * 10**9, bytes_accessed=4 << 20, transcendentals=0),
         name="front_own",
-    )(group, facet_rows, facet_cols, own)
+    )(group, offsets, own)
 
 
 def front_others_kernel(
-    group_ref, first_ref, second_ref, third_ref, row_table, col_table, begun_hbm, out_hbm,
-    spreads, turned, halves, sent, sems,
+    group_ref, first_ref, second_ref, third_ref, row_table, col_table, own_ref, out_ref, spreads, turned, halves,
 ):
-    copies = []
-    for index, ref in enumerate((first_ref, second_ref, third_ref)):
-        grid_slot(*unpacked(ref), row_table, col_table, spreads, turned, halves, sent.at[index])
-        source = (group_ref[0] + 3 - index) & 3
-        copy = pltpu.make_async_copy(sent.at[index], out_hbm.at[:, source], sems.at[index])
-        copy.start()
-        copies.append(copy)
-    for copy in copies:
-        copy.wait()
-
-
-def front_others(group, packs, row_table, col_table, begun):
+    group = group_ref[0]
+    for facet in range(32):
+        out_ref[facet, group & 3] = own_ref[facet]
+
+    def store(index, facet, value):
+        out_ref[facet, (group + 3 - index) & 3] = value
+
+    grid_slots([first_ref, second_ref, third_ref], row_table, col_table, spreads, turned, halves, store)
+
+
+def front_others(group, packs, row_table, col_table, own):
     return pl.pallas_call(
         front_others_kernel,
         out_shape=jax.ShapeDtypeStruct((32, 4, 64, 128), BF16),
-        in_specs=[smem()] + [vmem()] * 5 + [hbm()],
-        out_specs=hbm(),
+        in_specs=[smem()] + [vmem()] * 6,
+        out_specs=vmem(),
         scratch_shapes=front_scratch(3),
-        input_output_aliases={6: 0},
         compiler_params=pltpu.CompilerParams(vmem_limit_bytes=LIMIT),
         cost_estimate=pl.CostEstimate(flops=6 * 10**9, bytes_accessed=4 << 20, transcendentals=0),
         name="front_others",
-    )(group, *packs, row_table, col_table, begun)
+    )(group, *packs, row_table, col_table, own)
 
 
 def smem():
@@ -283,14 +303,14 @@
 
 
 def tables_kernel(
-    layer_ref, rows_ref, cols_ref, weights_ref, screen_hbm,
+    layer_ref, offsets_ref, weights_ref, screen_hbm,
     high_out, base_out, small_out, cell_out, own_out, other_out, screen, sems,
 ):
     layer = layer_ref[0]
     (arrival,) = fetch((screen_hbm.at[0, pl.ds(layer * 256, 256)],), (screen,), sems)
-    frequency, _ = lane_steps(rows_ref, 16, 64)
+    frequency, _ = lane_steps(picked(offsets_ref, 24, 16), 16, 64)
     high, middle, low = lane_roots(frequency, 0)
-    small, cell = offset_roots(cols_ref, 8), cell_roots()
+    small, cell = offset_roots(picked(offsets_ref, 40, 8), 8), cell_roots()
     for part in range(2):
         high_out[part] = high[part]
         small_out[part] = small[part]
@@ -312,7 +332,7 @@
             target[1, rows, :] = imag.astype(BF16)
 
 
-def tables(layer, sub_rows, sub_cols, weights, screen):
+def tables(layer, offsets, weights, screen):
     return pl.pallas_call(
         tables_kernel,
         out_shape=[
@@ -323,13 +343,13 @@
             jax.ShapeDtypeStruct((2, 256, 512), BF16),
             jax.ShapeDtypeStruct((2, 256, 512), BF16),
         ],
-        in_specs=[smem(), smem(), smem(), smem(), hbm()],
+        in_specs=[smem(), smem(), smem(), hbm()],
         out_specs=[vmem()] * 6,
         scratch_shapes=[pltpu.VMEM((256, 512), F32), pltpu.SemaphoreType.DMA((1,))],
         compiler_params=pltpu.CompilerParams(vmem_limit_bytes=LIMIT),
         cost_estimate=pl.CostEstimate(flops=10**9, bytes_accessed=8 << 20, transcendentals=0),
         name="tables",
-    )(layer, sub_rows, sub_cols, weights, screen)
+    )(layer, offsets, weights, screen)
 
 
 def middle_rows(half, blocks, high, base, row_table, store):
@@ -337,14 +357,14 @@
         row = pl.ds(half * 4 + index, 1)
         value = times((high[0, row, :], high[1, row, :]), (base[0], base[1]))
         for part in range(2):
-            row_table[index * 64 : index * 64 + 64, part * 1024 : part * 1024 + 1024] = value[part].astype(BF16)
+            row_table[part * 256 + index * 64 : part * 256 + index * 64 + 64, :] = value[part].astype(BF16)
     sign = jnp.where((iota((1, 128), 1) & 64) == 0, -1.0, 1.0)
     for pair in range(4):
         placed = jnp.concatenate(
-            [blocks[:, 2 * pair + part].reshape(1024, 128) for part in range(2)], axis=1
+            [blocks[(2 * pair + part) & 3, pair >> 1].reshape(1024, 128) for part in range(2)], axis=1
         )
-        straight = dot(row_table[:, :1024], placed)
-        crossed = dot(row_table[:, 1024:], placed)
+        both = dot(row_table[...], placed)
+        straight, crossed = both[:256], both[256:]
         for part in range(2):
             lanes = slice(part * 128, part * 128 + 128)
             value = straight[:, lanes] + pltpu.roll(crossed[:, lanes], 64, 1) * sign
@@ -369,7 +389,7 @@
         out_shape=jax.ShapeDtypeStruct((256, 1024), BF16),
         in_specs=[smem()] + [vmem()] * 3,
         out_specs=vmem(),
-        scratch_shapes=[pltpu.VMEM((256, 2048), BF16)],
+        scratch_shapes=[pltpu.VMEM((512, 1024), BF16)],
         compiler_params=pltpu.CompilerParams(vmem_limit_bytes=LIMIT),
         cost_estimate=pl.CostEstimate(flops=10**9, bytes_accessed=4 << 20, transcendentals=0),
         name="back_other",
@@ -405,7 +425,7 @@
         ],
         in_specs=[smem()] + [vmem()] * 6,
         out_specs=[vmem(), vmem()],
-        scratch_shapes=[pltpu.VMEM((256, 2048), BF16), pltpu.VMEM((256, 1024), BF16)],
+        scratch_shapes=[pltpu.VMEM((512, 1024), BF16), pltpu.VMEM((256, 1024), BF16)],
         compiler_params=pltpu.CompilerParams(vmem_limit_bytes=LIMIT),
         cost_estimate=pl.CostEstimate(flops=2 * 10**9, bytes_accessed=8 << 20, transcendentals=0),
         name="back_own",
@@ -415,11 +435,12 @@
 def finish_kernel(middle_ref, own_ref, col_ref, screen_ref, out_hbm, image, sems):
     leaving = []
     for chunk in range(2):
-        rows = slice(chunk * 128, chunk * 128 + 128)
-        value = screened(middle_ref[rows, :], col_ref[...], (screen_ref[0, rows, :], screen_ref[1, rows, :]))
+        lanes = slice(chunk * 256, chunk * 256 + 256)
+        facet = [dot(middle_ref[...], col_ref[:, part * 512 + chunk * 256 : part * 512 + chunk * 256 + 256]) for part in range(2)]
+        value = times(facet, [screen_ref[part, :, lanes].astype(F32) for part in range(2)])
         for part in range(2):
-            image[chunk, part] = own_ref[part, rows, :] + value[part]
-        copy = pltpu.make_async_copy(image.at[chunk], out_hbm.at[:, pl.ds(chunk * 128, 128)], sems.at[chunk])
+            image[chunk, part] = own_ref[part, :, lanes] + value[part]
+        copy = pltpu.make_async_copy(image.at[chunk], out_hbm.at[:, :, pl.ds(chunk * 256, 256)], sems.at[chunk])
         copy.start()
         leaving.append(copy)
     for copy in leaving:
@@ -432,7 +453,7 @@
         out_shape=jax.ShapeDtypeStruct((2, 256, 512), F32),
         in_specs=[vmem()] * 4,
         out_specs=hbm(),
-        scratch_shapes=[pltpu.VMEM((2, 2, 128, 512), F32), pltpu.SemaphoreType.DMA((2,))],
+        scratch_shapes=[pltpu.VMEM((2, 2, 256, 256), F32), pltpu.SemaphoreType.DMA((2,))],
         compiler_params=pltpu.CompilerParams(vmem_limit_bytes=LIMIT),
         cost_estimate=pl.CostEstimate(flops=10**9, bytes_accessed=8 << 20, transcendentals=0),
         name="finish",
@@ -444,7 +465,7 @@
 
 
 GROUPS = [
-    [position(x, 2 * k + l, y) for x in range(4) for l in range(2) for y in range(4)] for k in range(4)
+    [position(x, 2 * k + l, y) for y in range(4) for l in range(2) for x in range(4)] for k in range(4)
 ]
 
 
@@ -464,15 +485,16 @@
         block_counts,
         visibilities.reshape(2, 8, VB), kernels.reshape(2, 8, 8, VB), vis_offsets.reshape(2, 8, VB),
     )
+    offsets = jnp.concatenate([facet_rows, facet_cols, sub_rows, sub_cols])
     packs = [lax.ppermute(own, "sf", shifted(turn)) for turn in (1, 2, 3)]
-    facet_row_table, facet_col_table, begun = front_own(group, facet_rows, facet_cols, own)
-    outgoing = front_others(group, packs, facet_row_table, facet_col_table, begun)
+    facet_row_table, facet_col_table, own_sent = front_own(group, offsets, own)
+    outgoing = front_others(group, packs, facet_row_table, facet_col_table, own_sent)
     incoming = lax.all_to_all(
         outgoing, "sf", split_axis=0, concat_axis=0, tiled=True, axis_index_groups=GROUPS
     )
     layer = lax.axis_index("wa").reshape(1)
-    high, base, small, cell, own_screen, other_screen = tables(layer, sub_rows, sub_cols, layer_w, screen_n)
-    blocks = incoming.reshape(4, 8, 4, CON, 128)
+    high, base, small, cell, own_screen, other_screen = tables(layer, offsets, layer_w, screen_n)
+    blocks = incoming.reshape(4, 2, 4, 4, CON, 128)
     theirs = back_other(1 - layer, blocks, high, base)
     received = lax.ppermute(theirs, "wa", [(0, 1), (1, 0)])
     own_part, col_table = back_own(layer, blocks, high, base, small, cell, own_screen)

time: 71 us -> 68.6 us (0.966)
  waiting for transfers between devices: 22.8 us -> 21.3 us
  local copies, waits for them, and re-layouts: 6.8 us -> 5.47 us
  Pallas kernels: 17.8 us -> 16.8 us
  other arithmetic: 0 us -> 0.78 us
    all_to_all x1, waiting for transfers between devices: 22.8 us -> 21.3 us  [per_device(): lax.all_to_all(outgoing, 'sf', split_axis=0, concat_axis=0, tiled=True, a...]
    unnamed x24 -> x16, local copies, waits for them, and re-layouts: 6.8 us -> 5.47 us
    pallas_call x1, Pallas kernels: 6.62 us -> 5.77 us  [front_others(): pl.pallas_call(front_others_kernel, out_shape=jax.ShapeDtypeStruct((32, 4...]
    concatenate x0 -> x1, other arithmetic: none -> 0.78 us  [per_device(): offsets = jnp.concatenate([facet_rows, facet_cols, sub_rows, sub_cols])]
  transfers between devices with their start and end apart: 5 -> 5, of which waited for: 1 -> 1; matrix products, arithmetic and copies ran while one was open for 0% -> 1% of each run, Pallas kernels for 11% -> 12%
where the time goes in v4:
time: 68.6 us; the launch traced here: 68.2 us
  starting transfers between devices  22.9 us (33%)
  waiting for transfers between devices  21.3 us (31%)
  Pallas kernels  16.8 us (24%)
  local copies, waits for them, and re-layouts  5.47 us (8%)
  between operations  0.95 us (1%)
  other arithmetic  0.78 us (1%)
    all_to_all x1, waiting for transfers between devices, per_device(): lax.all_to_all(outgoing, 'sf', split_axis=0, concat_axis=0, tiled=True, a...  21.3 us
    ppermute x3, starting transfers between devices, per_device(): packs = [lax.ppermute(own, 'sf', shifted(turn)) for turn in (1, 2, 3)]  11.4 us
    all_to_all x1, starting transfers between devices, per_device(): lax.all_to_all(outgoing, 'sf', split_axis=0, concat_axis=0, tiled=True, a...  7.81 us
    pallas_call x1, Pallas kernels, front_others(): pl.pallas_call(front_others_kernel, out_shape=jax.ShapeDtypeStruct((32, 4...  5.77 us
    unnamed x16, local copies, waits for them, and re-layouts  5.47 us
    ppermute x1, starting transfers between devices, per_device(): received = lax.ppermute(theirs, 'wa', [(0, 1), (1, 0)])  3.67 us
    pallas_call x1, Pallas kernels, front_own(): pl.pallas_call(front_own_kernel, out_shape=[jax.ShapeDtypeStruct((512, 51...  3.47 us
    pallas_call x1, Pallas kernels, tables(): pl.pallas_call(tables_kernel, out_shape=[jax.ShapeDtypeStruct((2, 8, 1024...  2.38 us
  transfers between devices with their start and end apart: 5, of which 1 were waited for; matrix products, arithmetic and copies ran while one was open for 1% of the time, Pallas kernels for 12%

profile of v4, /device:TPU:1, one launch (start us, length us, event | category | flops | bytes accessed | tf_op | source)
XLA Modules:
  0.0 68.2 jit_solution(15550351946149894374)
XLA Ops:
  0.7 0.7 %copy-done.1 = bf16[2,8,1,1,8,128]{5,4,3,2,1,0:T(8,128)(2,1)S(1)} copy-done((bf16[2,8,1,1,8,128]{5,4,3,2,1,0:T(8,128)(2,1)S(1)}, bf16[2,8,1,1,8,128]{5,4,3,2,1,0:T(8,128)(2,1)}, u32[]{:S(2)}) %copy-start.1) | copy-done | bytes 32792
  1.4 0.7 %copy-done.2 = s32[2,1,1,8,128]{4,3,2,1,0:T(8,128)S(1)} copy-done((s32[2,1,1,8,128]{4,3,2,1,0:T(8,128)S(1)}, s32[2,1,1,8,128]{4,3,2,1,0:T(8,128)}, u32[]{:S(2)}) %copy-start.2) | copy-done | bytes 8216
  2.1 0.7 %copy-done.3 = bf16[2,1,1,8,128]{4,3,2,1,0:T(8,128)(2,1)S(1)} copy-done((bf16[2,1,1,8,128]{4,3,2,1,0:T(8,128)(2,1)S(1)}, bf16[2,1,1,8,128]{4,3,2,1,0:T(8,128)(2,1)}, u32[]{:S(2)}) %copy-start.3) | copy-done | bytes 4120
  2.8 0.1 pack.1.own_ref
  2.9 3.9 %collective-permute-start = (bf16[176,128]{1,0:T(8,128)(2,1)S(1)}, bf16[176,128]{1,0:T(8,128)(2,1)S(1)}, u32[]{:S(2)}, u32[]{:S(2)}) collective-permute-start(bf16[176,128]{1,0:T(8,128)(2,1)S(1)} %pack.1.own_ref), channel_id=1, source_target_pairs={{0,16},{2,18},{4,20},{6,22},{8,24},{10,26},{12,28},{14,30},{16,32}... | collective-permute-start | bytes 135176 | tf_op jit(solution)/shard_map/ppermute | solution.py:489
  6.8 5.1 %collective-permute-start.1 = (bf16[176,128]{1,0:T(8,128)(2,1)S(1)}, bf16[176,128]{1,0:T(8,128)(2,1)S(1)}, u32[]{:S(2)}, u32[]{:S(2)}) collective-permute-start(bf16[176,128]{1,0:T(8,128)(2,1)S(1)} %pack.1.own_ref), channel_id=1, source_target_pairs={{0,32},{2,34},{4,36},{6,38},{8,40},{10,42},{12,44},{14,46},{16,48}... | collective-permute-start | bytes 135176 | tf_op jit(solution)/shard_map/ppermute | solution.py:489
  11.9 2.4 %collective-permute-start.2 = (bf16[176,128]{1,0:T(8,128)(2,1)S(1)}, bf16[176,128]{1,0:T(8,128)(2,1)S(1)}, u32[]{:S(2)}, u32[]{:S(2)}) collective-permute-start(bf16[176,128]{1,0:T(8,128)(2,1)S(1)} %pack.1.own_ref), channel_id=1, source_target_pairs={{0,48},{2,50},{4,52},{6,54},{8,56},{10,58},{12,60},{14,62},{16,0},... | collective-permute-start | bytes 135176 | tf_op jit(solution)/shard_map/ppermute | solution.py:489
  14.3 0.8 %pad_add_fusion.offsets_ref = s32[48]{0:T(128)S(1)} fusion(s32[8]{0:T(128)} %param.15, s32[16]{0:T(128)} %param.14, s32[8]{0:T(128)} %param.17, s32[16]{0:T(128)} %param.16), kind=kLoop, calls=%fused_computation | loop fusion | flops 144 | bytes 384 | tf_op jit(solution)/shard_map/concatenate | solution.py:488
  15.0 3.5 %front_own.1 = (bf16[512,512]{1,0:T(8,128)(2,1)S(1)}, bf16[1024,1024]{1,0:T(8,128)(2,1)S(1)}, bf16[32,64,128]{2,1,0:T(8,128)(2,1)S(1)}) custom-call(s32[1]{0:T(128)} %bitcast.1.group_ref, s32[48]{0:T(128)S(1)} %pad_add_fusion.offsets_ref, bf16[176,128]{1,0:T(8,128)(2,1)S(1)} %pack.1.own_ref), custom_call_target="tpu_custom_call" | custom-call | flops 3000000000 | bytes 4194304 | tf_op jit(solution)/shard_map/front_own/pallas_call | solution.py:251
  18.5 0.0 collective-permute-done.first_ref
  18.5 0.0 collective-permute-done.1.second_ref
  18.6 5.8 %front_others.1 = bf16[32,4,64,128]{3,2,1,0:T(8,128)(2,1)S(1)} custom-call(s32[1]{0:T(128)} %bitcast.1.group_ref, bf16[176,128]{1,0:T(8,128)(2,1)S(1)} %collective-permute-done.first_ref, bf16[176,128]{1,0:T(8,128)(2,1)S(1)} %collective-permute-done.1.second_ref, bf16[176,128]{1,0:T(8,128)(2,1)S(1)} %collective-permute-done.2.third_ref, ...), custom_call_target="tpu_custom_call" | custom-call | flops 6000000000 | bytes 4194304 | tf_op jit(solution)/shard_map/front_others/pallas_call | solution.py:281
  24.3 1.3 %copy-done = bf16[32,4,64,128]{3,2,1,0:T(8,128)(2,1)} copy-done((bf16[32,4,64,128]{3,2,1,0:T(8,128)(2,1)}, bf16[32,4,64,128]{3,2,1,0:T(8,128)(2,1)S(1)}, u32[]{:S(2)}) %copy-start) | copy-done | bytes 2097176
  25.7 7.8 %all-to-all-start = ((bf16[32,4,64,128]{3,2,1,0:T(8,128)(2,1)}), bf16[32,4,64,128]{3,2,1,0:T(8,128)(2,1)S(1)}, u32[]{:S(2)}, u32[]{:S(2)}) async-start(bf16[32,4,64,128]{3,2,1,0:T(8,128)(2,1)} %copy-done), calls=%async_computation | async-start | bytes 4194304 | tf_op jit(solution)/shard_map/all_to_all | solution.py:492
  33.5 0.0 copy-start.4
  33.5 1.2 %copy-done.4 = f32[1,512,512]{2,1,0:T(8,128)S(1)} copy-done((f32[1,512,512]{2,1,0:T(8,128)S(1)}, f32[1,512,512]{2,1,0:T(8,128)}, u32[]{:S(2)}) %copy-start.4) | copy-done | bytes 1048600
  34.7 2.4 %tables.1 = (f32[2,8,1024]{2,1,0:T(8,128)S(1)}, f32[2,64,1024]{2,1,0:T(8,128)S(1)}, f32[2,8,512]{2,1,0:T(8,128)S(1)}, f32[2,64,512]{2,1,0:T(8,128)S(1)}, bf16[2,...) custom-call(s32[1]{0:T(128)} %bitcast.layer_ref.half_ref, s32[48]{0:T(128)S(1)} %pad_add_fusion.offsets_ref, ...), custom_call_target="tpu_custom_call" | custom-call | flops 1000000000 | bytes 8388608 | tf_op jit(solution)/shard_map/tables/pallas_call | solution.py:336
  37.1 0.0 copy-start.6
  37.1 0.8 %copy-done.6 = bf16[2,256,512]{2,1,0:T(8,128)(2,1)} copy-done((bf16[2,256,512]{2,1,0:T(8,128)(2,1)}, bf16[2,256,512]{2,1,0:T(8,128)(2,1)S(1)}, u32[]{:S(2)}) %copy-start.6) | copy-done | bytes 524312
  37.9 21.3 %all-to-all-done = bf16[32,4,64,128]{3,2,1,0:T(8,128)(2,1)S(1)} async-done(((bf16[32,4,64,128]{3,2,1,0:T(8,128)(2,1)}), bf16[32,4,64,128]{3,2,1,0:T(8,128)(2,1)S(1)}, u32[]{:S(2)}, u32[]{:S(2)}) %all-to-all-start) | async-done | bytes 2097184 | tf_op jit(solution)/shard_map/all_to_all | solution.py:492
  59.2 1.4 %back_other.1 = bf16[256,1024]{1,0:T(8,128)(2,1)S(1)} custom-call(s32[1]{0:T(128)S(6)} %sub.3.half_ref, bf16[4,2,4,4,64,128]{5,4,3,2,1,0:T(8,128)(2,1)S(1)} %bitcast.9, f32[2,8,1024]{2,1,0:T(8,128)S(1)} %get-tuple-element.19.high, f32[2,64,1024]{2,1,0:T(8,128)S(1)} %get-tuple-element.20.base), custom_call_target="tpu_custom_call" | custom-call | flops 1000000000 | bytes 4194304 | tf_op jit(solution)/shard_map/back_other/pallas_call | solution.py:387
  60.6 3.7 %collective-permute-start.3 = (bf16[256,1024]{1,0:T(8,128)(2,1)S(1)}, bf16[256,1024]{1,0:T(8,128)(2,1)S(1)}, u32[]{:S(2)}, u32[]{:S(2)}) collective-permute-start(bf16[256,1024]{1,0:T(8,128)(2,1)S(1)} %back_other.1), channel_id=1, source_target_pairs={{0,1},{1,0},{2,3},{3,2},{4,5},{5,4},{6,7},{7,6},{8,9},{9,8},{10,11... | collective-permute-start | bytes 1572872 | tf_op jit(solution)/shard_map/ppermute | solution.py:499
  64.3 2.1 %back_own.1 = (f32[2,256,512]{2,1,0:T(8,128)S(1)}, bf16[1024,1024]{1,0:T(8,128)(2,1)S(1)}) custom-call(s32[1]{0:T(128)} %bitcast.layer_ref.half_ref, bf16[4,2,4,4,64,128]{5,4,3,2,1,0:T(8,128)(2,1)S(1)} %bitcast.10, f32[2,8,1024]{2,1,0:T(8,128)S(1)} %get-tuple-element.19.high, f32[2,64,1024]{2,1,0:T(8,128)S(1)} %get-tuple-element.20.base, ...), custom_call_target="tpu_custom_call" | custom-call | flops 2000000000 | bytes 8388608 | tf_op jit(solution)/shard_map/back_own/pallas_call | solution.py:420
  66.4 1.6 %finish.1 = f32[2,256,512]{2,1,0:T(8,128)} custom-call(bf16[256,1024]{1,0:T(8,128)(2,1)S(1)} %collective-permute-done.3.middle_ref, f32[2,256,512]{2,1,0:T(8,128)S(1)} %get-tuple-element.24.own_ref, bf16[1024,1024]{1,0:T(8,128)(2,1)S(1)} %get-tuple-element.25.col_ref, bf16[2,256,512]{2,1,0:T(8,128)(2,1)S(1)} %get-tuple-element.26.screen_ref), custom_call_target="tpu_custom_call" | custom-call | flops 1000000000 | bytes 8388608 | tf_op jit(solution)/shard_map/finish/pallas_call | solution.py:451
  (10 shorter events, 0.0 us)
Async XLA Ops:
  0.7 0.8 %copy-start.1 = (bf16[2,8,1,1,8,128]{5,4,3,2,1,0:T(8,128)(2,1)S(1)}, bf16[2,8,1,1,8,128]{5,4,3,2,1,0:T(8,128)(2,1)}, u32[]{:S(2)}) copy-start(bf16[2,8,1,1,8,128]{5,4,3,2,1,0:T(8,128)(2,1)} %param.11) | copy-start | bytes 98308
  1.4 0.7 %copy-start.2 = (s32[2,1,1,8,128]{4,3,2,1,0:T(8,128)S(1)}, s32[2,1,1,8,128]{4,3,2,1,0:T(8,128)}, u32[]{:S(2)}) copy-start(s32[2,1,1,8,128]{4,3,2,1,0:T(8,128)} %param.12) | copy-start | bytes 24580
  2.1 0.7 %copy-start.3 = (bf16[2,1,1,8,128]{4,3,2,1,0:T(8,128)(2,1)S(1)}, bf16[2,1,1,8,128]{4,3,2,1,0:T(8,128)(2,1)}, u32[]{:S(2)}) copy-start(bf16[2,1,1,8,128]{4,3,2,1,0:T(8,128)(2,1)} %param.10) | copy-start | bytes 12292
  2.9 15.7 %collective-permute-start = (bf16[176,128]{1,0:T(8,128)(2,1)S(1)}, bf16[176,128]{1,0:T(8,128)(2,1)S(1)}, u32[]{:S(2)}, u32[]{:S(2)}) collective-permute-start(bf16[176,128]{1,0:T(8,128)(2,1)S(1)} %pack.1.own_ref), channel_id=1, source_target_pairs={{0,16},{2,18},{4,20},{6,22},{8,24},{10,26},{12,28},{14,30},{16,32}... | collective-permute-start | bytes 135176 | tf_op jit(solution)/shard_map/ppermute | solution.py:489
  6.8 11.8 %collective-permute-start.1 = (bf16[176,128]{1,0:T(8,128)(2,1)S(1)}, bf16[176,128]{1,0:T(8,128)(2,1)S(1)}, u32[]{:S(2)}, u32[]{:S(2)}) collective-permute-start(bf16[176,128]{1,0:T(8,128)(2,1)S(1)} %pack.1.own_ref), channel_id=1, source_target_pairs={{0,32},{2,34},{4,36},{6,38},{8,40},{10,42},{12,44},{14,46},{16,48}... | collective-permute-start | bytes 135176 | tf_op jit(solution)/shard_map/ppermute | solution.py:489
  11.9 6.7 %collective-permute-start.2 = (bf16[176,128]{1,0:T(8,128)(2,1)S(1)}, bf16[176,128]{1,0:T(8,128)(2,1)S(1)}, u32[]{:S(2)}, u32[]{:S(2)}) collective-permute-start(bf16[176,128]{1,0:T(8,128)(2,1)S(1)} %pack.1.own_ref), channel_id=1, source_target_pairs={{0,48},{2,50},{4,52},{6,54},{8,56},{10,58},{12,60},{14,62},{16,0},... | collective-permute-start | bytes 135176 | tf_op jit(solution)/shard_map/ppermute | solution.py:489
  24.3 1.3 %copy-start = (bf16[32,4,64,128]{3,2,1,0:T(8,128)(2,1)}, bf16[32,4,64,128]{3,2,1,0:T(8,128)(2,1)S(1)}, u32[]{:S(2)}) copy-start(bf16[32,4,64,128]{3,2,1,0:T(8,128)(2,1)S(1)} %front_others.1) | copy-start | bytes 6291460
  25.7 7.8 %copy-start.5 = (f32[2]{0:T(128)S(1)}, f32[2]{0:T(128)}, u32[]{:S(2)}) copy-start(f32[2]{0:T(128)} %weights_ref.1) | copy-start | bytes 28
  25.7 33.6 %all-to-all-start = ((bf16[32,4,64,128]{3,2,1,0:T(8,128)(2,1)}), bf16[32,4,64,128]{3,2,1,0:T(8,128)(2,1)S(1)}, u32[]{:S(2)}, u32[]{:S(2)}) async-start(bf16[32,4,64,128]{3,2,1,0:T(8,128)(2,1)} %copy-done), calls=%async_computation | async-start | bytes 4194304 | tf_op jit(solution)/shard_map/all_to_all | solution.py:492
  33.5 1.2 %copy-start.4 = (f32[1,512,512]{2,1,0:T(8,128)S(1)}, f32[1,512,512]{2,1,0:T(8,128)}, u32[]{:S(2)}) copy-start(f32[1,512,512]{2,1,0:T(8,128)} %screen_hbm.1) | copy-start | bytes 3145732
  37.1 0.8 %copy-start.6 = (bf16[2,256,512]{2,1,0:T(8,128)(2,1)}, bf16[2,256,512]{2,1,0:T(8,128)(2,1)S(1)}, u32[]{:S(2)}) copy-start(bf16[2,256,512]{2,1,0:T(8,128)(2,1)S(1)} %get-tuple-element.23.screen) | copy-start | bytes 1572868
  59.2 5.1 %copy-start.7 = (bf16[2,256,512]{2,1,0:T(8,128)(2,1)S(1)}, bf16[2,256,512]{2,1,0:T(8,128)(2,1)}, u32[]{:S(2)}) copy-start(bf16[2,256,512]{2,1,0:T(8,128)(2,1)} %copy-done.6) | copy-start | bytes 1572868
  60.6 5.8 %collective-permute-start.3 = (bf16[256,1024]{1,0:T(8,128)(2,1)S(1)}, bf16[256,1024]{1,0:T(8,128)(2,1)S(1)}, u32[]{:S(2)}, u32[]{:S(2)}) collective-permute-start(bf16[256,1024]{1,0:T(8,128)(2,1)S(1)} %back_other.1), channel_id=1, source_target_pairs={{0,1},{1,0},{2,3},{3,2},{4,5},{5,4},{6,7},{7,6},{8,9},{9,8},{10,11... | collective-permute-start | bytes 1572872 | tf_op jit(solution)/shard_map/ppermute | solution.py:499

commit v5 on v4

--- a/solution.py
+++ b/solution.py
@@ -116,36 +116,45 @@
     return copies
 
 
-def pack_kernel(counts, vis, kernels, all_offsets, out_ref):
+def pack_kernel(counts, inputs, out_ref):
     live = counts[0, 0]
     slot = iota((8, 128), 0)
-    samples = [jnp.where(slot < live, vis[part].astype(F32), 0.0) for part in range(2)]
+    vis = inputs[0:16, :].astype(F32)
+    kernels = inputs[16:144, :].astype(F32)
+    high = inputs[144:160, :].astype(F32)
+    low = inputs[160:176, :].astype(F32)
+    samples = [jnp.where(slot < live, vis[part * 8 : part * 8 + 8], 0.0) for part in range(2)]
     out_ref[0:16, :] = jnp.concatenate(samples, axis=0).astype(BF16)
     for axis in range(2):
-        offsets = all_offsets[axis]
-        low = offsets & 7
-        digits = jnp.concatenate([(offsets >> 3).astype(F32), low.astype(F32)], axis=0)
+        rows = slice(axis * 8, axis * 8 + 8)
+        digits = jnp.concatenate([high[rows], low[rows]], axis=0)
         out_ref[16 + axis * 16 : 32 + axis * 16, :] = digits.astype(BF16)
         turned = []
         for block in range(8):
-            shift = (slot - low[block : block + 1, :]) & 7
+            shift = (slot - low[axis * 8 + block : axis * 8 + block + 1, :].astype(jnp.int32)) & 7
             values = jnp.zeros((8, VB), F32)
             for column in range(8):
-                entry = kernels[axis, column, block : block + 1, :].astype(F32)
-                values = jnp.where(shift == column, entry, values)
+                row = axis * 64 + column * 8 + block
+                values = jnp.where(shift == column, kernels[row : row + 1, :], values)
             turned.append(values)
         out_ref[48 + axis * 64 : 112 + axis * 64, :] = jnp.concatenate(turned, axis=0).astype(BF16)
 
 
 def pack(counts, vis, kernels, offsets):
+    inputs = jnp.concatenate(
+        [
+            vis.reshape(16, VB), kernels.reshape(128, VB),
+            (offsets >> 3).astype(BF16).reshape(16, VB), (offsets & 7).astype(BF16).reshape(16, VB),
+        ]
+    )
     return pl.pallas_call(
         pack_kernel,
         out_shape=jax.ShapeDtypeStruct((176, 128), BF16),
-        in_specs=[smem()] + [vmem()] * 3,
+        in_specs=[smem(), vmem()],
         out_specs=vmem(),
         compiler_params=pltpu.CompilerParams(vmem_limit_bytes=LIMIT),
         name="pack",
-    )(counts, vis, kernels, offsets)
+    )(counts, inputs)
 
 
 def lane_table(offsets_ref, count, width, lead, out_ref, place):
@@ -187,7 +196,7 @@
 
 
 def peer(row, column):
-    return (column & 3) * 8 + (column >> 2) * 4 + row
+    return (column >> 2) * 16 + (column & 3) * 4 + row * 1
 
 
 def grid_slots(refs, row_table, col_table, spread, turned, halves, store):
@@ -361,7 +370,7 @@
     sign = jnp.where((iota((1, 128), 1) & 64) == 0, -1.0, 1.0)
     for pair in range(4):
         placed = jnp.concatenate(
-            [blocks[(2 * pair + part) & 3, pair >> 1].reshape(1024, 128) for part in range(2)], axis=1
+            [blocks[pair >> 1, (2 * pair + part) & 3, :].reshape(1024, 128) for part in range(2)], axis=1
         )
         both = dot(row_table[...], placed)
         straight, crossed = both[:256], both[256:]
@@ -465,7 +474,7 @@
 
 
 GROUPS = [
-    [position(x, 2 * k + l, y) for y in range(4) for l in range(2) for x in range(4)] for k in range(4)
+    [position(x, 2 * k + l, y) for l in range(2) for y in range(4) for x in range(4)] for k in range(4)
 ]
 
 
@@ -494,7 +503,7 @@
     )
     layer = lax.axis_index("wa").reshape(1)
     high, base, small, cell, own_screen, other_screen = tables(layer, offsets, layer_w, screen_n)
-    blocks = incoming.reshape(4, 2, 4, 4, CON, 128)
+    blocks = incoming.reshape(2, 4, 4, 4, CON, 128)
     theirs = back_other(1 - layer, blocks, high, base)
     received = lax.ppermute(theirs, "wa", [(0, 1), (1, 0)])
     own_part, col_table = back_own(layer, blocks, high, base, small, cell, own_screen)

time: 68.6 us -> 67.7 us (0.987)
  local copies, waits for them, and re-layouts: 5.47 us -> 3.35 us
  other arithmetic: 0.78 us -> 2.25 us
  waiting for transfers between devices: 21.3 us -> 20 us
  starting transfers between devices: 22.9 us -> 24 us
    unnamed x16 -> x10, local copies, waits for them, and re-layouts: 5.47 us -> 3.35 us
    all_to_all x1, waiting for transfers between devices: 21.3 us -> 20 us  [per_device(): lax.all_to_all(outgoing, 'sf', split_axis=0, concat_axis=0, tiled=True, a...]
    ppermute x1, starting transfers between devices: 3.67 us -> 4.82 us  [per_device(): received = lax.ppermute(theirs, 'wa', [(0, 1), (1, 0)])]
    concatenate x0 -> x1, other arithmetic: none -> 0.77 us  [pack(): jnp.concatenate([vis.reshape(16, VB), kernels.reshape(128, VB), (offsets...]
    convert_element_type x0 -> x1, other arithmetic: none -> 0.7 us  [pack(): (offsets >> 3).astype(BF16).reshape(16, VB)]
where the time goes in v5:
time: 67.7 us; the launch traced here: 67.4 us
  starting transfers between devices  24 us (35%)
  waiting for transfers between devices  20 us (30%)
  Pallas kernels  16.8 us (25%)
  local copies, waits for them, and re-layouts  3.35 us (5%)
  other arithmetic  2.25 us (3%)
  between operations  0.94 us (1%)
    all_to_all x1, waiting for transfers between devices, per_device(): lax.all_to_all(outgoing, 'sf', split_axis=0, concat_axis=0, tiled=True, a...  20 us
    ppermute x3, starting transfers between devices, per_device(): packs = [lax.ppermute(own, 'sf', shifted(turn)) for turn in (1, 2, 3)]  11.4 us
    all_to_all x1, starting transfers between devices, per_device(): lax.all_to_all(outgoing, 'sf', split_axis=0, concat_axis=0, tiled=True, a...  7.8 us
    pallas_call x1, Pallas kernels, front_others(): pl.pallas_call(front_others_kernel, out_shape=jax.ShapeDtypeStruct((32, 4...  5.77 us
    ppermute x1, starting transfers between devices, per_device(): received = lax.ppermute(theirs, 'wa', [(0, 1), (1, 0)])  4.82 us
    pallas_call x1, Pallas kernels, front_own(): pl.pallas_call(front_own_kernel, out_shape=[jax.ShapeDtypeStruct((512, 51...  3.47 us
    unnamed x10, local copies, waits for them, and re-layouts  3.35 us
    pallas_call x1, Pallas kernels, tables(): pl.pallas_call(tables_kernel, out_shape=[jax.ShapeDtypeStruct((2, 8, 1024...  2.38 us
  transfers between devices with their start and end apart: 5, of which 1 were waited for; matrix products, arithmetic and copies ran while one was open for 1% of the time, Pallas kernels for 12%

profile of v5, /device:TPU:1, one launch (start us, length us, event | category | flops | bytes accessed | tf_op | source)
XLA Modules:
  0.0 67.4 jit_solution(470156118788240786)
XLA Ops:
  0.0 0.7 %fusion = (bf16[16,128]{1,0:T(8,128)(2,1)S(1)}, bf16[16,128]{1,0:T(8,128)(2,1)S(1)}) fusion(s32[2,1,1,8,128]{4,3,2,1,0:T(8,128)} %param.12), kind=kLoop, calls=%fused_computation.3 | loop fusion | flops 8192 | bytes 16384 | tf_op jit(solution)/shard_map/convert_element_type | solution.py:147
  1.4 0.8 %pad_maximum_fusion.inputs = bf16[176,128]{1,0:T(8,128)(2,1)S(1)} fusion(bf16[16,128]{1,0:T(8,128)(2,1)S(1)} %get-tuple-element.28, bf16[16,128]{1,0:T(8,128)(2,1)S(1)} %get-tuple-element.27, bf16[128,128]{1,0:T(8,128)(2,1)} %bitcast.14, bf16[16,128]{1,0:T(8,128)(2,1)} %bitcast.15), kind=kLoop, calls=%fused_computation | loop fusion | flops 180224 | bytes 90112 | tf_op jit(solution)/shard_map/concatenate | solution.py:144
  2.1 0.1 pack.1.own_ref
  2.2 3.9 %collective-permute-start = (bf16[176,128]{1,0:T(8,128)(2,1)S(1)}, bf16[176,128]{1,0:T(8,128)(2,1)S(1)}, u32[]{:S(2)}, u32[]{:S(2)}) collective-permute-start(bf16[176,128]{1,0:T(8,128)(2,1)S(1)} %pack.1.own_ref), channel_id=1, source_target_pairs={{0,16},{2,18},{4,20},{6,22},{8,24},{10,26},{12,28},{14,30},{16,32}... | collective-permute-start | bytes 135176 | tf_op jit(solution)/shard_map/ppermute | solution.py:498
  6.1 5.1 %collective-permute-start.1 = (bf16[176,128]{1,0:T(8,128)(2,1)S(1)}, bf16[176,128]{1,0:T(8,128)(2,1)S(1)}, u32[]{:S(2)}, u32[]{:S(2)}) collective-permute-start(bf16[176,128]{1,0:T(8,128)(2,1)S(1)} %pack.1.own_ref), channel_id=1, source_target_pairs={{0,32},{2,34},{4,36},{6,38},{8,40},{10,42},{12,44},{14,46},{16,48}... | collective-permute-start | bytes 135176 | tf_op jit(solution)/shard_map/ppermute | solution.py:498
  11.2 2.4 %collective-permute-start.2 = (bf16[176,128]{1,0:T(8,128)(2,1)S(1)}, bf16[176,128]{1,0:T(8,128)(2,1)S(1)}, u32[]{:S(2)}, u32[]{:S(2)}) collective-permute-start(bf16[176,128]{1,0:T(8,128)(2,1)S(1)} %pack.1.own_ref), channel_id=1, source_target_pairs={{0,48},{2,50},{4,52},{6,54},{8,56},{10,58},{12,60},{14,62},{16,0},... | collective-permute-start | bytes 135176 | tf_op jit(solution)/shard_map/ppermute | solution.py:498
  13.6 0.8 %pad_add_fusion.offsets_ref = s32[48]{0:T(128)S(1)} fusion(s32[8]{0:T(128)} %param.15, s32[16]{0:T(128)} %param.14, s32[8]{0:T(128)} %param.17, s32[16]{0:T(128)} %param.16), kind=kLoop, calls=%fused_computation.5 | loop fusion | flops 144 | bytes 384 | tf_op jit(solution)/shard_map/concatenate | solution.py:497
  14.4 3.5 %front_own.1 = (bf16[512,512]{1,0:T(8,128)(2,1)S(1)}, bf16[1024,1024]{1,0:T(8,128)(2,1)S(1)}, bf16[32,64,128]{2,1,0:T(8,128)(2,1)S(1)}) custom-call(s32[1]{0:T(128)} %bitcast.1.group_ref, s32[48]{0:T(128)S(1)} %pad_add_fusion.offsets_ref, bf16[176,128]{1,0:T(8,128)(2,1)S(1)} %pack.1.own_ref), custom_call_target="tpu_custom_call" | custom-call | flops 3000000000 | bytes 4194304 | tf_op jit(solution)/shard_map/front_own/pallas_call | solution.py:260
  17.8 0.0 collective-permute-done.first_ref
  17.9 0.0 collective-permute-done.1.second_ref
  17.9 0.0 collective-permute-done.2.third_ref
  17.9 5.8 %front_others.1 = bf16[32,4,64,128]{3,2,1,0:T(8,128)(2,1)S(1)} custom-call(s32[1]{0:T(128)} %bitcast.1.group_ref, bf16[176,128]{1,0:T(8,128)(2,1)S(1)} %collective-permute-done.first_ref, bf16[176,128]{1,0:T(8,128)(2,1)S(1)} %collective-permute-done.1.second_ref, bf16[176,128]{1,0:T(8,128)(2,1)S(1)} %collective-permute-done.2.third_ref, ...), custom_call_target="tpu_custom_call" | custom-call | flops 6000000000 | bytes 4194304 | tf_op jit(solution)/shard_map/front_others/pallas_call | solution.py:290
  23.7 1.3 %copy-done = bf16[32,4,64,128]{3,2,1,0:T(8,128)(2,1)} copy-done((bf16[32,4,64,128]{3,2,1,0:T(8,128)(2,1)}, bf16[32,4,64,128]{3,2,1,0:T(8,128)(2,1)S(1)}, u32[]{:S(2)}) %copy-start) | copy-done | bytes 2097176
  25.0 7.8 %all-to-all-start = ((bf16[32,4,64,128]{3,2,1,0:T(8,128)(2,1)}), bf16[32,4,64,128]{3,2,1,0:T(8,128)(2,1)S(1)}, u32[]{:S(2)}, u32[]{:S(2)}) async-start(bf16[32,4,64,128]{3,2,1,0:T(8,128)(2,1)} %copy-done), calls=%async_computation | async-start | bytes 4194304 | tf_op jit(solution)/shard_map/all_to_all | solution.py:501
  32.8 0.0 copy-start.1
  32.8 1.2 %copy-done.1 = f32[1,512,512]{2,1,0:T(8,128)S(1)} copy-done((f32[1,512,512]{2,1,0:T(8,128)S(1)}, f32[1,512,512]{2,1,0:T(8,128)}, u32[]{:S(2)}) %copy-start.1) | copy-done | bytes 1048600
  34.0 2.4 %tables.1 = (f32[2,8,1024]{2,1,0:T(8,128)S(1)}, f32[2,64,1024]{2,1,0:T(8,128)S(1)}, f32[2,8,512]{2,1,0:T(8,128)S(1)}, f32[2,64,512]{2,1,0:T(8,128)S(1)}, bf16[2,...) custom-call(s32[1]{0:T(128)} %bitcast.layer_ref.half_ref, s32[48]{0:T(128)S(1)} %pad_add_fusion.offsets_ref, ...), custom_call_target="tpu_custom_call" | custom-call | flops 1000000000 | bytes 8388608 | tf_op jit(solution)/shard_map/tables/pallas_call | solution.py:345
  36.4 0.0 copy-start.3
  36.4 0.8 %copy-done.3 = bf16[2,256,512]{2,1,0:T(8,128)(2,1)} copy-done((bf16[2,256,512]{2,1,0:T(8,128)(2,1)}, bf16[2,256,512]{2,1,0:T(8,128)(2,1)S(1)}, u32[]{:S(2)}) %copy-start.3) | copy-done | bytes 524312
  37.2 20.0 %all-to-all-done = bf16[32,4,64,128]{3,2,1,0:T(8,128)(2,1)S(1)} async-done(((bf16[32,4,64,128]{3,2,1,0:T(8,128)(2,1)}), bf16[32,4,64,128]{3,2,1,0:T(8,128)(2,1)S(1)}, u32[]{:S(2)}, u32[]{:S(2)}) %all-to-all-start) | async-done | bytes 2097184 | tf_op jit(solution)/shard_map/all_to_all | solution.py:501
  57.3 1.4 %back_other.1 = bf16[256,1024]{1,0:T(8,128)(2,1)S(1)} custom-call(s32[1]{0:T(128)S(6)} %sub.3.half_ref, bf16[2,4,4,4,64,128]{5,4,3,2,1,0:T(8,128)(2,1)S(1)} %bitcast.12, f32[2,8,1024]{2,1,0:T(8,128)S(1)} %get-tuple-element.19.high, f32[2,64,1024]{2,1,0:T(8,128)S(1)} %get-tuple-element.20.base), custom_call_target="tpu_custom_call" | custom-call | flops 1000000000 | bytes 4194304 | tf_op jit(solution)/shard_map/back_other/pallas_call | solution.py:396
  58.7 4.8 %collective-permute-start.3 = (bf16[256,1024]{1,0:T(8,128)(2,1)S(1)}, bf16[256,1024]{1,0:T(8,128)(2,1)S(1)}, u32[]{:S(2)}, u32[]{:S(2)}) collective-permute-start(bf16[256,1024]{1,0:T(8,128)(2,1)S(1)} %back_other.1), channel_id=1, source_target_pairs={{0,1},{1,0},{2,3},{3,2},{4,5},{5,4},{6,7},{7,6},{8,9},{9,8},{10,11... | collective-permute-start | bytes 1572872 | tf_op jit(solution)/shard_map/ppermute | solution.py:508
  63.5 2.1 %back_own.1 = (f32[2,256,512]{2,1,0:T(8,128)S(1)}, bf16[1024,1024]{1,0:T(8,128)(2,1)S(1)}) custom-call(s32[1]{0:T(128)} %bitcast.layer_ref.half_ref, bf16[2,4,4,4,64,128]{5,4,3,2,1,0:T(8,128)(2,1)S(1)} %bitcast.13, f32[2,8,1024]{2,1,0:T(8,128)S(1)} %get-tuple-element.19.high, f32[2,64,1024]{2,1,0:T(8,128)S(1)} %get-tuple-element.20.base, ...), custom_call_target="tpu_custom_call" | custom-call | flops 2000000000 | bytes 8388608 | tf_op jit(solution)/shard_map/back_own/pallas_call | solution.py:429
  65.6 1.6 %finish.1 = f32[2,256,512]{2,1,0:T(8,128)} custom-call(bf16[256,1024]{1,0:T(8,128)(2,1)S(1)} %collective-permute-done.3.middle_ref, f32[2,256,512]{2,1,0:T(8,128)S(1)} %get-tuple-element.24.own_ref, bf16[1024,1024]{1,0:T(8,128)(2,1)S(1)} %get-tuple-element.25.col_ref, bf16[2,256,512]{2,1,0:T(8,128)(2,1)S(1)} %get-tuple-element.26.screen_ref), custom_call_target="tpu_custom_call" | custom-call | flops 1000000000 | bytes 8388608 | tf_op jit(solution)/shard_map/finish/pallas_call | solution.py:460
  (6 shorter events, 0.0 us)
Async XLA Ops:
  2.2 15.7 %collective-permute-start = (bf16[176,128]{1,0:T(8,128)(2,1)S(1)}, bf16[176,128]{1,0:T(8,128)(2,1)S(1)}, u32[]{:S(2)}, u32[]{:S(2)}) collective-permute-start(bf16[176,128]{1,0:T(8,128)(2,1)S(1)} %pack.1.own_ref), channel_id=1, source_target_pairs={{0,16},{2,18},{4,20},{6,22},{8,24},{10,26},{12,28},{14,30},{16,32}... | collective-permute-start | bytes 135176 | tf_op jit(solution)/shard_map/ppermute | solution.py:498
  6.1 11.8 %collective-permute-start.1 = (bf16[176,128]{1,0:T(8,128)(2,1)S(1)}, bf16[176,128]{1,0:T(8,128)(2,1)S(1)}, u32[]{:S(2)}, u32[]{:S(2)}) collective-permute-start(bf16[176,128]{1,0:T(8,128)(2,1)S(1)} %pack.1.own_ref), channel_id=1, source_target_pairs={{0,32},{2,34},{4,36},{6,38},{8,40},{10,42},{12,44},{14,46},{16,48}... | collective-permute-start | bytes 135176 | tf_op jit(solution)/shard_map/ppermute | solution.py:498
  11.2 6.7 %collective-permute-start.2 = (bf16[176,128]{1,0:T(8,128)(2,1)S(1)}, bf16[176,128]{1,0:T(8,128)(2,1)S(1)}, u32[]{:S(2)}, u32[]{:S(2)}) collective-permute-start(bf16[176,128]{1,0:T(8,128)(2,1)S(1)} %pack.1.own_ref), channel_id=1, source_target_pairs={{0,48},{2,50},{4,52},{6,54},{8,56},{10,58},{12,60},{14,62},{16,0},... | collective-permute-start | bytes 135176 | tf_op jit(solution)/shard_map/ppermute | solution.py:498
  23.7 1.3 %copy-start = (bf16[32,4,64,128]{3,2,1,0:T(8,128)(2,1)}, bf16[32,4,64,128]{3,2,1,0:T(8,128)(2,1)S(1)}, u32[]{:S(2)}) copy-start(bf16[32,4,64,128]{3,2,1,0:T(8,128)(2,1)S(1)} %front_others.1) | copy-start | bytes 6291460
  25.0 7.8 %copy-start.2 = (f32[2]{0:T(128)S(1)}, f32[2]{0:T(128)}, u32[]{:S(2)}) copy-start(f32[2]{0:T(128)} %weights_ref.1) | copy-start | bytes 28
  25.0 32.3 %all-to-all-start = ((bf16[32,4,64,128]{3,2,1,0:T(8,128)(2,1)}), bf16[32,4,64,128]{3,2,1,0:T(8,128)(2,1)S(1)}, u32[]{:S(2)}, u32[]{:S(2)}) async-start(bf16[32,4,64,128]{3,2,1,0:T(8,128)(2,1)} %copy-done), calls=%async_computation | async-start | bytes 4194304 | tf_op jit(solution)/shard_map/all_to_all | solution.py:501
  32.8 1.2 %copy-start.1 = (f32[1,512,512]{2,1,0:T(8,128)S(1)}, f32[1,512,512]{2,1,0:T(8,128)}, u32[]{:S(2)}) copy-start(f32[1,512,512]{2,1,0:T(8,128)} %screen_hbm.1) | copy-start | bytes 3145732
  36.4 0.8 %copy-start.3 = (bf16[2,256,512]{2,1,0:T(8,128)(2,1)}, bf16[2,256,512]{2,1,0:T(8,128)(2,1)S(1)}, u32[]{:S(2)}) copy-start(bf16[2,256,512]{2,1,0:T(8,128)(2,1)S(1)} %get-tuple-element.23.screen) | copy-start | bytes 1572868
  57.3 6.2 %copy-start.4 = (bf16[2,256,512]{2,1,0:T(8,128)(2,1)S(1)}, bf16[2,256,512]{2,1,0:T(8,128)(2,1)}, u32[]{:S(2)}) copy-start(bf16[2,256,512]{2,1,0:T(8,128)(2,1)} %copy-done.3) | copy-start | bytes 1572868
  58.7 7.0 %collective-permute-start.3 = (bf16[256,1024]{1,0:T(8,128)(2,1)S(1)}, bf16[256,1024]{1,0:T(8,128)(2,1)S(1)}, u32[]{:S(2)}, u32[]{:S(2)}) collective-permute-start(bf16[256,1024]{1,0:T(8,128)(2,1)S(1)} %back_other.1), channel_id=1, source_target_pairs={{0,1},{1,0},{2,3},{3,2},{4,5},{5,4},{6,7},{7,6},{8,9},{9,8},{10,11... | collective-permute-start | bytes 1572872 | tf_op jit(solution)/shard_map/ppermute | solution.py:508

commit v6 on v5

--- a/solution.py
+++ b/solution.py
@@ -495,7 +495,8 @@
         visibilities.reshape(2, 8, VB), kernels.reshape(2, 8, 8, VB), vis_offsets.reshape(2, 8, VB),
     )
     offsets = jnp.concatenate([facet_rows, facet_cols, sub_rows, sub_cols])
-    packs = [lax.ppermute(own, "sf", shifted(turn)) for turn in (1, 2, 3)]
+    first, third = (lax.ppermute(own, "sf", shifted(turn)) for turn in (1, 3))
+    packs = [first, lax.ppermute(first, "sf", shifted(1)), third]
     facet_row_table, facet_col_table, own_sent = front_own(group, offsets, own)
     outgoing = front_others(group, packs, facet_row_table, facet_col_table, own_sent)
     incoming = lax.all_to_all(

time: 67.7 us -> 65.5 us (0.968)
  starting transfers between devices: 24 us -> 21.5 us
    ppermute x3, starting transfers between devices: 11.4 us -> 7.84 us  [the longest x2 7.02 us: per_device(): first, third = (lax.ppermute(own, 'sf', shifted(turn)) for turn in (1, 3))]
    ppermute x3, waiting for transfers between devices: 0.01 us -> 1.32 us  [the longest x1 0.7 us: per_device(): packs = [first, lax.ppermute(first, 'sf', shifted(1)), third]]
    ppermute x1, starting transfers between devices: 4.82 us -> 5.84 us  [per_device(): received = lax.ppermute(theirs, 'wa', [(0, 1), (1, 0)])]
    all_to_all x1, waiting for transfers between devices: 20 us -> 19.1 us  [per_device(): lax.all_to_all(outgoing, 'sf', split_axis=0, concat_axis=0, tiled=True, a...]
  transfers between devices with their start and end apart: 5 -> 5, of which waited for: 1 -> 3; matrix products, arithmetic and copies ran while one was open for 1% -> 1% of each run, Pallas kernels for 12% -> 12%
where the time goes in v6:
time: 65.5 us; the launch traced here: 65.2 us
  starting transfers between devices  21.5 us (33%)
  waiting for transfers between devices  20.4 us (31%)
  Pallas kernels  16.8 us (26%)
  local copies, waits for them, and re-layouts  3.35 us (5%)
  other arithmetic  2.25 us (3%)
  between operations  0.92 us (1%)
    all_to_all x1, waiting for transfers between devices, per_device(): lax.all_to_all(outgoing, 'sf', split_axis=0, concat_axis=0, tiled=True, a...  19.1 us
    all_to_all x1, starting transfers between devices, per_device(): lax.all_to_all(outgoing, 'sf', split_axis=0, concat_axis=0, tiled=True, a...  7.8 us
    ppermute x2, starting transfers between devices, per_device(): first, third = (lax.ppermute(own, 'sf', shifted(turn)) for turn in (1, 3))  7.02 us
    ppermute x1, starting transfers between devices, per_device(): received = lax.ppermute(theirs, 'wa', [(0, 1), (1, 0)])  5.84 us
    pallas_call x1, Pallas kernels, front_others(): pl.pallas_call(front_others_kernel, out_shape=jax.ShapeDtypeStruct((32, 4...  5.76 us
    pallas_call x1, Pallas kernels, front_own(): pl.pallas_call(front_own_kernel, out_shape=[jax.ShapeDtypeStruct((512, 51...  3.47 us
    unnamed x10, local copies, waits for them, and re-layouts  3.35 us
    pallas_call x1, Pallas kernels, tables(): pl.pallas_call(tables_kernel, out_shape=[jax.ShapeDtypeStruct((2, 8, 1024...  2.38 us
  transfers between devices with their start and end apart: 5, of which 3 were waited for; matrix products, arithmetic and copies ran while one was open for 1% of the time, Pallas kernels for 12%

profile of v6, /device:TPU:1, one launch (start us, length us, event | category | flops | bytes accessed | tf_op | source)
XLA Modules:
  0.0 65.2 jit_solution(6719987508374862576)
XLA Ops:
  0.0 0.7 %fusion = (bf16[16,128]{1,0:T(8,128)(2,1)S(1)}, bf16[16,128]{1,0:T(8,128)(2,1)S(1)}) fusion(s32[2,1,1,8,128]{4,3,2,1,0:T(8,128)} %param.12), kind=kLoop, calls=%fused_computation.3 | loop fusion | flops 8192 | bytes 16384 | tf_op jit(solution)/shard_map/convert_element_type | solution.py:147
  1.4 0.8 %pad_maximum_fusion.inputs = bf16[176,128]{1,0:T(8,128)(2,1)S(1)} fusion(bf16[16,128]{1,0:T(8,128)(2,1)S(1)} %get-tuple-element.28, bf16[16,128]{1,0:T(8,128)(2,1)S(1)} %get-tuple-element.27, bf16[128,128]{1,0:T(8,128)(2,1)} %bitcast.14, bf16[16,128]{1,0:T(8,128)(2,1)} %bitcast.15), kind=kLoop, calls=%fused_computation | loop fusion | flops 180224 | bytes 90112 | tf_op jit(solution)/shard_map/concatenate | solution.py:144
  2.1 0.1 pack.1.own_ref
  2.2 3.9 %collective-permute-start = (bf16[176,128]{1,0:T(8,128)(2,1)S(1)}, bf16[176,128]{1,0:T(8,128)(2,1)S(1)}, u32[]{:S(2)}, u32[]{:S(2)}) collective-permute-start(bf16[176,128]{1,0:T(8,128)(2,1)S(1)} %pack.1.own_ref), channel_id=1, source_target_pairs={{0,16},{2,18},{4,20},{6,22},{8,24},{10,26},{12,28},{14,30},{16,32}... | collective-permute-start | bytes 135176 | tf_op jit(solution)/shard_map/ppermute | solution.py:498
  6.1 3.1 %collective-permute-start.2 = (bf16[176,128]{1,0:T(8,128)(2,1)S(1)}, bf16[176,128]{1,0:T(8,128)(2,1)S(1)}, u32[]{:S(2)}, u32[]{:S(2)}) collective-permute-start(bf16[176,128]{1,0:T(8,128)(2,1)S(1)} %pack.1.own_ref), channel_id=1, source_target_pairs={{0,48},{2,50},{4,52},{6,54},{8,56},{10,58},{12,60},{14,62},{16,0},... | collective-permute-start | bytes 135176 | tf_op jit(solution)/shard_map/ppermute | solution.py:498
  9.2 0.8 %pad_add_fusion.offsets_ref = s32[48]{0:T(128)S(1)} fusion(s32[8]{0:T(128)} %param.15, s32[16]{0:T(128)} %param.14, s32[8]{0:T(128)} %param.17, s32[16]{0:T(128)} %param.16), kind=kLoop, calls=%fused_computation.5 | loop fusion | flops 144 | bytes 384 | tf_op jit(solution)/shard_map/concatenate | solution.py:497
  10.0 0.6 collective-permute-done.first_ref
  10.6 0.8 %collective-permute-start.1 = (bf16[176,128]{1,0:T(8,128)(2,1)S(1)}, bf16[176,128]{1,0:T(8,128)(2,1)S(1)}, u32[]{:S(2)}, u32[]{:S(2)}) collective-permute-start(bf16[176,128]{1,0:T(8,128)(2,1)S(1)} %collective-permute-done.first_ref), channel_id=1, source_target_pairs={{0,16},{2,18},{4,20},{6,22},{8,24},{10,26},{12,28},{14,30},{16,32}... | collective-permute-start | bytes 135176 | tf_op jit(solution)/shard_map/ppermute | solution.py:499
  11.4 3.5 %front_own.1 = (bf16[512,512]{1,0:T(8,128)(2,1)S(1)}, bf16[1024,1024]{1,0:T(8,128)(2,1)S(1)}, bf16[32,64,128]{2,1,0:T(8,128)(2,1)S(1)}) custom-call(s32[1]{0:T(128)} %bitcast.1.group_ref, s32[48]{0:T(128)S(1)} %pad_add_fusion.offsets_ref, bf16[176,128]{1,0:T(8,128)(2,1)S(1)} %pack.1.own_ref), custom_call_target="tpu_custom_call" | custom-call | flops 3000000000 | bytes 4194304 | tf_op jit(solution)/shard_map/front_own/pallas_call | solution.py:260
  14.9 0.0 collective-permute-done.2.third_ref
  14.9 0.7 %collective-permute-done.1.second_ref = bf16[176,128]{1,0:T(8,128)(2,1)S(1)} collective-permute-done((bf16[176,128]{1,0:T(8,128)(2,1)S(1)}, bf16[176,128]{1,0:T(8,128)(2,1)S(1)}, u32[]{:S(2)}, u32[]{:S(2)}) %collective-permute-start.1) | collective-permute-done | bytes 45088 | tf_op jit(solution)/shard_map/ppermute | solution.py:499
  15.6 5.8 %front_others.1 = bf16[32,4,64,128]{3,2,1,0:T(8,128)(2,1)S(1)} custom-call(s32[1]{0:T(128)} %bitcast.1.group_ref, bf16[176,128]{1,0:T(8,128)(2,1)S(1)} %collective-permute-done.first_ref, bf16[176,128]{1,0:T(8,128)(2,1)S(1)} %collective-permute-done.1.second_ref, bf16[176,128]{1,0:T(8,128)(2,1)S(1)} %collective-permute-done.2.third_ref, ...), custom_call_target="tpu_custom_call" | custom-call | flops 6000000000 | bytes 4194304 | tf_op jit(solution)/shard_map/front_others/pallas_call | solution.py:290
  21.4 1.3 %copy-done = bf16[32,4,64,128]{3,2,1,0:T(8,128)(2,1)} copy-done((bf16[32,4,64,128]{3,2,1,0:T(8,128)(2,1)}, bf16[32,4,64,128]{3,2,1,0:T(8,128)(2,1)S(1)}, u32[]{:S(2)}) %copy-start) | copy-done | bytes 2097176
  22.7 7.8 %all-to-all-start = ((bf16[32,4,64,128]{3,2,1,0:T(8,128)(2,1)}), bf16[32,4,64,128]{3,2,1,0:T(8,128)(2,1)S(1)}, u32[]{:S(2)}, u32[]{:S(2)}) async-start(bf16[32,4,64,128]{3,2,1,0:T(8,128)(2,1)} %copy-done), calls=%async_computation | async-start | bytes 4194304 | tf_op jit(solution)/shard_map/all_to_all | solution.py:502
  30.6 0.0 copy-start.1
  30.6 1.2 %copy-done.1 = f32[1,512,512]{2,1,0:T(8,128)S(1)} copy-done((f32[1,512,512]{2,1,0:T(8,128)S(1)}, f32[1,512,512]{2,1,0:T(8,128)}, u32[]{:S(2)}) %copy-start.1) | copy-done | bytes 1048600
  31.8 2.4 %tables.1 = (f32[2,8,1024]{2,1,0:T(8,128)S(1)}, f32[2,64,1024]{2,1,0:T(8,128)S(1)}, f32[2,8,512]{2,1,0:T(8,128)S(1)}, f32[2,64,512]{2,1,0:T(8,128)S(1)}, bf16[2,...) custom-call(s32[1]{0:T(128)} %bitcast.layer_ref.half_ref, s32[48]{0:T(128)S(1)} %pad_add_fusion.offsets_ref, ...), custom_call_target="tpu_custom_call" | custom-call | flops 1000000000 | bytes 8388608 | tf_op jit(solution)/shard_map/tables/pallas_call | solution.py:345
  34.2 0.0 copy-start.3
  34.2 0.8 %copy-done.3 = bf16[2,256,512]{2,1,0:T(8,128)(2,1)} copy-done((bf16[2,256,512]{2,1,0:T(8,128)(2,1)}, bf16[2,256,512]{2,1,0:T(8,128)(2,1)S(1)}, u32[]{:S(2)}) %copy-start.3) | copy-done | bytes 524312
  35.0 19.1 %all-to-all-done = bf16[32,4,64,128]{3,2,1,0:T(8,128)(2,1)S(1)} async-done(((bf16[32,4,64,128]{3,2,1,0:T(8,128)(2,1)}), bf16[32,4,64,128]{3,2,1,0:T(8,128)(2,1)S(1)}, u32[]{:S(2)}, u32[]{:S(2)}) %all-to-all-start) | async-done | bytes 2097184 | tf_op jit(solution)/shard_map/all_to_all | solution.py:502
  54.1 1.4 %back_other.1 = bf16[256,1024]{1,0:T(8,128)(2,1)S(1)} custom-call(s32[1]{0:T(128)S(6)} %sub.3.half_ref, bf16[2,4,4,4,64,128]{5,4,3,2,1,0:T(8,128)(2,1)S(1)} %bitcast.12, f32[2,8,1024]{2,1,0:T(8,128)S(1)} %get-tuple-element.19.high, f32[2,64,1024]{2,1,0:T(8,128)S(1)} %get-tuple-element.20.base), custom_call_target="tpu_custom_call" | custom-call | flops 1000000000 | bytes 4194304 | tf_op jit(solution)/shard_map/back_other/pallas_call | solution.py:396
  55.5 5.8 %collective-permute-start.3 = (bf16[256,1024]{1,0:T(8,128)(2,1)S(1)}, bf16[256,1024]{1,0:T(8,128)(2,1)S(1)}, u32[]{:S(2)}, u32[]{:S(2)}) collective-permute-start(bf16[256,1024]{1,0:T(8,128)(2,1)S(1)} %back_other.1), channel_id=1, source_target_pairs={{0,1},{1,0},{2,3},{3,2},{4,5},{5,4},{6,7},{7,6},{8,9},{9,8},{10,11... | collective-permute-start | bytes 1572872 | tf_op jit(solution)/shard_map/ppermute | solution.py:509
  61.3 2.1 %back_own.1 = (f32[2,256,512]{2,1,0:T(8,128)S(1)}, bf16[1024,1024]{1,0:T(8,128)(2,1)S(1)}) custom-call(s32[1]{0:T(128)} %bitcast.layer_ref.half_ref, bf16[2,4,4,4,64,128]{5,4,3,2,1,0:T(8,128)(2,1)S(1)} %bitcast.13, f32[2,8,1024]{2,1,0:T(8,128)S(1)} %get-tuple-element.19.high, f32[2,64,1024]{2,1,0:T(8,128)S(1)} %get-tuple-element.20.base, ...), custom_call_target="tpu_custom_call" | custom-call | flops 2000000000 | bytes 8388608 | tf_op jit(solution)/shard_map/back_own/pallas_call | solution.py:429
  63.4 1.6 %finish.1 = f32[2,256,512]{2,1,0:T(8,128)} custom-call(bf16[256,1024]{1,0:T(8,128)(2,1)S(1)} %collective-permute-done.3.middle_ref, f32[2,256,512]{2,1,0:T(8,128)S(1)} %get-tuple-element.24.own_ref, bf16[1024,1024]{1,0:T(8,128)(2,1)S(1)} %get-tuple-element.25.col_ref, bf16[2,256,512]{2,1,0:T(8,128)(2,1)S(1)} %get-tuple-element.26.screen_ref), custom_call_target="tpu_custom_call" | custom-call | flops 1000000000 | bytes 8388608 | tf_op jit(solution)/shard_map/finish/pallas_call | solution.py:460
  (6 shorter events, 0.0 us)
Async XLA Ops:
  2.2 8.4 %collective-permute-start = (bf16[176,128]{1,0:T(8,128)(2,1)S(1)}, bf16[176,128]{1,0:T(8,128)(2,1)S(1)}, u32[]{:S(2)}, u32[]{:S(2)}) collective-permute-start(bf16[176,128]{1,0:T(8,128)(2,1)S(1)} %pack.1.own_ref), channel_id=1, source_target_pairs={{0,16},{2,18},{4,20},{6,22},{8,24},{10,26},{12,28},{14,30},{16,32}... | collective-permute-start | bytes 135176 | tf_op jit(solution)/shard_map/ppermute | solution.py:498
  6.1 8.8 %collective-permute-start.2 = (bf16[176,128]{1,0:T(8,128)(2,1)S(1)}, bf16[176,128]{1,0:T(8,128)(2,1)S(1)}, u32[]{:S(2)}, u32[]{:S(2)}) collective-permute-start(bf16[176,128]{1,0:T(8,128)(2,1)S(1)} %pack.1.own_ref), channel_id=1, source_target_pairs={{0,48},{2,50},{4,52},{6,54},{8,56},{10,58},{12,60},{14,62},{16,0},... | collective-permute-start | bytes 135176 | tf_op jit(solution)/shard_map/ppermute | solution.py:498
  10.6 5.0 %collective-permute-start.1 = (bf16[176,128]{1,0:T(8,128)(2,1)S(1)}, bf16[176,128]{1,0:T(8,128)(2,1)S(1)}, u32[]{:S(2)}, u32[]{:S(2)}) collective-permute-start(bf16[176,128]{1,0:T(8,128)(2,1)S(1)} %collective-permute-done.first_ref), channel_id=1, source_target_pairs={{0,16},{2,18},{4,20},{6,22},{8,24},{10,26},{12,28},{14,30},{16,32}... | collective-permute-start | bytes 135176 | tf_op jit(solution)/shard_map/ppermute | solution.py:499
  21.4 1.3 %copy-start = (bf16[32,4,64,128]{3,2,1,0:T(8,128)(2,1)}, bf16[32,4,64,128]{3,2,1,0:T(8,128)(2,1)S(1)}, u32[]{:S(2)}) copy-start(bf16[32,4,64,128]{3,2,1,0:T(8,128)(2,1)S(1)} %front_others.1) | copy-start | bytes 6291460
  22.7 7.8 %copy-start.2 = (f32[2]{0:T(128)S(1)}, f32[2]{0:T(128)}, u32[]{:S(2)}) copy-start(f32[2]{0:T(128)} %weights_ref.1) | copy-start | bytes 28
  22.7 31.3 %all-to-all-start = ((bf16[32,4,64,128]{3,2,1,0:T(8,128)(2,1)}), bf16[32,4,64,128]{3,2,1,0:T(8,128)(2,1)S(1)}, u32[]{:S(2)}, u32[]{:S(2)}) async-start(bf16[32,4,64,128]{3,2,1,0:T(8,128)(2,1)} %copy-done), calls=%async_computation | async-start | bytes 4194304 | tf_op jit(solution)/shard_map/all_to_all | solution.py:502
  30.6 1.2 %copy-start.1 = (f32[1,512,512]{2,1,0:T(8,128)S(1)}, f32[1,512,512]{2,1,0:T(8,128)}, u32[]{:S(2)}) copy-start(f32[1,512,512]{2,1,0:T(8,128)} %screen_hbm.1) | copy-start | bytes 3145732
  34.2 0.8 %copy-start.3 = (bf16[2,256,512]{2,1,0:T(8,128)(2,1)}, bf16[2,256,512]{2,1,0:T(8,128)(2,1)S(1)}, u32[]{:S(2)}) copy-start(bf16[2,256,512]{2,1,0:T(8,128)(2,1)S(1)} %get-tuple-element.23.screen) | copy-start | bytes 1572868
  54.0 7.3 %copy-start.4 = (bf16[2,256,512]{2,1,0:T(8,128)(2,1)S(1)}, bf16[2,256,512]{2,1,0:T(8,128)(2,1)}, u32[]{:S(2)}) copy-start(bf16[2,256,512]{2,1,0:T(8,128)(2,1)} %copy-done.3) | copy-start | bytes 1572868
  55.5 8.0 %collective-permute-start.3 = (bf16[256,1024]{1,0:T(8,128)(2,1)S(1)}, bf16[256,1024]{1,0:T(8,128)(2,1)S(1)}, u32[]{:S(2)}, u32[]{:S(2)}) collective-permute-start(bf16[256,1024]{1,0:T(8,128)(2,1)S(1)} %back_other.1), channel_id=1, source_target_pairs={{0,1},{1,0},{2,3},{3,2},{4,5},{5,4},{6,7},{7,6},{8,9},{9,8},{10,11... | collective-permute-start | bytes 1572872 | tf_op jit(solution)/shard_map/ppermute | solution.py:509

commit v7 on v6

--- a/solution.py
+++ b/solution.py
@@ -196,7 +196,7 @@
 
 
 def peer(row, column):
-    return (column >> 2) * 16 + (column & 3) * 4 + row * 1
+    return (column >> 2) * 16 + row * 4 + (column & 3) * 1
 
 
 def grid_slots(refs, row_table, col_table, spread, turned, halves, store):
@@ -370,7 +370,7 @@
     sign = jnp.where((iota((1, 128), 1) & 64) == 0, -1.0, 1.0)
     for pair in range(4):
         placed = jnp.concatenate(
-            [blocks[pair >> 1, (2 * pair + part) & 3, :].reshape(1024, 128) for part in range(2)], axis=1
+            [blocks[pair >> 1, :, (2 * pair + part) & 3].reshape(1024, 128) for part in range(2)], axis=1
         )
         both = dot(row_table[...], placed)
         straight, crossed = both[:256], both[256:]
@@ -474,7 +474,7 @@
 
 
 GROUPS = [
-    [position(x, 2 * k + l, y) for l in range(2) for y in range(4) for x in range(4)] for k in range(4)
+    [position(x, 2 * k + l, y) for l in range(2) for x in range(4) for y in range(4)] for k in range(4)
 ]
 
 

time: 65.5 us -> 64.7 us (0.988)
  waiting for transfers between devices: 20.4 us -> 19.6 us
    all_to_all x1, waiting for transfers between devices: 19.1 us -> 18.3 us  [per_device(): lax.all_to_all(outgoing, 'sf', split_axis=0, concat_axis=0, tiled=True, a...]
where the time goes in v7:
time: 64.7 us; the launch traced here: 64.4 us
  starting transfers between devices  21.5 us (33%)
  waiting for transfers between devices  19.6 us (30%)
  Pallas kernels  16.8 us (26%)
  local copies, waits for them, and re-layouts  3.35 us (5%)
  other arithmetic  2.25 us (3%)
  between operations  0.92 us (1%)
    all_to_all x1, waiting for transfers between devices, per_device(): lax.all_to_all(outgoing, 'sf', split_axis=0, concat_axis=0, tiled=True, a...  18.3 us
    all_to_all x1, starting transfers between devices, per_device(): lax.all_to_all(outgoing, 'sf', split_axis=0, concat_axis=0, tiled=True, a...  7.8 us
    ppermute x2, starting transfers between devices, per_device(): first, third = (lax.ppermute(own, 'sf', shifted(turn)) for turn in (1, 3))  7.02 us
    ppermute x1, starting transfers between devices, per_device(): received = lax.ppermute(theirs, 'wa', [(0, 1), (1, 0)])  5.82 us
    pallas_call x1, Pallas kernels, front_others(): pl.pallas_call(front_others_kernel, out_shape=jax.ShapeDtypeStruct((32, 4...  5.76 us
    pallas_call x1, Pallas kernels, front_own(): pl.pallas_call(front_own_kernel, out_shape=[jax.ShapeDtypeStruct((512, 51...  3.47 us
    unnamed x10, local copies, waits for them, and re-layouts  3.35 us
    pallas_call x1, Pallas kernels, tables(): pl.pallas_call(tables_kernel, out_shape=[jax.ShapeDtypeStruct((2, 8, 1024...  2.38 us
  transfers between devices with their start and end apart: 5, of which 3 were waited for; matrix products, arithmetic and copies ran while one was open for 1% of the time, Pallas kernels for 12%

profile of v7, /device:TPU:1, one launch (start us, length us, event | category | flops | bytes accessed | tf_op | source)
XLA Modules:
  0.0 64.4 jit_solution(1108862438564551487)
XLA Ops:
  0.0 0.7 %fusion = (bf16[16,128]{1,0:T(8,128)(2,1)S(1)}, bf16[16,128]{1,0:T(8,128)(2,1)S(1)}) fusion(s32[2,1,1,8,128]{4,3,2,1,0:T(8,128)} %param.12), kind=kLoop, calls=%fused_computation.3 | loop fusion | flops 8192 | bytes 16384 | tf_op jit(solution)/shard_map/convert_element_type | solution.py:147
  1.4 0.8 %pad_maximum_fusion.inputs = bf16[176,128]{1,0:T(8,128)(2,1)S(1)} fusion(bf16[16,128]{1,0:T(8,128)(2,1)S(1)} %get-tuple-element.28, bf16[16,128]{1,0:T(8,128)(2,1)S(1)} %get-tuple-element.27, bf16[128,128]{1,0:T(8,128)(2,1)} %bitcast.14, bf16[16,128]{1,0:T(8,128)(2,1)} %bitcast.15), kind=kLoop, calls=%fused_computation | loop fusion | flops 180224 | bytes 90112 | tf_op jit(solution)/shard_map/concatenate | solution.py:144
  2.1 0.1 pack.1.own_ref
  2.2 3.9 %collective-permute-start = (bf16[176,128]{1,0:T(8,128)(2,1)S(1)}, bf16[176,128]{1,0:T(8,128)(2,1)S(1)}, u32[]{:S(2)}, u32[]{:S(2)}) collective-permute-start(bf16[176,128]{1,0:T(8,128)(2,1)S(1)} %pack.1.own_ref), channel_id=1, source_target_pairs={{0,16},{2,18},{4,20},{6,22},{8,24},{10,26},{12,28},{14,30},{16,32}... | collective-permute-start | bytes 135176 | tf_op jit(solution)/shard_map/ppermute | solution.py:498
  6.1 3.1 %collective-permute-start.2 = (bf16[176,128]{1,0:T(8,128)(2,1)S(1)}, bf16[176,128]{1,0:T(8,128)(2,1)S(1)}, u32[]{:S(2)}, u32[]{:S(2)}) collective-permute-start(bf16[176,128]{1,0:T(8,128)(2,1)S(1)} %pack.1.own_ref), channel_id=1, source_target_pairs={{0,48},{2,50},{4,52},{6,54},{8,56},{10,58},{12,60},{14,62},{16,0},... | collective-permute-start | bytes 135176 | tf_op jit(solution)/shard_map/ppermute | solution.py:498
  9.2 0.8 %pad_add_fusion.offsets_ref = s32[48]{0:T(128)S(1)} fusion(s32[8]{0:T(128)} %param.15, s32[16]{0:T(128)} %param.14, s32[8]{0:T(128)} %param.17, s32[16]{0:T(128)} %param.16), kind=kLoop, calls=%fused_computation.5 | loop fusion | flops 144 | bytes 384 | tf_op jit(solution)/shard_map/concatenate | solution.py:497
  10.0 0.6 collective-permute-done.first_ref
  10.6 0.8 %collective-permute-start.1 = (bf16[176,128]{1,0:T(8,128)(2,1)S(1)}, bf16[176,128]{1,0:T(8,128)(2,1)S(1)}, u32[]{:S(2)}, u32[]{:S(2)}) collective-permute-start(bf16[176,128]{1,0:T(8,128)(2,1)S(1)} %collective-permute-done.first_ref), channel_id=1, source_target_pairs={{0,16},{2,18},{4,20},{6,22},{8,24},{10,26},{12,28},{14,30},{16,32}... | collective-permute-start | bytes 135176 | tf_op jit(solution)/shard_map/ppermute | solution.py:499
  11.4 3.5 %front_own.1 = (bf16[512,512]{1,0:T(8,128)(2,1)S(1)}, bf16[1024,1024]{1,0:T(8,128)(2,1)S(1)}, bf16[32,64,128]{2,1,0:T(8,128)(2,1)S(1)}) custom-call(s32[1]{0:T(128)} %bitcast.1.group_ref, s32[48]{0:T(128)S(1)} %pad_add_fusion.offsets_ref, bf16[176,128]{1,0:T(8,128)(2,1)S(1)} %pack.1.own_ref), custom_call_target="tpu_custom_call" | custom-call | flops 3000000000 | bytes 4194304 | tf_op jit(solution)/shard_map/front_own/pallas_call | solution.py:260
  14.9 0.0 collective-permute-done.2.third_ref
  14.9 0.7 %collective-permute-done.1.second_ref = bf16[176,128]{1,0:T(8,128)(2,1)S(1)} collective-permute-done((bf16[176,128]{1,0:T(8,128)(2,1)S(1)}, bf16[176,128]{1,0:T(8,128)(2,1)S(1)}, u32[]{:S(2)}, u32[]{:S(2)}) %collective-permute-start.1) | collective-permute-done | bytes 45088 | tf_op jit(solution)/shard_map/ppermute | solution.py:499
  15.6 5.8 %front_others.1 = bf16[32,4,64,128]{3,2,1,0:T(8,128)(2,1)S(1)} custom-call(s32[1]{0:T(128)} %bitcast.1.group_ref, bf16[176,128]{1,0:T(8,128)(2,1)S(1)} %collective-permute-done.first_ref, bf16[176,128]{1,0:T(8,128)(2,1)S(1)} %collective-permute-done.1.second_ref, bf16[176,128]{1,0:T(8,128)(2,1)S(1)} %collective-permute-done.2.third_ref, ...), custom_call_target="tpu_custom_call" | custom-call | flops 6000000000 | bytes 4194304 | tf_op jit(solution)/shard_map/front_others/pallas_call | solution.py:290
  21.4 1.3 %copy-done = bf16[32,4,64,128]{3,2,1,0:T(8,128)(2,1)} copy-done((bf16[32,4,64,128]{3,2,1,0:T(8,128)(2,1)}, bf16[32,4,64,128]{3,2,1,0:T(8,128)(2,1)S(1)}, u32[]{:S(2)}) %copy-start) | copy-done | bytes 2097176
  22.7 7.8 %all-to-all-start = ((bf16[32,4,64,128]{3,2,1,0:T(8,128)(2,1)}), bf16[32,4,64,128]{3,2,1,0:T(8,128)(2,1)S(1)}, u32[]{:S(2)}, u32[]{:S(2)}) async-start(bf16[32,4,64,128]{3,2,1,0:T(8,128)(2,1)} %copy-done), calls=%async_computation | async-start | bytes 4194304 | tf_op jit(solution)/shard_map/all_to_all | solution.py:502
  30.6 0.0 copy-start.1
  30.6 1.2 %copy-done.1 = f32[1,512,512]{2,1,0:T(8,128)S(1)} copy-done((f32[1,512,512]{2,1,0:T(8,128)S(1)}, f32[1,512,512]{2,1,0:T(8,128)}, u32[]{:S(2)}) %copy-start.1) | copy-done | bytes 1048600
  31.8 2.4 %tables.1 = (f32[2,8,1024]{2,1,0:T(8,128)S(1)}, f32[2,64,1024]{2,1,0:T(8,128)S(1)}, f32[2,8,512]{2,1,0:T(8,128)S(1)}, f32[2,64,512]{2,1,0:T(8,128)S(1)}, bf16[2,...) custom-call(s32[1]{0:T(128)} %bitcast.layer_ref.half_ref, s32[48]{0:T(128)S(1)} %pad_add_fusion.offsets_ref, ...), custom_call_target="tpu_custom_call" | custom-call | flops 1000000000 | bytes 8388608 | tf_op jit(solution)/shard_map/tables/pallas_call | solution.py:345
  34.2 0.0 copy-start.3
  34.2 0.8 %copy-done.3 = bf16[2,256,512]{2,1,0:T(8,128)(2,1)} copy-done((bf16[2,256,512]{2,1,0:T(8,128)(2,1)}, bf16[2,256,512]{2,1,0:T(8,128)(2,1)S(1)}, u32[]{:S(2)}) %copy-start.3) | copy-done | bytes 524312
  35.0 18.3 %all-to-all-done = bf16[32,4,64,128]{3,2,1,0:T(8,128)(2,1)S(1)} async-done(((bf16[32,4,64,128]{3,2,1,0:T(8,128)(2,1)}), bf16[32,4,64,128]{3,2,1,0:T(8,128)(2,1)S(1)}, u32[]{:S(2)}, u32[]{:S(2)}) %all-to-all-start) | async-done | bytes 2097184 | tf_op jit(solution)/shard_map/all_to_all | solution.py:502
  53.3 1.4 %back_other.1 = bf16[256,1024]{1,0:T(8,128)(2,1)S(1)} custom-call(s32[1]{0:T(128)S(6)} %sub.3.half_ref, bf16[2,4,4,4,64,128]{5,4,3,2,1,0:T(8,128)(2,1)S(1)} %bitcast.12, f32[2,8,1024]{2,1,0:T(8,128)S(1)} %get-tuple-element.19.high, f32[2,64,1024]{2,1,0:T(8,128)S(1)} %get-tuple-element.20.base), custom_call_target="tpu_custom_call" | custom-call | flops 1000000000 | bytes 4194304 | tf_op jit(solution)/shard_map/back_other/pallas_call | solution.py:396
  54.7 5.8 %collective-permute-start.3 = (bf16[256,1024]{1,0:T(8,128)(2,1)S(1)}, bf16[256,1024]{1,0:T(8,128)(2,1)S(1)}, u32[]{:S(2)}, u32[]{:S(2)}) collective-permute-start(bf16[256,1024]{1,0:T(8,128)(2,1)S(1)} %back_other.1), channel_id=1, source_target_pairs={{0,1},{1,0},{2,3},{3,2},{4,5},{5,4},{6,7},{7,6},{8,9},{9,8},{10,11... | collective-permute-start | bytes 1572872 | tf_op jit(solution)/shard_map/ppermute | solution.py:509
  60.5 2.1 %back_own.1 = (f32[2,256,512]{2,1,0:T(8,128)S(1)}, bf16[1024,1024]{1,0:T(8,128)(2,1)S(1)}) custom-call(s32[1]{0:T(128)} %bitcast.layer_ref.half_ref, bf16[2,4,4,4,64,128]{5,4,3,2,1,0:T(8,128)(2,1)S(1)} %bitcast.13, f32[2,8,1024]{2,1,0:T(8,128)S(1)} %get-tuple-element.19.high, f32[2,64,1024]{2,1,0:T(8,128)S(1)} %get-tuple-element.20.base, ...), custom_call_target="tpu_custom_call" | custom-call | flops 2000000000 | bytes 8388608 | tf_op jit(solution)/shard_map/back_own/pallas_call | solution.py:429
  62.6 1.6 %finish.1 = f32[2,256,512]{2,1,0:T(8,128)} custom-call(bf16[256,1024]{1,0:T(8,128)(2,1)S(1)} %collective-permute-done.3.middle_ref, f32[2,256,512]{2,1,0:T(8,128)S(1)} %get-tuple-element.24.own_ref, bf16[1024,1024]{1,0:T(8,128)(2,1)S(1)} %get-tuple-element.25.col_ref, bf16[2,256,512]{2,1,0:T(8,128)(2,1)S(1)} %get-tuple-element.26.screen_ref), custom_call_target="tpu_custom_call" | custom-call | flops 1000000000 | bytes 8388608 | tf_op jit(solution)/shard_map/finish/pallas_call | solution.py:460
  (6 shorter events, 0.0 us)
Async XLA Ops:
  2.2 8.4 %collective-permute-start = (bf16[176,128]{1,0:T(8,128)(2,1)S(1)}, bf16[176,128]{1,0:T(8,128)(2,1)S(1)}, u32[]{:S(2)}, u32[]{:S(2)}) collective-permute-start(bf16[176,128]{1,0:T(8,128)(2,1)S(1)} %pack.1.own_ref), channel_id=1, source_target_pairs={{0,16},{2,18},{4,20},{6,22},{8,24},{10,26},{12,28},{14,30},{16,32}... | collective-permute-start | bytes 135176 | tf_op jit(solution)/shard_map/ppermute | solution.py:498
  6.1 8.8 %collective-permute-start.2 = (bf16[176,128]{1,0:T(8,128)(2,1)S(1)}, bf16[176,128]{1,0:T(8,128)(2,1)S(1)}, u32[]{:S(2)}, u32[]{:S(2)}) collective-permute-start(bf16[176,128]{1,0:T(8,128)(2,1)S(1)} %pack.1.own_ref), channel_id=1, source_target_pairs={{0,48},{2,50},{4,52},{6,54},{8,56},{10,58},{12,60},{14,62},{16,0},... | collective-permute-start | bytes 135176 | tf_op jit(solution)/shard_map/ppermute | solution.py:498
  10.6 5.0 %collective-permute-start.1 = (bf16[176,128]{1,0:T(8,128)(2,1)S(1)}, bf16[176,128]{1,0:T(8,128)(2,1)S(1)}, u32[]{:S(2)}, u32[]{:S(2)}) collective-permute-start(bf16[176,128]{1,0:T(8,128)(2,1)S(1)} %collective-permute-done.first_ref), channel_id=1, source_target_pairs={{0,16},{2,18},{4,20},{6,22},{8,24},{10,26},{12,28},{14,30},{16,32}... | collective-permute-start | bytes 135176 | tf_op jit(solution)/shard_map/ppermute | solution.py:499
  21.4 1.3 %copy-start = (bf16[32,4,64,128]{3,2,1,0:T(8,128)(2,1)}, bf16[32,4,64,128]{3,2,1,0:T(8,128)(2,1)S(1)}, u32[]{:S(2)}) copy-start(bf16[32,4,64,128]{3,2,1,0:T(8,128)(2,1)S(1)} %front_others.1) | copy-start | bytes 6291460
  22.7 7.8 %copy-start.2 = (f32[2]{0:T(128)S(1)}, f32[2]{0:T(128)}, u32[]{:S(2)}) copy-start(f32[2]{0:T(128)} %weights_ref.1) | copy-start | bytes 28
  22.7 30.5 %all-to-all-start = ((bf16[32,4,64,128]{3,2,1,0:T(8,128)(2,1)}), bf16[32,4,64,128]{3,2,1,0:T(8,128)(2,1)S(1)}, u32[]{:S(2)}, u32[]{:S(2)}) async-start(bf16[32,4,64,128]{3,2,1,0:T(8,128)(2,1)} %copy-done), calls=%async_computation | async-start | bytes 4194304 | tf_op jit(solution)/shard_map/all_to_all | solution.py:502
  30.6 1.2 %copy-start.1 = (f32[1,512,512]{2,1,0:T(8,128)S(1)}, f32[1,512,512]{2,1,0:T(8,128)}, u32[]{:S(2)}) copy-start(f32[1,512,512]{2,1,0:T(8,128)} %screen_hbm.1) | copy-start | bytes 3145732
  34.2 0.8 %copy-start.3 = (bf16[2,256,512]{2,1,0:T(8,128)(2,1)}, bf16[2,256,512]{2,1,0:T(8,128)(2,1)S(1)}, u32[]{:S(2)}) copy-start(bf16[2,256,512]{2,1,0:T(8,128)(2,1)S(1)} %get-tuple-element.23.screen) | copy-start | bytes 1572868
  53.3 7.2 %copy-start.4 = (bf16[2,256,512]{2,1,0:T(8,128)(2,1)S(1)}, bf16[2,256,512]{2,1,0:T(8,128)(2,1)}, u32[]{:S(2)}) copy-start(bf16[2,256,512]{2,1,0:T(8,128)(2,1)} %copy-done.3) | copy-start | bytes 1572868
  54.7 7.9 %collective-permute-start.3 = (bf16[256,1024]{1,0:T(8,128)(2,1)S(1)}, bf16[256,1024]{1,0:T(8,128)(2,1)S(1)}, u32[]{:S(2)}, u32[]{:S(2)}) collective-permute-start(bf16[256,1024]{1,0:T(8,128)(2,1)S(1)} %back_other.1), channel_id=1, source_target_pairs={{0,1},{1,0},{2,3},{3,2},{4,5},{5,4},{6,7},{7,6},{8,9},{9,8},{10,11... | collective-permute-start | bytes 1572872 | tf_op jit(solution)/shard_map/ppermute | solution.py:509
